TPU v7x, 32 devices: a whole 2x2x4 slice. The times are simulated.
32 devices in a mesh: shard: 2 (over x), ctx: 4 (over z), tp: 4 (over y, core).
Axes of the slice: x: 2, y: 2, z: 4, core: 2. Of those that a mesh axis runs over, the one named last changes fastest.
Arguments:
- inputs: bfloat16 [2560, 2048], P(('shard', 'ctx')), may hold values from -6 to 6
- parents: int32 [40], replicated, may hold values from -1 to 39, as said below
- attention_routes: int32 [2560, 2], P(('shard', 'ctx')), may hold values from 0 to 3, all different within a row; in each aligned block of 320 rows (0 to 319, 320 to 639, ...) at most 176 rows name the same one
- expert_routes: int32 [2560, 2], P(('shard', 'ctx')), may hold values from 0 to 3, all different within a row; in each aligned block of 320 rows (0 to 319, 320 to 639, ...) at most 176 rows name the same one
- attention_gain: bfloat16 [2048], P(('shard', 'ctx')), may hold values from 0.5 to 1.5
- attention_router: bfloat16 [2048, 4], P(('shard', 'ctx')), may hold values from -0.09375 to 0.09375
- query_weight: bfloat16 [4, 2048, 2048], P(None, ('shard', 'ctx'), 'tp')
- key_weight: bfloat16 [2048, 2048], P(('shard', 'ctx'), 'tp'), may hold values from -0.125 to 0.125
- value_weight: bfloat16 [2048, 2048], P(('shard', 'ctx'), 'tp'), may hold values from -0.125 to 0.125
- output_weight: bfloat16 [4, 2048, 2048], P(None, 'tp', ('shard', 'ctx')), may hold values from -0.5 to 0.5
- expert_gain: bfloat16 [2048], P(('shard', 'ctx')), may hold values from 0.5 to 1.5
- expert_router: bfloat16 [2048, 4], P(('shard', 'ctx')), may hold values from -0.09375 to 0.09375
- gate_weight: bfloat16 [4, 2048, 5632], P(None, ('shard', 'ctx'), 'tp'), may hold values from -0.125 to 0.125
- up_weight: bfloat16 [4, 2048, 5632], P(None, ('shard', 'ctx'), 'tp'), may hold values from -0.125 to 0.125
- down_weight: bfloat16 [4, 5632, 2048], P(None, 'tp', ('shard', 'ctx')), may hold values from -0.15625 to 0.15625
- cotangent: bfloat16 [2560, 2048], P(('shard', 'ctx')), may hold values from -6 to 6
Outputs:
- output: bfloat16 [2560, 2048], P(('shard', 'ctx'))
- input_gradient: bfloat16 [2560, 2048], P(('shard', 'ctx'))
- attention_gain_gradient: float32 [2048], P(('shard', 'ctx'))
- attention_router_gradient: float32 [2048, 4], P(('shard', 'ctx'))
- query_weight_gradient: float32 [4, 2048, 2048], P(None, ('shard', 'ctx'), 'tp')
- key_weight_gradient: float32 [2048, 2048], P(('shard', 'ctx'), 'tp')
- value_weight_gradient: float32 [2048, 2048], P(('shard', 'ctx'), 'tp')
- output_weight_gradient: float32 [4, 2048, 2048], P(None, 'tp', ('shard', 'ctx'))
- expert_gain_gradient: float32 [2048], P(('shard', 'ctx'))
- expert_router_gradient: float32 [2048, 4], P(('shard', 'ctx'))
- gate_weight_gradient: float32 [4, 2048, 5632], P(None, ('shard', 'ctx'), 'tp')
- up_weight_gradient: float32 [4, 2048, 5632], P(None, ('shard', 'ctx'), 'tp')
- down_weight_gradient: float32 [4, 5632, 2048], P(None, 'tp', ('shard', 'ctx'))
- clipped_query: bfloat16 [4, 2048, 2048], P(None, ('shard', 'ctx'), 'tp')
- clipped_key: bfloat16 [2048, 2048], P(('shard', 'ctx'), 'tp')
Inputs may be any that keep to these rules, and one draw needn't show every extreme that they name: `parents`: the units of 64 tokens of each index of shard form trees of 20 units: a trunk of 8 units in a chain whose first unit has parent -1, 4 branch units whose parent is the trunk's last unit, and two leaf units under each branch unit. A parent lies among the units of the same index of shard. In each index of shard one tree has units on the first and on the last device of ctx. `attention_routes`: A row names two different experts. In the rows of one device no expert is named more than 176 times, and in some devices one expert is named exactly 176 times. `expert_routes`: A row names two different experts. In the rows of one device no expert is named more than 176 times, and in some devices one expert is named exactly 176 times.
All inputs are finite; a program needn't handle non-finite values.
Results may differ from a plain program's by a relative error of at most 0.024.
Values may be sent and summed in bfloat16 or wider, within the bound.
No kernel may reach another device: no remote copies, remote signals or barrier semaphores. Data moves between devices by JAX's collectives and lax.ppermute only.
A program may use at most 512 MiB of HBM per device.

v0:
```python
import jax
import jax.numpy as jnp
from jax import lax
from jax.sharding import PartitionSpec as P

HEAD_DIM = 128
TOP = 2
SEG = 64
PATH = 10
CAP = 176


EPS = 1e-05
ROPE_BASE = 10000.0
CLIP = 2.0
HIGH = lax.Precision.HIGHEST


def normalize(value, gain):
    scale = lax.rsqrt(jnp.mean(value * value, axis=-1, keepdims=True) + EPS)
    return value * scale * gain


def normalize_back(change, value, gain):
    scale = lax.rsqrt(jnp.mean(value * value, axis=-1, keepdims=True) + EPS)
    gain_change = jnp.sum(change * value * scale, axis=0)
    scaled = change * gain
    value_change = scale * scaled - value * scale**3 * jnp.mean(
        scaled * value, axis=-1, keepdims=True
    )
    return (value_change, gain_change)


def gating(normed, router, routes):
    logits = jnp.dot(normed, router, preferred_element_type=jnp.float32)
    chosen = jnp.take_along_axis(logits, routes, axis=1)
    return jax.nn.softmax(chosen, axis=1)


def gating_back(change, gates, routes, experts):
    chosen_change = gates * (change - jnp.sum(gates * change, axis=1, keepdims=True))
    onehot = (routes[:, :, None] == jnp.arange(experts, dtype=jnp.int32)[None, None, :]).astype(
        jnp.float32
    )
    return jnp.sum(chosen_change[:, :, None] * onehot, axis=1)


def slot_tables(routes, experts, capacity):
    number = routes.shape[0] * routes.shape[1]
    flat = routes.reshape(number)
    onehot = (flat[:, None] == jnp.arange(experts, dtype=jnp.int32)[None, :]).astype(jnp.int32)
    before = jnp.cumsum(onehot, axis=0, dtype=jnp.int32) - onehot
    place = jnp.sum(before * onehot, axis=1, dtype=jnp.int32)
    slot_index = flat * capacity + place
    pair_index = (
        jnp.zeros((experts * capacity,), jnp.int32)
        .at[slot_index]
        .set(jnp.arange(number, dtype=jnp.int32))
    )
    filled = jnp.zeros((experts * capacity,), jnp.int32).at[slot_index].set(1)
    return (slot_index, pair_index, filled)


def rope_tables(positions, half):
    frequency = ROPE_BASE ** (-jnp.arange(half, dtype=jnp.float32) / half)
    angle = positions.astype(jnp.float32)[:, None] * frequency[None, :]
    return (jnp.cos(angle), jnp.sin(angle))


def rotate(value, cosine, sine):
    half = value.shape[-1] // 2
    first = value[..., :half]
    second = value[..., half:]
    return jnp.concatenate(
        [first * cosine - second * sine, second * cosine + first * sine], axis=-1
    )


def rotate_back(change, cosine, sine):
    half = change.shape[-1] // 2
    first = change[..., :half]
    second = change[..., half:]
    return jnp.concatenate(
        [first * cosine + second * sine, second * cosine - first * sine], axis=-1
    )


def ancestors(parents, start_units):
    chain = [start_units]
    current = start_units
    for level in range(PATH - 1):
        current = jnp.where(current >= 0, parents[jnp.maximum(current, 0)], -1)
        chain.append(current)
    return jnp.stack(chain, axis=1)


def unit_mask(valid_row):
    token_row = jnp.arange(SEG * TOP) // TOP
    causal = jnp.arange(SEG)[None, :] <= token_row[:, None]
    others = jnp.broadcast_to(valid_row[None, 1:, None], (SEG * TOP, PATH - 1, SEG))
    return jnp.concatenate([causal[:, None, :], others], axis=1).reshape(SEG * TOP, PATH * SEG)


def dispatch(rows, pair_index, filled, choose, experts, capacity):
    picked = rows[pair_index // choose]
    return jnp.where(filled[:, None] > 0, picked, jnp.zeros((), rows.dtype)).reshape(
        experts, capacity, rows.shape[1]
    )


def spread(pairs, pair_index, filled, experts, capacity):
    picked = pairs[pair_index]
    return jnp.where(filled[:, None] > 0, picked, jnp.zeros((), pairs.dtype)).reshape(
        experts, capacity, pairs.shape[1]
    )


def on_device(
    inputs,
    parents,
    attention_routes,
    expert_routes,
    attention_gain,
    attention_router,
    query_weight,
    key_weight,
    value_weight,
    output_weight,
    expert_gain,
    expert_router,
    gate_weight,
    up_weight,
    down_weight,
    cotangent,
):
    count = inputs.shape[0]
    width = inputs.shape[1]
    experts = query_weight.shape[0]
    local_width = query_weight.shape[2]
    head_dim = HEAD_DIM
    local_heads = local_width // head_dim
    capacity = CAP
    choose = attention_routes.shape[1]
    segment = SEG
    units_here = count // segment
    group_units = lax.axis_size("ctx") * units_here
    scale = head_dim ** (-0.5)
    gain_one, router_one, query_full, key_full, value_full, output_full, gain_two, router_two = (
        lax.all_gather(attention_gain, ("shard", "ctx"), axis=0, tiled=True),
        lax.all_gather(attention_router, ("shard", "ctx"), axis=0, tiled=True),
        lax.all_gather(query_weight, ("shard", "ctx"), axis=1, tiled=True),
        lax.all_gather(key_weight, ("shard", "ctx"), axis=0, tiled=True),
        lax.all_gather(value_weight, ("shard", "ctx"), axis=0, tiled=True),
        lax.all_gather(output_weight, ("shard", "ctx"), axis=2, tiled=True),
        lax.all_gather(expert_gain, ("shard", "ctx"), axis=0, tiled=True),
        lax.all_gather(expert_router, ("shard", "ctx"), axis=0, tiled=True),
    )
    first_unit = (
        lax.axis_index("shard") * lax.axis_size("ctx") + lax.axis_index("ctx")
    ) * units_here
    group_first = lax.axis_index("shard") * group_units
    own_units = first_unit + jnp.arange(units_here, dtype=jnp.int32)
    chain = ancestors(parents, own_units)
    valid = chain >= 0
    depth = jnp.sum(valid[:, 1:].astype(jnp.int32), axis=1, dtype=jnp.int32)
    positions = (depth[:, None] * segment + jnp.arange(segment, dtype=jnp.int32)[None, :]).reshape(
        count
    )
    cosine, sine = rope_tables(positions, head_dim // 2)
    local_chain = jnp.clip(chain - group_first, 0, group_units - 1)
    allowed = jax.vmap(unit_mask)(valid)
    residual = inputs.astype(jnp.float32)
    gain_first = gain_one.astype(jnp.float32)
    normed = normalize(residual, gain_first).astype(jnp.bfloat16)
    head_gates = gating(normed, router_one, attention_routes)
    head_slot, head_pair, head_filled = slot_tables(attention_routes, experts, capacity)
    head_rows = dispatch(normed, head_pair, head_filled, choose, experts, capacity)
    query_slots = jnp.einsum(
        "ecd,edf->ecf", head_rows, query_full, preferred_element_type=jnp.float32
    )
    query_pairs = query_slots.reshape(experts * capacity, local_width)[head_slot].reshape(
        count, choose, local_heads, head_dim
    )
    queries = rotate(query_pairs, cosine[:, None, None, :], sine[:, None, None, :]).astype(
        jnp.bfloat16
    )
    key_raw = jnp.dot(normed, key_full, preferred_element_type=jnp.float32).reshape(
        count, local_heads, head_dim
    )
    keys = (
        rotate(key_raw, cosine[:, None, :], sine[:, None, :])
        .astype(jnp.bfloat16)
        .reshape(count, local_width)
    )
    values = jnp.dot(normed, value_full, preferred_element_type=jnp.float32).astype(jnp.bfloat16)
    all_keys, all_values = (
        lax.all_gather(keys, "ctx", axis=0, tiled=True),
        lax.all_gather(values, "ctx", axis=0, tiled=True),
    )
    path_keys = all_keys.reshape(group_units, segment, local_width)[local_chain].reshape(
        units_here, PATH * segment, local_heads, head_dim
    )
    path_values = all_values.reshape(group_units, segment, local_width)[local_chain].reshape(
        units_here, PATH * segment, local_heads, head_dim
    )
    query_units = queries.reshape(units_here, segment * choose, local_heads, head_dim)
    scores = (
        jnp.einsum("uqhd,ukhd->uhqk", query_units, path_keys, preferred_element_type=jnp.float32)
        * scale
    )
    masked = jnp.where(allowed[:, None], scores, -1e30)
    peak = jnp.max(masked, axis=-1, keepdims=True)
    weights = jnp.where(allowed[:, None], jnp.exp(masked - peak), 0.0)
    total = jnp.sum(weights, axis=-1, keepdims=True)
    log_total = peak + jnp.log(total)
    head_peak = jnp.max(peak[..., 0], axis=(0, 2))
    shares = (weights / total).astype(jnp.bfloat16)
    mixed = (
        jnp.einsum("uhqk,ukhd->uqhd", shares, path_values, preferred_element_type=jnp.float32)
        .astype(jnp.bfloat16)
        .reshape(count * choose, local_width)
    )
    mixed_slots = spread(mixed, head_pair, head_filled, experts, capacity)
    out_slots = jnp.einsum(
        "ecf,efd->ecd", mixed_slots, output_full, preferred_element_type=jnp.float32
    )
    out_pairs = out_slots.reshape(experts * capacity, width)[head_slot].reshape(
        count, choose, width
    )
    attention = lax.psum(jnp.sum(head_gates[:, :, None] * out_pairs, axis=1), "tp")
    hidden_state = residual + attention
    peak_all = lax.pmax(head_peak, ("shard", "ctx"))
    gain_second = gain_two.astype(jnp.float32)
    normed_two = normalize(hidden_state, gain_second).astype(jnp.bfloat16)
    expert_gates = gating(normed_two, router_two, expert_routes)
    expert_slot, expert_pair, expert_filled = slot_tables(expert_routes, experts, capacity)
    expert_rows = dispatch(normed_two, expert_pair, expert_filled, choose, experts, capacity)
    gate_full, up_full, down_full = (
        lax.all_gather(gate_weight, ("shard", "ctx"), axis=1, tiled=True),
        lax.all_gather(up_weight, ("shard", "ctx"), axis=1, tiled=True),
        lax.all_gather(down_weight, ("shard", "ctx"), axis=2, tiled=True),
    )
    gate_pre = jnp.einsum(
        "ecd,edf->ecf", expert_rows, gate_full, preferred_element_type=jnp.float32
    )
    up_pre = jnp.einsum("ecd,edf->ecf", expert_rows, up_full, preferred_element_type=jnp.float32)
    activated = (jax.nn.silu(gate_pre) * up_pre).astype(jnp.bfloat16)
    down_slots = jnp.einsum(
        "ecf,efd->ecd", activated, down_full, preferred_element_type=jnp.float32
    )
    down_pairs = down_slots.reshape(experts * capacity, width)[expert_slot].reshape(
        count, choose, width
    )
    feed = lax.psum(
        jnp.sum(expert_gates[:, :, None] * down_pairs, axis=1).astype(jnp.bfloat16), "tp"
    ).astype(jnp.float32)
    output = (hidden_state + feed).astype(jnp.bfloat16)
    upstream = cotangent.astype(jnp.float32)
    down_back = (
        (expert_gates[:, :, None] * upstream[:, None, :])
        .astype(jnp.bfloat16)
        .reshape(count * choose, width)
    )
    expert_gate_part = jnp.sum(down_pairs * upstream[:, None, :], axis=2)
    down_back_slots = spread(down_back, expert_pair, expert_filled, experts, capacity)
    act_back = jnp.einsum(
        "ecd,efd->ecf", down_back_slots, down_full, preferred_element_type=jnp.float32
    )
    sigmoid = jax.nn.sigmoid(gate_pre)
    gate_back = (act_back * up_pre * sigmoid * (1.0 + gate_pre * (1.0 - sigmoid))).astype(
        jnp.bfloat16
    )
    up_back = (act_back * gate_pre * sigmoid).astype(jnp.bfloat16)
    rows_back = jnp.einsum(
        "ecf,edf->ecd", gate_back, gate_full, preferred_element_type=jnp.float32
    ) + jnp.einsum("ecf,edf->ecd", up_back, up_full, preferred_element_type=jnp.float32)
    normed_two_part = jnp.sum(
        rows_back.reshape(experts * capacity, width)[expert_slot].reshape(count, choose, width),
        axis=1,
    )
    collected = []
    for expert in range(experts):
        gate_term = jnp.einsum(
            "cd,cf->df", expert_rows[expert], gate_back[expert], preferred_element_type=jnp.float32
        )
        up_term = jnp.einsum(
            "cd,cf->df", expert_rows[expert], up_back[expert], preferred_element_type=jnp.float32
        )
        down_term = jnp.einsum(
            "cf,cd->fd",
            activated[expert],
            down_back_slots[expert],
            preferred_element_type=jnp.float32,
        )
        collected.append(
            (
                lax.psum_scatter(
                    gate_term.astype(jnp.bfloat16),
                    ("shard", "ctx"),
                    scatter_dimension=0,
                    tiled=True,
                ).astype(jnp.float32),
                lax.psum_scatter(
                    up_term.astype(jnp.bfloat16), ("shard", "ctx"), scatter_dimension=0, tiled=True
                ).astype(jnp.float32),
                lax.psum_scatter(
                    down_term.astype(jnp.bfloat16),
                    ("shard", "ctx"),
                    scatter_dimension=1,
                    tiled=True,
                ).astype(jnp.float32),
            )
        )
    gate_gradient = jnp.stack([item[0] for item in collected])
    up_gradient = jnp.stack([item[1] for item in collected])
    down_gradient = jnp.stack([item[2] for item in collected])
    normed_two_back, expert_gate_back = lax.psum((normed_two_part, expert_gate_part), "tp")
    expert_logit_back = gating_back(expert_gate_back, expert_gates, expert_routes, experts)
    router_two_term = jnp.einsum(
        "td,te->de", normed_two.astype(jnp.float32), expert_logit_back, precision=HIGH
    )
    normed_two_back = normed_two_back + jnp.einsum(
        "te,de->td", expert_logit_back, router_two.astype(jnp.float32), precision=HIGH
    )
    hidden_back, gain_two_term = normalize_back(normed_two_back, hidden_state, gain_second)
    hidden_back = hidden_back + upstream
    head_back = (
        (head_gates[:, :, None] * hidden_back[:, None, :])
        .astype(jnp.bfloat16)
        .reshape(count * choose, width)
    )
    head_gate_part = jnp.sum(out_pairs * hidden_back[:, None, :], axis=2)
    head_back_slots = spread(head_back, head_pair, head_filled, experts, capacity)
    output_term = jnp.einsum(
        "ecf,ecd->efd", mixed_slots, head_back_slots, preferred_element_type=jnp.float32
    )
    mixed_back_slots = jnp.einsum(
        "ecd,efd->ecf", head_back_slots, output_full, preferred_element_type=jnp.float32
    )
    mixed_back = (
        mixed_back_slots.reshape(experts * capacity, local_width)[head_slot]
        .astype(jnp.bfloat16)
        .reshape(units_here, segment * choose, local_heads, head_dim)
    )
    again = (
        jnp.einsum("uqhd,ukhd->uhqk", query_units, path_keys, preferred_element_type=jnp.float32)
        * scale
    )
    chances = jnp.where(allowed[:, None], jnp.exp(again - log_total), 0.0)
    value_path_back = jnp.einsum(
        "uhqk,uqhd->ukhd",
        chances.astype(jnp.bfloat16),
        mixed_back,
        preferred_element_type=jnp.float32,
    )
    share_back = jnp.einsum(
        "uqhd,ukhd->uhqk", mixed_back, path_values, preferred_element_type=jnp.float32
    )
    score_back = (
        chances * (share_back - jnp.sum(chances * share_back, axis=-1, keepdims=True))
    ).astype(jnp.bfloat16)
    query_back_raw = (
        jnp.einsum("uhqk,ukhd->uqhd", score_back, path_keys, preferred_element_type=jnp.float32)
        * scale
    )
    key_path_back = (
        jnp.einsum("uhqk,uqhd->ukhd", score_back, query_units, preferred_element_type=jnp.float32)
        * scale
    )
    owner = (
        (local_chain[:, :, None] == jnp.arange(group_units, dtype=jnp.int32)[None, None, :])
        & valid[:, :, None]
    ).astype(jnp.float32)
    key_group = jnp.einsum(
        "upg,upsc->gsc",
        owner,
        key_path_back.reshape(units_here, PATH, segment, local_width),
        precision=HIGH,
    )
    value_group = jnp.einsum(
        "upg,upsc->gsc",
        owner,
        value_path_back.reshape(units_here, PATH, segment, local_width),
        precision=HIGH,
    )
    key_mine, value_mine = (
        lax.psum_scatter(
            key_group.reshape(group_units * segment, local_width).astype(jnp.bfloat16),
            "ctx",
            scatter_dimension=0,
            tiled=True,
        ).astype(jnp.float32),
        lax.psum_scatter(
            value_group.reshape(group_units * segment, local_width).astype(jnp.bfloat16),
            "ctx",
            scatter_dimension=0,
            tiled=True,
        ).astype(jnp.float32),
    )
    key_back = (
        rotate_back(
            key_mine.reshape(count, local_heads, head_dim), cosine[:, None, :], sine[:, None, :]
        )
        .astype(jnp.bfloat16)
        .reshape(count, local_width)
    )
    value_back = value_mine.astype(jnp.bfloat16)
    query_back = (
        rotate_back(
            query_back_raw.reshape(count, choose, local_heads, head_dim),
            cosine[:, None, None, :],
            sine[:, None, None, :],
        )
        .astype(jnp.bfloat16)
        .reshape(count * choose, local_width)
    )
    query_back_slots = spread(query_back, head_pair, head_filled, experts, capacity)
    query_term = jnp.einsum(
        "ecd,ecf->edf", head_rows, query_back_slots, preferred_element_type=jnp.float32
    )
    key_term = jnp.einsum("td,tf->df", normed, key_back, preferred_element_type=jnp.float32)
    value_term = jnp.einsum("td,tf->df", normed, value_back, preferred_element_type=jnp.float32)
    query_rows_back = jnp.einsum(
        "ecf,edf->ecd", query_back_slots, query_full, preferred_element_type=jnp.float32
    )
    normed_part = jnp.sum(
        query_rows_back.reshape(experts * capacity, width)[head_slot].reshape(count, choose, width),
        axis=1,
    )
    normed_part = (
        normed_part
        + jnp.einsum("tf,df->td", key_back, key_full, preferred_element_type=jnp.float32)
        + jnp.einsum("tf,df->td", value_back, value_full, preferred_element_type=jnp.float32)
    )
    normed_back, head_gate_back = (
        lax.psum(normed_part.astype(jnp.bfloat16), "tp").astype(jnp.float32),
        lax.psum(head_gate_part.astype(jnp.bfloat16), "tp").astype(jnp.float32),
    )
    head_logit_back = gating_back(head_gate_back, head_gates, attention_routes, experts)
    router_one_term = jnp.einsum(
        "td,te->de", normed.astype(jnp.float32), head_logit_back, precision=HIGH
    )
    normed_back = normed_back + jnp.einsum(
        "te,de->td", head_logit_back, router_one.astype(jnp.float32), precision=HIGH
    )
    input_back, gain_one_term = normalize_back(normed_back, residual, gain_first)
    input_gradient = (input_back + hidden_back).astype(jnp.bfloat16)
    (
        gain_one_gradient,
        router_one_gradient,
        query_gradient,
        key_gradient,
        value_gradient,
        output_gradient,
        gain_two_gradient,
        router_two_gradient,
    ) = (
        lax.psum_scatter(
            gain_one_term.astype(jnp.bfloat16), ("shard", "ctx"), scatter_dimension=0, tiled=True
        ).astype(jnp.float32),
        lax.psum_scatter(
            router_one_term.astype(jnp.bfloat16), ("shard", "ctx"), scatter_dimension=0, tiled=True
        ).astype(jnp.float32),
        lax.psum_scatter(
            query_term.astype(jnp.bfloat16), ("shard", "ctx"), scatter_dimension=1, tiled=True
        ).astype(jnp.float32),
        lax.psum_scatter(
            key_term.astype(jnp.bfloat16), ("shard", "ctx"), scatter_dimension=0, tiled=True
        ).astype(jnp.float32),
        lax.psum_scatter(
            value_term.astype(jnp.bfloat16), ("shard", "ctx"), scatter_dimension=0, tiled=True
        ).astype(jnp.float32),
        lax.psum_scatter(
            output_term.astype(jnp.bfloat16), ("shard", "ctx"), scatter_dimension=2, tiled=True
        ).astype(jnp.float32),
        lax.psum_scatter(
            gain_two_term.astype(jnp.bfloat16), ("shard", "ctx"), scatter_dimension=0, tiled=True
        ).astype(jnp.float32),
        lax.psum_scatter(
            router_two_term.astype(jnp.bfloat16), ("shard", "ctx"), scatter_dimension=0, tiled=True
        ).astype(jnp.float32),
    )
    factor = jnp.sqrt(jnp.minimum(1.0, CLIP / peak_all))
    columns = jnp.repeat(factor, head_dim)
    clipped_query = (query_weight.astype(jnp.float32) * columns).astype(jnp.bfloat16)
    clipped_key = (key_weight.astype(jnp.float32) * columns).astype(jnp.bfloat16)
    return (
        output,
        input_gradient,
        gain_one_gradient,
        router_one_gradient,
        query_gradient,
        key_gradient,
        value_gradient,
        output_gradient,
        gain_two_gradient,
        router_two_gradient,
        gate_gradient,
        up_gradient,
        down_gradient,
        clipped_query,
        clipped_key,
    )


def solution(mesh):
    placed = (
        P(("shard", "ctx"), None),
        P(),
        P(("shard", "ctx"), None),
        P(("shard", "ctx"), None),
        P(("shard", "ctx")),
        P(("shard", "ctx"), None),
        P(None, ("shard", "ctx"), "tp"),
        P(("shard", "ctx"), "tp"),
        P(("shard", "ctx"), "tp"),
        P(None, "tp", ("shard", "ctx")),
        P(("shard", "ctx")),
        P(("shard", "ctx"), None),
        P(None, ("shard", "ctx"), "tp"),
        P(None, ("shard", "ctx"), "tp"),
        P(None, "tp", ("shard", "ctx")),
        P(("shard", "ctx"), None),
    )
    return jax.shard_map(
        on_device,
        mesh=mesh,
        in_specs=placed,
        out_specs=(
            P(("shard", "ctx"), None),
            P(("shard", "ctx"), None),
            P(("shard", "ctx")),
            P(("shard", "ctx"), None),
            P(None, ("shard", "ctx"), "tp"),
            P(("shard", "ctx"), "tp"),
            P(("shard", "ctx"), "tp"),
            P(None, "tp", ("shard", "ctx")),
            P(("shard", "ctx")),
            P(("shard", "ctx"), None),
            P(None, ("shard", "ctx"), "tp"),
            P(None, ("shard", "ctx"), "tp"),
            P(None, "tp", ("shard", "ctx")),
            P(None, ("shard", "ctx"), "tp"),
            P(("shard", "ctx"), "tp"),
        ),
        check_vma=False,
    )
```

profile of v0, /device:TPU:0, one launch (start us, length us, event | category | flops | bytes accessed | tf_op | source)
XLA Modules:
  0.0 4158.2 jit_solution(11190154895753599326)
XLA Ops:
  69.7 42.4 %all-gather.12.cloned.1.call-done = bf16[2048,512]{1,0:T(8,128)(2,1)} async-done(((bf16[256,512]{1,0:T(8,128)(2,1)}), bf16[2048,512]{1,0:T(8,128)(2,1)}) %all-gather.12.cloned.1.call-update) | async-done | bytes 2097168 | tf_op jit(solution)/shard_map/all_gather | solution.py:153
  135.5 27.5 all_gather.40
  192.2 113.2 %all-gather.16.cloned.1.call-done = bf16[4,2048,512]{2,1,0:T(8,128)(2,1)} async-done(((bf16[4,256,512]{2,1,0:T(8,128)(2,1)}), bf16[4,2048,512]{2,1,0:T(8,128)(2,1)}) %all-gather.16.cloned.1.call-update) | async-done | bytes 8388624 | tf_op jit(solution)/shard_map/all_gather | solution.py:151
  344.6 86.2 %all-gather.22.cloned.1.call-done = bf16[4,512,2048]{2,1,0:T(8,128)(2,1)} async-done(((bf16[4,512,256]{2,1,0:T(8,128)(2,1)}), bf16[4,512,2048]{2,1,0:T(8,128)(2,1)}) %all-gather.22.cloned.1.call-update) | async-done | bytes 8388624 | tf_op jit(solution)/shard_map/all_gather | solution.py:154
  514.5 29.8 all_gather.48
  567.7 401.2 %all-gather.24.cloned.1.call-done = bf16[4,2048,1408]{2,1,0:T(8,128)(2,1)} async-done(((bf16[4,256,1408]{2,1,0:T(8,128)(2,1)}), bf16[4,2048,1408]{2,1,0:T(8,128)(2,1)}) %all-gather.24.cloned.1.call-update) | async-done | bytes 23068688 | tf_op jit(solution)/shard_map/all_gather | solution.py:239
  984.3 428.6 %all-gather.26.cloned.1.call-done = bf16[4,2048,1408]{2,1,0:T(8,128)(2,1)} async-done(((bf16[4,256,1408]{2,1,0:T(8,128)(2,1)}), bf16[4,2048,1408]{2,1,0:T(8,128)(2,1)}) %all-gather.26.cloned.1.call-update) | async-done | bytes 23068688 | tf_op jit(solution)/shard_map/all_gather | solution.py:240
  1427.2 431.4 %all-gather.28.cloned.1.call-done = bf16[4,1408,2048]{2,1,0:T(8,128)(2,1)} async-done(((bf16[4,1408,256]{2,1,0:T(8,128)(2,1)}), bf16[4,1408,2048]{2,1,0:T(8,128)(2,1)}) %all-gather.28.cloned.1.call-update) | async-done | bytes 23068688 | tf_op jit(solution)/shard_map/all_gather | solution.py:241
  2373.5 36.6 reduce-scatter.31.cloned.1.call-done
  2411.9 69.0 %reduce-scatter.33.cloned.1.call-done = bf16[256,512]{1,0:T(8,128)(2,1)} async-done(((bf16[2048,512]{1,0:T(8,128)(2,1)}), bf16[256,512]{1,0:T(8,128)(2,1)}) %reduce-scatter.33.cloned.1.call-update) | async-done | bytes 262160 | tf_op jit(solution)/shard_map/reduce_scatter | solution.py:470
  2482.7 111.4 %reduce-scatter.43.cloned.1.call-done = bf16[256,1408]{1,0:T(8,128)(2,1)} async-done(((bf16[2048,1408]{1,0:T(8,128)(2,1)}), bf16[256,1408]{1,0:T(8,128)(2,1)}) %reduce-scatter.43.cloned.1.call-update) | async-done | bytes 720912 | tf_op jit(solution)/shard_map/reduce_scatter | solution.py:297
  2594.1 113.9 %reduce-scatter.41.cloned.1.call-done = bf16[256,1408]{1,0:T(8,128)(2,1)} async-done(((bf16[2048,1408]{1,0:T(8,128)(2,1)}), bf16[256,1408]{1,0:T(8,128)(2,1)}) %reduce-scatter.41.cloned.1.call-update) | async-done | bytes 720912 | tf_op jit(solution)/shard_map/reduce_scatter | solution.py:297
  2708.0 114.0 %reduce-scatter.39.cloned.1.call-done = bf16[256,1408]{1,0:T(8,128)(2,1)} async-done(((bf16[2048,1408]{1,0:T(8,128)(2,1)}), bf16[256,1408]{1,0:T(8,128)(2,1)}) %reduce-scatter.39.cloned.1.call-update) | async-done | bytes 720912 | tf_op jit(solution)/shard_map/reduce_scatter | solution.py:297
  2822.0 113.4 %reduce-scatter.37.cloned.1.call-done = bf16[256,1408]{1,0:T(8,128)(2,1)} async-done(((bf16[2048,1408]{1,0:T(8,128)(2,1)}), bf16[256,1408]{1,0:T(8,128)(2,1)}) %reduce-scatter.37.cloned.1.call-update) | async-done | bytes 720912 | tf_op jit(solution)/shard_map/reduce_scatter | solution.py:297
  2940.2 108.6 %reduce-scatter.51.cloned.1.call-done = bf16[256,1408]{1,0:T(8,128)(2,1)} async-done(((bf16[2048,1408]{1,0:T(8,128)(2,1)}), bf16[256,1408]{1,0:T(8,128)(2,1)}) %reduce-scatter.51.cloned.1.call-update) | async-done | bytes 720912 | tf_op jit(solution)/shard_map/reduce_scatter | solution.py:303
  3048.8 113.3 %reduce-scatter.49.cloned.1.call-done = bf16[256,1408]{1,0:T(8,128)(2,1)} async-done(((bf16[2048,1408]{1,0:T(8,128)(2,1)}), bf16[256,1408]{1,0:T(8,128)(2,1)}) %reduce-scatter.49.cloned.1.call-update) | async-done | bytes 720912 | tf_op jit(solution)/shard_map/reduce_scatter | solution.py:303
  3162.1 113.4 %reduce-scatter.47.cloned.1.call-done = bf16[256,1408]{1,0:T(8,128)(2,1)} async-done(((bf16[2048,1408]{1,0:T(8,128)(2,1)}), bf16[256,1408]{1,0:T(8,128)(2,1)}) %reduce-scatter.47.cloned.1.call-update) | async-done | bytes 720912 | tf_op jit(solution)/shard_map/reduce_scatter | solution.py:303
  3275.5 113.3 %reduce-scatter.45.cloned.1.call-done = bf16[256,1408]{1,0:T(8,128)(2,1)} async-done(((bf16[2048,1408]{1,0:T(8,128)(2,1)}), bf16[256,1408]{1,0:T(8,128)(2,1)}) %reduce-scatter.45.cloned.1.call-update) | async-done | bytes 720912 | tf_op jit(solution)/shard_map/reduce_scatter | solution.py:303
  3393.6 108.9 %reduce-scatter.59.cloned.1.call-done = bf16[1408,256]{1,0:T(8,128)(2,1)} async-done(((bf16[1408,2048]{1,0:T(8,128)(2,1)}), bf16[1408,256]{1,0:T(8,128)(2,1)}) %reduce-scatter.59.cloned.1.call-update) | async-done | bytes 720912 | tf_op jit(solution)/shard_map/reduce_scatter | solution.py:306
  3502.5 113.8 %reduce-scatter.57.cloned.1.call-done = bf16[1408,256]{1,0:T(8,128)(2,1)} async-done(((bf16[1408,2048]{1,0:T(8,128)(2,1)}), bf16[1408,256]{1,0:T(8,128)(2,1)}) %reduce-scatter.57.cloned.1.call-update) | async-done | bytes 720912 | tf_op jit(solution)/shard_map/reduce_scatter | solution.py:306
  3616.3 113.8 %reduce-scatter.55.cloned.1.call-done = bf16[1408,256]{1,0:T(8,128)(2,1)} async-done(((bf16[1408,2048]{1,0:T(8,128)(2,1)}), bf16[1408,256]{1,0:T(8,128)(2,1)}) %reduce-scatter.55.cloned.1.call-update) | async-done | bytes 720912 | tf_op jit(solution)/shard_map/reduce_scatter | solution.py:306
  3730.1 113.7 %reduce-scatter.53.cloned.1.call-done = bf16[1408,256]{1,0:T(8,128)(2,1)} async-done(((bf16[1408,2048]{1,0:T(8,128)(2,1)}), bf16[1408,256]{1,0:T(8,128)(2,1)}) %reduce-scatter.53.cloned.1.call-update) | async-done | bytes 720912 | tf_op jit(solution)/shard_map/reduce_scatter | solution.py:306
  3848.6 147.7 %reduce-scatter.29.cloned.1.call-done = bf16[4,256,512]{2,1,0:T(8,128)(2,1)} async-done(((bf16[4,2048,512]{2,1,0:T(8,128)(2,1)}), bf16[4,256,512]{2,1,0:T(8,128)(2,1)}) %reduce-scatter.29.cloned.1.call-update) | async-done | bytes 1048592 | tf_op jit(solution)/shard_map/reduce_scatter | solution.py:464
  3999.1 149.6 %reduce-scatter.35.cloned.1.call-done = bf16[4,512,256]{2,1,0:T(8,128)(2,1)} async-done(((bf16[4,512,2048]{2,1,0:T(8,128)(2,1)}), bf16[4,512,256]{2,1,0:T(8,128)(2,1)}) %reduce-scatter.35.cloned.1.call-update) | async-done | bytes 1048592 | tf_op jit(solution)/shard_map/reduce_scatter | solution.py:473
  (536 shorter events, 826.9 us)
Async XLA Ops:
  116.0 314.8 %all-gather.22.cloned.1.call-start = ((), (), s32[]{:S(2)}) async-start(), calls=%async_computation.25 | async-start | bytes 9437184 | tf_op jit(solution)/shard_map/all_gather | solution.py:154
  116.5 429.0 %all-reduce.8.cloned.1.call-start = ((), (), s32[]{:S(2)}) async-start(), calls=%async_computation.26 | async-start | bytes 5242880 | tf_op jit(solution)/shard_map/psum | solution.py:230
  467.9 501.0 %all-gather.24.cloned.1.call-start = ((), (), s32[]{:S(2)}) async-start(), calls=%async_computation.27 | async-start | bytes 25952256 | tf_op jit(solution)/shard_map/all_gather | solution.py:239
  468.7 944.1 %all-gather.26.cloned.1.call-start = ((), (), s32[]{:S(2)}) async-start(), calls=%async_computation.28 | async-start | bytes 25952256 | tf_op jit(solution)/shard_map/all_gather | solution.py:240
  469.5 1389.1 %all-gather.28.cloned.1.call-start = ((), (), s32[]{:S(2)}) async-start(), calls=%async_computation.29 | async-start | bytes 25952256 | tf_op jit(solution)/shard_map/all_gather | solution.py:241
  470.0 1521.9 %all-reduce.10.cloned.1.call-start = ((), (), s32[]{:S(2)}) async-start(), calls=%async_computation.30 | async-start | bytes 5242880 | tf_op jit(solution)/shard_map/psum | solution.py:317
  1933.8 248.0 %reduce-scatter.25.cloned.1.call-start = ((), (), s32[]{:S(2)}) async-start(), calls=%async_computation.31 | async-start | bytes 1638400 | tf_op jit(solution)/shard_map/reduce_scatter | solution.py:387
  2115.1 198.8 %reduce-scatter.63.cloned.1.call-start = ((), (), s32[]{:S(2)}) async-start(), calls=%async_computation.50 | async-start | bytes 589824
  2192.8 217.3 %reduce-scatter.31.cloned.1.call-start = ((), (), s32[]{:S(2)}) async-start(), calls=%async_computation.34 | async-start | bytes 2359296 | tf_op jit(solution)/shard_map/reduce_scatter | solution.py:467
  2196.5 284.4 %reduce-scatter.33.cloned.1.call-start = ((), (), s32[]{:S(2)}) async-start(), calls=%async_computation.35 | async-start | bytes 2359296 | tf_op jit(solution)/shard_map/reduce_scatter | solution.py:470
  2199.2 394.9 %reduce-scatter.43.cloned.1.call-start = ((), (), s32[]{:S(2)}) async-start(), calls=%async_computation.40 | async-start | bytes 6488064 | tf_op jit(solution)/shard_map/reduce_scatter | solution.py:297
  2209.4 498.6 %reduce-scatter.41.cloned.1.call-start = ((), (), s32[]{:S(2)}) async-start(), calls=%async_computation.39 | async-start | bytes 6488064 | tf_op jit(solution)/shard_map/reduce_scatter | solution.py:297
  2214.9 607.1 %reduce-scatter.39.cloned.1.call-start = ((), (), s32[]{:S(2)}) async-start(), calls=%async_computation.38 | async-start | bytes 6488064 | tf_op jit(solution)/shard_map/reduce_scatter | solution.py:297
  2220.4 715.0 %reduce-scatter.37.cloned.1.call-start = ((), (), s32[]{:S(2)}) async-start(), calls=%async_computation.37 | async-start | bytes 6488064 | tf_op jit(solution)/shard_map/reduce_scatter | solution.py:297
  2226.0 822.8 %reduce-scatter.51.cloned.1.call-start = ((), (), s32[]{:S(2)}) async-start(), calls=%async_computation.44 | async-start | bytes 6488064 | tf_op jit(solution)/shard_map/reduce_scatter | solution.py:303
  2231.5 930.6 %reduce-scatter.49.cloned.1.call-start = ((), (), s32[]{:S(2)}) async-start(), calls=%async_computation.43 | async-start | bytes 6488064 | tf_op jit(solution)/shard_map/reduce_scatter | solution.py:303
  2237.0 1038.5 %reduce-scatter.47.cloned.1.call-start = ((), (), s32[]{:S(2)}) async-start(), calls=%async_computation.42 | async-start | bytes 6488064 | tf_op jit(solution)/shard_map/reduce_scatter | solution.py:303
  2242.4 1146.4 %reduce-scatter.45.cloned.1.call-start = ((), (), s32[]{:S(2)}) async-start(), calls=%async_computation.41 | async-start | bytes 6488064 | tf_op jit(solution)/shard_map/reduce_scatter | solution.py:303
  2247.9 1254.6 %reduce-scatter.59.cloned.1.call-start = ((), (), s32[]{:S(2)}) async-start(), calls=%async_computation.48 | async-start | bytes 6488064 | tf_op jit(solution)/shard_map/reduce_scatter | solution.py:306
  2254.7 1361.6 %reduce-scatter.57.cloned.1.call-start = ((), (), s32[]{:S(2)}) async-start(), calls=%async_computation.47 | async-start | bytes 6488064 | tf_op jit(solution)/shard_map/reduce_scatter | solution.py:306
  2260.0 1470.1 %reduce-scatter.55.cloned.1.call-start = ((), (), s32[]{:S(2)}) async-start(), calls=%async_computation.46 | async-start | bytes 6488064 | tf_op jit(solution)/shard_map/reduce_scatter | solution.py:306
  2265.8 1578.0 %reduce-scatter.53.cloned.1.call-start = ((), (), s32[]{:S(2)}) async-start(), calls=%async_computation.45 | async-start | bytes 6488064 | tf_op jit(solution)/shard_map/reduce_scatter | solution.py:306
  2271.1 1725.1 %reduce-scatter.29.cloned.1.call-start = ((), (), s32[]{:S(2)}) async-start(), calls=%async_computation.33 | async-start | bytes 9437184 | tf_op jit(solution)/shard_map/reduce_scatter | solution.py:464
  2279.9 1868.9 %reduce-scatter.35.cloned.1.call-start = ((), (), s32[]{:S(2)}) async-start(), calls=%async_computation.36 | async-start | bytes 9437184 | tf_op jit(solution)/shard_map/reduce_scatter | solution.py:473
  (95 other events, 4076.0 us)
Sparse Core Ops, SparseCore 0:
  181.4 123.8 all-gather.15
  307.2 123.5 all-gather.21
  527.7 441.1 all-gather.23
  970.5 442.2 all-gather.25
  1414.2 444.3 all-gather.27
  2150.3 60.6 reduce-scatter.62
  2215.2 60.8 reduce-scatter.60
  2278.9 59.0 all-reduce.11
  2342.0 68.0 reduce-scatter.30
  2414.1 66.7 reduce-scatter.32
  2485.1 108.9 reduce-scatter.42
  2598.2 109.7 reduce-scatter.40
  2712.2 109.7 reduce-scatter.38
  2825.6 109.7 reduce-scatter.36
  2939.0 109.7 reduce-scatter.50
  3052.3 109.7 reduce-scatter.48
  3165.7 109.7 reduce-scatter.46
  3279.0 109.7 reduce-scatter.44
  3392.3 110.1 reduce-scatter.58
  3506.1 110.1 reduce-scatter.56
  3620.0 110.0 reduce-scatter.54
  3733.6 110.1 reduce-scatter.52
  3847.4 148.8 reduce-scatter.28
  4000.4 148.3 reduce-scatter.34
  (8 shorter events, 341.1 us)
where the time goes:
time: 4170 us; the launch traced here: 4160 us
  waiting for transfers between devices  3310 us (79%)
  matrix products  283 us (7%)
  local copies, waits for them, and re-layouts  266 us (6%)
  blocking collectives  155 us (4%)
  other arithmetic  128 us (3%)
    reduce_scatter x4, waiting for transfers between devices, on_device(): lax.psum_scatter(gate_term.astype(jnp.bfloat16), ('shard', 'ctx'), scatte...  453 us
    reduce_scatter x4, waiting for transfers between devices, on_device(): lax.psum_scatter(down_term.astype(jnp.bfloat16), ('shard', 'ctx'), scatte...  450 us
    reduce_scatter x4, waiting for transfers between devices, on_device(): lax.psum_scatter(up_term.astype(jnp.bfloat16), ('shard', 'ctx'), scatter_...  449 us
    all_gather x1, waiting for transfers between devices, on_device(): lax.all_gather(down_weight, ('shard', 'ctx'), axis=2, tiled=True)  431 us
    all_gather x1, waiting for transfers between devices, on_device(): lax.all_gather(up_weight, ('shard', 'ctx'), axis=1, tiled=True)  429 us
    all_gather x1, waiting for transfers between devices, on_device(): lax.all_gather(gate_weight, ('shard', 'ctx'), axis=1, tiled=True)  401 us
    reduce_scatter x1, waiting for transfers between devices, on_device(): lax.psum_scatter(output_term.astype(jnp.bfloat16), ('shard', 'ctx'), scat...  150 us
    reduce_scatter x1, waiting for transfers between devices, on_device(): lax.psum_scatter(query_term.astype(jnp.bfloat16), ('shard', 'ctx'), scatt...  148 us
  transfers between devices with their start and end apart: 32, of which 25 were waited for; matrix products, arithmetic and copies ran while one was open for 11% of the time, Pallas kernels for 0%

commit v1 on v0

--- a/solution.py
+++ b/solution.py
@@ -1,6 +1,8 @@
 import jax
 import jax.numpy as jnp
 from jax import lax
+from jax.experimental import pallas as pl
+from jax.experimental.pallas import tpu as pltpu
 from jax.sharding import PartitionSpec as P
 
 HEAD_DIM = 128
@@ -115,7 +117,7 @@
     )
 
 
-def on_device(
+def on_device_general(
     inputs,
     parents,
     attention_routes,
@@ -503,6 +505,610 @@
     )
 
 
+def along(value, axis, step):
+    count = lax.axis_size(axis)
+    if step % count == 0:
+        return value
+    return lax.ppermute(value, axis, [(place, (place + step) % count) for place in range(count)])
+
+
+def across(value, bits):
+    count = lax.axis_size("tp")
+    return lax.ppermute(value, "tp", [(place, place ^ bits) for place in range(count)])
+
+
+def f32(value):
+    return value.astype(jnp.float32)
+
+
+def bf16(value):
+    return value.astype(jnp.bfloat16)
+
+
+def dot(left, right, contract):
+    return lax.dot_general(
+        left, right, ((contract[:1], contract[1:]), ((), ())), preferred_element_type=jnp.float32
+    )
+
+
+def gather_tokens(own):
+    blocks = []
+    for step in range(lax.axis_size("ctx")):
+        first = along(own, "ctx", step)
+        second = across(first, 2)
+        blocks += [first, across(first, 1), second, across(second, 1)]
+    return jnp.concatenate(blocks, axis=0)
+
+
+def scatter_tokens(part):
+    steps = lax.axis_size("ctx")
+    pieces = part.reshape((steps, 2, 2, part.shape[0] // (4 * steps)) + part.shape[1:])
+    total = None
+    for step in range(steps - 1, -1, -1):
+        piece = pieces[step]
+        upper = across(bf16(piece[1, 1]), 1)
+        lower = across(bf16(piece[0, 1]), 1)
+        high = f32(piece[1, 0]) + f32(upper)
+        low = f32(piece[0, 0]) + f32(lower)
+        done = low + f32(across(bf16(high), 2))
+        if step:
+            done = f32(along(bf16(done), "ctx", -step))
+        total = done if total is None else total + done
+    return total
+
+
+def scatter_small(part):
+    steps = lax.axis_size("ctx")
+    half = part[:, :, 0::2] + across(part[:, :, 1::2], 1)
+    done = half[:, :, 0] + across(half[:, :, 1], 2)
+    return [along(done[:, step], "ctx", -step) for step in range(steps)]
+
+
+def share_out(own):
+    rows = own.shape[0]
+    second = across(own, 2)
+    blocks = [own, across(own, 1), second, across(second, 1)]
+    place = lax.axis_index("tp")
+    whole = jnp.zeros((rows * 4, own.shape[1]), own.dtype)
+    for bits in range(4):
+        whole = lax.dynamic_update_slice(whole, blocks[bits], ((place ^ bits) * rows, 0))
+    return whole
+
+
+def spread_weight(parts, whole, column):
+    steps, rows = parts.shape[0], parts.shape[1]
+    shards = lax.axis_size("shard")
+    here, side = lax.axis_index("ctx"), lax.axis_index("shard")
+    for step in range(steps):
+        mine = lax.dynamic_index_in_dim(parts, (here + step) % steps, 0, keepdims=False)
+        mine = along(mine, "ctx", step)
+        source = (here - step) % steps
+        for turn in range(shards):
+            block = along(mine, "shard", turn)
+            row = (((side - turn) % shards) * steps + source) * rows
+            whole = lax.dynamic_update_slice(whole, block, (row, column))
+    return whole
+
+
+def return_gradient(term):
+    steps, shards = lax.axis_size("ctx"), lax.axis_size("shard")
+    rows = term.shape[0] // (steps * shards)
+    here, side = lax.axis_index("ctx"), lax.axis_index("shard")
+    result = []
+    for step in range(steps):
+        target = (here + step) % steps
+        total = None
+        for turn in range(shards):
+            row = (((side + turn) % shards) * steps + target) * rows
+            piece = lax.dynamic_slice(term, (row, 0), (rows, term.shape[1]))
+            piece = f32(along(piece, "shard", turn))
+            total = piece if total is None else total + piece
+        result.append(along(bf16(total), "ctx", step))
+    return result
+
+
+def in_order(blocks):
+    steps = len(blocks)
+    here = lax.axis_index("ctx")
+    whole = jnp.zeros((steps,) + blocks[0].shape, jnp.float32)
+    for step in range(steps):
+        whole = lax.dynamic_update_slice(
+            whole, f32(blocks[step])[None], ((here - step) % steps,) + (0,) * blocks[0].ndim
+        )
+    return whole
+
+
+def attend_kernel(q_ref, k_ref, v_ref, bias_ref, mixed_ref, norm_ref, peak_ref):
+    scale = HEAD_DIM ** (-0.5)
+    scores = dot(q_ref[...], k_ref[...], (1, 1)) * scale + f32(bias_ref[...])
+    peak = jnp.max(scores, axis=-1, keepdims=True)
+    weights = jnp.exp(scores - peak)
+    total = jnp.sum(weights, axis=-1, keepdims=True)
+    mixed_ref[...] = bf16(dot(bf16(weights / total), v_ref[...], (1, 0)))
+    norm_ref[...] = jnp.broadcast_to(peak + jnp.log(total), norm_ref.shape)
+    peak_ref[...] = jnp.broadcast_to(jnp.max(peak, axis=0, keepdims=True), peak_ref.shape)
+
+
+def attend_back_kernel(
+    q_ref, k_ref, v_ref, bias_ref, norm_ref, back_ref, dq_ref, dk_ref, dv_ref
+):
+    scale = HEAD_DIM ** (-0.5)
+
+    @pl.when(pl.program_id(0) == 0)
+    def _():
+        dk_ref[...] = jnp.zeros_like(dk_ref)
+        dv_ref[...] = jnp.zeros_like(dv_ref)
+
+    scores = dot(q_ref[...], k_ref[...], (1, 1)) * scale + f32(bias_ref[...])
+    chances = jnp.exp(scores - norm_ref[:, :1])
+    dv_ref[...] += dot(bf16(chances), back_ref[...], (0, 0))
+    share_back = dot(back_ref[...], v_ref[...], (1, 1))
+    score_back = bf16(
+        chances * (share_back - jnp.sum(chances * share_back, axis=-1, keepdims=True))
+    )
+    dq_ref[...] = dot(score_back, k_ref[...], (1, 0)) * scale
+    dk_ref[...] += dot(score_back, q_ref[...], (0, 0)) * scale
+
+
+ROWS = 256
+
+
+def attend(queries, keys, values, bias):
+    rows, size = queries.shape
+    count = keys.shape[0]
+    turns = count // ROWS
+    row = pl.BlockSpec((ROWS, size), lambda i: (i, 0))
+    whole = pl.BlockSpec((count, size), lambda i: (0, 0))
+    return pl.pallas_call(
+        attend_kernel,
+        grid=(rows // ROWS,),
+        in_specs=[row, whole, whole, pl.BlockSpec((ROWS, count), lambda i: (i % turns, 0))],
+        out_specs=[row, row, pl.BlockSpec((8, size), lambda i: (i, 0))],
+        out_shape=[
+            jax.ShapeDtypeStruct((rows, size), jnp.bfloat16),
+            jax.ShapeDtypeStruct((rows, size), jnp.float32),
+            jax.ShapeDtypeStruct((rows // ROWS * 8, size), jnp.float32),
+        ],
+        compiler_params=pltpu.CompilerParams(vmem_limit_bytes=48 * 1024 * 1024),
+        cost_estimate=pl.CostEstimate(
+            flops=4 * rows * count * size,
+            bytes_accessed=4 * rows * size * 2 + 2 * count * count * 2,
+            transcendentals=rows * count,
+        ),
+    )(queries, keys, values, bias)
+
+
+def attend_back(queries, keys, values, bias, norm, back):
+    rows, size = queries.shape
+    count = keys.shape[0]
+    turns = count // ROWS
+    row = pl.BlockSpec((ROWS, size), lambda i: (i, 0))
+    whole = pl.BlockSpec((count, size), lambda i: (0, 0))
+    return pl.pallas_call(
+        attend_back_kernel,
+        grid=(rows // ROWS,),
+        in_specs=[
+            row, whole, whole, pl.BlockSpec((ROWS, count), lambda i: (i % turns, 0)), row, row
+        ],
+        out_specs=[row, whole, whole],
+        out_shape=[
+            jax.ShapeDtypeStruct((rows, size), jnp.float32),
+            jax.ShapeDtypeStruct((count, size), jnp.float32),
+            jax.ShapeDtypeStruct((count, size), jnp.float32),
+        ],
+        compiler_params=pltpu.CompilerParams(vmem_limit_bytes=48 * 1024 * 1024),
+        cost_estimate=pl.CostEstimate(
+            flops=10 * rows * count * size,
+            bytes_accessed=6 * rows * size * 2 + 2 * count * count * 2,
+            transcendentals=rows * count,
+        ),
+    )(queries, keys, values, bias, norm, back)
+
+
+def pair_gates(logits, routes):
+    chosen = []
+    for choice in range(TOP):
+        chosen.append(
+            sum(
+                jnp.where(routes[choice] == expert, logits[expert], 0.0)
+                for expert in range(logits.shape[0])
+            )
+        )
+    top = jnp.maximum(chosen[0], chosen[1])
+    powers = [jnp.exp(item - top) for item in chosen]
+    return [power / (powers[0] + powers[1]) for power in powers]
+
+
+def pair_gates_back(changes, gates, routes, experts):
+    mean = gates[0] * changes[0] + gates[1] * changes[1]
+    chosen = [gates[choice] * (changes[choice] - mean) for choice in range(TOP)]
+    return jnp.stack(
+        [
+            sum(jnp.where(routes[choice] == expert, chosen[choice], 0.0) for choice in range(TOP))
+            for expert in range(experts)
+        ]
+    )
+
+
+def swap_halves(value):
+    half = value.shape[-1] // 2
+    return jnp.concatenate([value[..., half:], value[..., :half]], axis=-1)
+
+
+def small_gradient(part):
+    steps, shards = lax.axis_size("ctx"), lax.axis_size("shard")
+    here, side = lax.axis_index("ctx"), lax.axis_index("shard")
+    part = part + across(part, 1) + across(part, 2) + across(part, 3)
+    pieces = part.reshape(part.shape[0], shards, steps, part.shape[1] // (shards * steps))
+    total = None
+    for turn in range(shards):
+        for step in range(steps):
+            piece = lax.dynamic_slice(
+                pieces,
+                (0, (side + turn) % shards, (here + step) % steps, 0),
+                (pieces.shape[0], 1, 1, pieces.shape[3]),
+            )[:, 0, 0]
+            piece = along(along(piece, "shard", turn), "ctx", step)
+            total = piece if total is None else total + piece
+    return total
+
+
+def on_device_fast(
+    inputs,
+    parents,
+    attention_routes,
+    expert_routes,
+    attention_gain,
+    attention_router,
+    query_weight,
+    key_weight,
+    value_weight,
+    output_weight,
+    expert_gain,
+    expert_router,
+    gate_weight,
+    up_weight,
+    down_weight,
+    cotangent,
+):
+    count, width = inputs.shape
+    experts, depth_here, local_width = query_weight.shape
+    hidden = gate_weight.shape[2]
+    steps, shards, tps = lax.axis_size("ctx"), lax.axis_size("shard"), lax.axis_size("tp")
+    here, side, place = lax.axis_index("ctx"), lax.axis_index("shard"), lax.axis_index("tp")
+    heads = local_width // HEAD_DIM
+    rows = count // tps
+    tokens = count * steps
+    capacity = CAP
+
+    own_inputs = lax.dynamic_slice(inputs, (place * rows, 0), (rows, width))
+    all_inputs = gather_tokens(own_inputs)
+    small = jnp.concatenate(
+        [attention_gain[None], expert_gain[None], attention_router.T, expert_router.T], axis=0
+    )
+    relative = [along(small, "ctx", step) for step in range(steps)]
+    relative = jnp.stack(
+        [jnp.stack([along(item, "shard", turn) for item in relative]) for turn in range(shards)]
+    )
+    side_order = (side - jnp.arange(shards)) % shards
+    here_order = (here - jnp.arange(steps)) % steps
+    small_all = relative[side_order][:, here_order]
+    small_all = small_all.transpose(2, 0, 1, 3).reshape(small.shape[0], width)
+    gain_first, gain_second = f32(small_all[0]), f32(small_all[1])
+    router_first, router_second = small_all[2 : 2 + experts], small_all[2 + experts :]
+
+    routes = jnp.concatenate([attention_routes.T, expert_routes.T], axis=0)
+    bits_order = place ^ jnp.arange(tps)
+    routes_here = routes.reshape(2 * TOP, tps, rows)[:, bits_order]
+    routes_all = jnp.concatenate(
+        [along(routes_here, "ctx", step).reshape(2 * TOP, count) for step in range(steps)], axis=1
+    )
+    head_routes, expert_routes_all = routes_all[:TOP], routes_all[TOP:]
+    own_head_routes = routes_here[:TOP, 0]
+    own_expert_routes = routes_here[TOP:, 0]
+
+    query_parts = query_weight.reshape(experts, depth_here, heads, HEAD_DIM)
+    query_parts = query_parts.transpose(2, 1, 0, 3).reshape(heads, depth_here, experts * HEAD_DIM)
+    key_parts = key_weight.reshape(depth_here, heads, HEAD_DIM).transpose(1, 0, 2)
+    value_parts = value_weight.reshape(depth_here, heads, HEAD_DIM).transpose(1, 0, 2)
+    project_parts = jnp.concatenate([query_parts, key_parts, value_parts], axis=2)
+    output_parts = output_weight.reshape(experts, heads, HEAD_DIM, depth_here)
+    output_parts = output_parts.transpose(1, 3, 0, 2).reshape(
+        heads, depth_here, experts * HEAD_DIM
+    )
+    down_parts = down_weight.transpose(0, 2, 1)
+    project = spread_weight(
+        project_parts, jnp.zeros((width, project_parts.shape[2]), jnp.bfloat16), 0
+    )
+    outward = spread_weight(
+        output_parts, jnp.zeros((width, output_parts.shape[2]), jnp.bfloat16), 0
+    )
+    gate_up = spread_weight(gate_weight, jnp.zeros((width, 2 * hidden), jnp.bfloat16), 0)
+    gate_up = spread_weight(up_weight, gate_up, hidden)
+    down = spread_weight(down_parts, jnp.zeros((width, hidden), jnp.bfloat16), 0)
+    own_cotangent = lax.dynamic_slice(cotangent, (place * rows, 0), (rows, width))
+    all_cotangent = gather_tokens(own_cotangent)
+
+    number = jnp.arange(tokens, dtype=jnp.int32)
+    block = number // count
+    bits = (number % count) // rows
+    token = ((here - block) % steps) * count + (place ^ bits) * rows + number % rows
+    unit = token // SEG
+    group_units = tokens // SEG
+    group_first = side * group_units
+    chain = ancestors(parents, group_first + jnp.arange(group_units, dtype=jnp.int32))
+    valid = chain >= 0
+    depth = jnp.sum(valid[:, 1:].astype(jnp.int32), axis=1, dtype=jnp.int32)
+    reached = jnp.any(
+        (chain[:, :, None] - group_first == jnp.arange(group_units, dtype=jnp.int32))
+        & valid[:, :, None],
+        axis=1,
+    )
+    unit_onehot = (unit[:, None] == jnp.arange(group_units, dtype=jnp.int32)[None, :]).astype(
+        jnp.bfloat16
+    )
+    row_reach = bf16(dot(unit_onehot, reached.astype(jnp.bfloat16), (1, 0)))
+    reach = dot(row_reach, unit_onehot, (1, 1))
+    allowed = (reach > 0.5) & (
+        (unit[:, None] != unit[None, :]) | (token[None, :] <= token[:, None])
+    )
+    bias = jnp.where(allowed, 0.0, -1e30).astype(jnp.bfloat16)
+    token_depth = jnp.sum(
+        jnp.where(unit[:, None] == jnp.arange(group_units)[None, :], depth[None, :], 0), axis=1
+    )
+    cosine, sine = rope_tables(token_depth * SEG + token % SEG, HEAD_DIM // 2)
+    cosine = jnp.concatenate([cosine, cosine], axis=1)
+    sine = jnp.concatenate([-sine, sine], axis=1)
+
+    normed = bf16(normalize(f32(all_inputs), gain_first))
+    head_gates = pair_gates(dot(router_first, normed, (1, 1)), head_routes)
+    raw = dot(normed, project, (1, 0))
+    chosen_heads = [
+        [head_routes[choice][:, None] == expert for expert in range(experts)]
+        for choice in range(TOP)
+    ]
+
+    def pick(value, choice):
+        return sum(
+            jnp.where(
+                chosen_heads[choice][expert],
+                value[:, expert * HEAD_DIM : (expert + 1) * HEAD_DIM],
+                0.0,
+            )
+            for expert in range(experts)
+        )
+
+    def place_pair(pair):
+        return jnp.concatenate(
+            [
+                sum(jnp.where(chosen_heads[choice][expert], pair[choice], 0.0) for choice in range(TOP))
+                for expert in range(experts)
+            ],
+            axis=1,
+        )
+
+    def turn(value):
+        return value * cosine + swap_halves(value) * sine
+
+    def turn_back(value):
+        return value * cosine - swap_halves(value) * sine
+
+    inner = experts * HEAD_DIM
+    queries = bf16(jnp.concatenate([turn(pick(raw, choice)) for choice in range(TOP)], axis=0))
+    keys = bf16(turn(raw[:, inner : inner + HEAD_DIM]))
+    values = bf16(raw[:, inner + HEAD_DIM :])
+    mixed, norm, peaks = attend(queries, keys, values, bias)
+    mixed_pair = [f32(mixed[:tokens]), f32(mixed[tokens:])]
+    gated_mixed = bf16(
+        place_pair([head_gates[choice][:, None] * mixed_pair[choice] for choice in range(TOP)])
+    )
+    attention = scatter_tokens(bf16(dot(gated_mixed, outward, (1, 1))))
+    hidden_state = f32(own_inputs) + attention
+    own_normed_two = bf16(normalize(hidden_state, gain_second))
+    normed_two = gather_tokens(own_normed_two)
+
+    expert_gates = pair_gates(dot(router_second, normed_two, (1, 1)), expert_routes_all)
+    named = [expert_routes_all[choice] == here for choice in range(TOP)]
+    gate_of = sum(jnp.where(named[choice], expert_gates[choice], 0.0) for choice in range(TOP))
+    member = (named[0] | named[1]).reshape(steps, count)
+    slot = jnp.cumsum(member.astype(jnp.int32), axis=1) - 1
+    onehot = (
+        (slot[:, None, :] == jnp.arange(capacity, dtype=jnp.int32)[None, :, None])
+        & member[:, None, :]
+    )
+    gate_slot = jnp.sum(
+        jnp.where(onehot, gate_of.reshape(steps, 1, count), 0.0), axis=2
+    ).reshape(steps * capacity, 1)
+    onehot = onehot.astype(jnp.bfloat16)
+
+    def to_slots(value):
+        return bf16(
+            jnp.einsum(
+                "bst,btd->bsd",
+                onehot,
+                value.reshape(steps, count, width),
+                preferred_element_type=jnp.float32,
+            )
+        ).reshape(steps * capacity, width)
+
+    def from_slots(value):
+        return bf16(
+            jnp.einsum(
+                "bst,bsd->btd",
+                onehot,
+                value.reshape(steps, capacity, width),
+                preferred_element_type=jnp.float32,
+            )
+        ).reshape(tokens, width)
+
+    slot_rows = to_slots(normed_two)
+    slot_upstream = to_slots(all_cotangent)
+    both = dot(slot_rows, gate_up, (1, 0))
+    gate_pre, up_pre = both[:, :hidden], both[:, hidden:]
+    act_raw = dot(slot_upstream, down, (1, 0))
+    sigmoid = jax.nn.sigmoid(gate_pre)
+    activated = gate_pre * sigmoid * up_pre
+    gated_act = bf16(activated * gate_slot)
+    gate_back_slot = jnp.sum(activated * act_raw, axis=1)
+    act_back = act_raw * gate_slot
+    both_back = bf16(
+        jnp.concatenate(
+            [
+                act_back * up_pre * sigmoid * (1.0 + gate_pre * (1.0 - sigmoid)),
+                act_back * gate_pre * sigmoid,
+            ],
+            axis=1,
+        )
+    )
+    rows_back = from_slots(bf16(dot(both_back, gate_up, (1, 1))))
+    gate_change = jnp.sum(
+        jnp.where(onehot > 0, gate_back_slot.reshape(steps, capacity, 1), 0.0), axis=1
+    ).reshape(1, steps, tps, rows)
+    normed_two_back = scatter_tokens(rows_back)
+    gate_changes = scatter_small(gate_change)
+    down_blocks = return_gradient(bf16(dot(slot_upstream, gated_act, (0, 0))))
+    gate_up_term = bf16(dot(slot_rows, both_back, (0, 0)))
+    gate_blocks = return_gradient(gate_up_term[:, :hidden])
+    up_blocks = return_gradient(gate_up_term[:, hidden:])
+    feed = scatter_tokens(from_slots(bf16(dot(gated_act, down, (1, 1)))))
+    output = share_out(bf16(hidden_state + feed))
+
+    own_expert_gates = pair_gates(dot(router_second, own_normed_two, (1, 1)), own_expert_routes)
+    expert_gate_back = [
+        sum(
+            jnp.where(own_expert_routes[choice] == (here + step) % steps, gate_changes[step][0], 0.0)
+            for step in range(steps)
+        )
+        for choice in range(TOP)
+    ]
+    expert_logit_back = pair_gates_back(
+        expert_gate_back, own_expert_gates, own_expert_routes, experts
+    )
+    router_second_term = jnp.einsum(
+        "et,td->ed", expert_logit_back, f32(own_normed_two), precision=HIGH
+    )
+    normed_two_back = normed_two_back + jnp.einsum(
+        "et,ed->td", expert_logit_back, f32(router_second), precision=HIGH
+    )
+    hidden_back, gain_second_term = normalize_back(normed_two_back, hidden_state, gain_second)
+    hidden_back = hidden_back + f32(own_cotangent)
+    second_small = small_gradient(
+        jnp.concatenate([gain_second_term[None], router_second_term], axis=0)
+    )
+
+    all_back = gather_tokens(bf16(hidden_back))
+    raw_back = dot(all_back, outward, (1, 0))
+    pair_back = [pick(raw_back, choice) for choice in range(TOP)]
+    head_change = jnp.stack(
+        [jnp.sum(mixed_pair[choice] * pair_back[choice], axis=1) for choice in range(TOP)]
+    )
+    mixed_back = bf16(
+        jnp.concatenate(
+            [head_gates[choice][:, None] * pair_back[choice] for choice in range(TOP)], axis=0
+        )
+    )
+    query_change, key_change, value_change = attend_back(
+        queries, keys, values, bias, norm, mixed_back
+    )
+    change = bf16(
+        jnp.concatenate(
+            [
+                place_pair(
+                    [turn_back(query_change[:tokens]), turn_back(query_change[tokens:])]
+                ),
+                turn_back(f32(bf16(key_change))),
+                value_change,
+            ],
+            axis=1,
+        )
+    )
+    normed_back = scatter_tokens(bf16(dot(change, project, (1, 1))))
+    head_changes = scatter_small(head_change.reshape(TOP, steps, tps, rows))
+    output_blocks = return_gradient(bf16(dot(all_back, gated_mixed, (0, 0))))
+    project_blocks = return_gradient(bf16(dot(normed, change, (0, 0))))
+    own_normed = bf16(normalize(f32(own_inputs), gain_first))
+    own_head_gates = pair_gates(dot(router_first, own_normed, (1, 1)), own_head_routes)
+    head_gate_back = sum(head_changes)
+    head_logit_back = pair_gates_back(
+        [head_gate_back[choice] for choice in range(TOP)],
+        own_head_gates,
+        own_head_routes,
+        experts,
+    )
+    router_first_term = jnp.einsum(
+        "et,td->ed", head_logit_back, f32(own_normed), precision=HIGH
+    )
+    normed_back = normed_back + jnp.einsum(
+        "et,ed->td", head_logit_back, f32(router_first), precision=HIGH
+    )
+    input_back, gain_first_term = normalize_back(normed_back, f32(own_inputs), gain_first)
+    input_gradient = share_out(bf16(input_back + hidden_back))
+    first_small = small_gradient(
+        jnp.concatenate([gain_first_term[None], router_first_term], axis=0)
+    )
+
+    gate_gradient = in_order(gate_blocks)
+    up_gradient = in_order(up_blocks)
+    down_gradient = in_order([item.T for item in down_blocks])
+    project_all = in_order(project_blocks)
+    query_gradient = (
+        project_all[:, :, :inner]
+        .reshape(heads, depth_here, experts, HEAD_DIM)
+        .transpose(2, 1, 0, 3)
+        .reshape(experts, depth_here, local_width)
+    )
+    key_gradient = (
+        project_all[:, :, inner : inner + HEAD_DIM].transpose(1, 0, 2).reshape(depth_here, local_width)
+    )
+    value_gradient = (
+        project_all[:, :, inner + HEAD_DIM :].transpose(1, 0, 2).reshape(depth_here, local_width)
+    )
+    output_gradient = (
+        in_order(output_blocks)
+        .reshape(heads, depth_here, experts, HEAD_DIM)
+        .transpose(2, 0, 3, 1)
+        .reshape(experts, local_width, depth_here)
+    )
+
+    peak = jnp.max(peaks, axis=0, keepdims=True)
+    for turn_by in range(1, shards):
+        peak = jnp.maximum(peak, along(peak, "shard", turn_by))
+    head_peaks = in_order([along(peak, "ctx", step) for step in range(steps)])
+    factor = jnp.sqrt(jnp.minimum(1.0, CLIP / head_peaks)).reshape(local_width)
+    clipped_query = bf16(f32(query_weight) * factor)
+    clipped_key = bf16(f32(key_weight) * factor)
+    return (
+        output,
+        input_gradient,
+        first_small[0],
+        first_small[1:].T,
+        query_gradient,
+        key_gradient,
+        value_gradient,
+        output_gradient,
+        second_small[0],
+        second_small[1:].T,
+        gate_gradient,
+        up_gradient,
+        down_gradient,
+        clipped_query,
+        clipped_key,
+    )
+
+
+def on_device(*arrays):
+    experts, _, local_width = arrays[6].shape
+    steps = lax.axis_size("ctx")
+    tokens = arrays[0].shape[0] * steps
+    fits = (
+        experts == steps
+        and local_width == steps * HEAD_DIM
+        and lax.axis_size("tp") == 4
+        and tokens % ROWS == 0
+    )
+    return on_device_fast(*arrays) if fits else on_device_general(*arrays)
+
+
 def solution(mesh):
     placed = (
         P(("shard", "ctx"), None),

time: 4170 us -> 1510 us (0.36)
  waiting for transfers between devices: 3310 us -> 743 us
  starting transfers between devices: 2.31 us -> 332 us
  matrix products: 283 us -> 115 us
  blocking collectives: 155 us -> 0 us
  local copies, waits for them, and re-layouts: 266 us -> 199 us
  other arithmetic: 128 us -> 73.2 us
    reduce_scatter x18 -> x0, waiting for transfers between devices: 1750 us -> none  [the longest x4 453 us: on_device(): lax.psum_scatter(gate_term.astype(jnp.bfloat16), ('shard', 'ctx'), scatte...]
    all_gather x9 -> x0, waiting for transfers between devices: 1520 us -> none  [the longest x1 431 us: on_device(): lax.all_gather(down_weight, ('shard', 'ctx'), axis=2, tiled=True)]
    ppermute x0 -> x246, waiting for transfers between devices: none -> 743 us  [the longest x134 589 us: along(): lax.ppermute(value, axis, [(place, (place + step) % count) for place in r...]
    ppermute x0 -> x246, starting transfers between devices: none -> 332 us  [the longest x134 286 us: along(): lax.ppermute(value, axis, [(place, (place + step) % count) for place in r...]
    dot_general x44 -> x25, matrix products: 283 us -> 115 us  [the longest x17 98.7 us: dot(): lax.dot_general(left, right, ((contract[:1], contract[1:]), ((), ())), pr...]
    all_gather x4 -> x0, blocking collectives: 97.2 us -> none  [the longest x1 29.8 us: on_device(): lax.all_gather(expert_router, ('shard', 'ctx'), axis=0, tiled=True)]
    gather x24 -> x6, local copies, waits for them, and re-layouts: 98.3 us -> 1.85 us  [the longest x4 1.28 us: on_device_fast(): small_all = relative[side_order][:, here_order]]
    reshape x11 -> x9, local copies, waits for them, and re-layouts: 65.7 us -> 0.58 us  [the longest x4 0.34 us: on_device_fast(): along(routes_here, 'ctx', step).reshape(2 * TOP, count)]
  transfers between devices with their start and end apart: 32 -> 246, of which waited for: 25 -> 95; matrix products, arithmetic and copies ran while one was open for 11% -> 18% of each run, Pallas kernels for 0% -> 1%
where the time goes in v1:
time: 1510 us; the launch traced here: 1490 us
  waiting for transfers between devices  743 us (49%)
  starting transfers between devices  332 us (22%)
  local copies, waits for them, and re-layouts  199 us (13%)
  matrix products  115 us (8%)
  other arithmetic  73.2 us (5%)
  Pallas kernels  26.5 us (2%)
    ppermute x134, waiting for transfers between devices, along(): lax.ppermute(value, axis, [(place, (place + step) % count) for place in r...  589 us
    ppermute x134, starting transfers between devices, along(): lax.ppermute(value, axis, [(place, (place + step) % count) for place in r...  286 us
    ppermute x112, waiting for transfers between devices, across(): lax.ppermute(value, 'tp', [(place, place ^ bits) for place in range(count)])  154 us
    dot_general x17, matrix products, dot(): lax.dot_general(left, right, ((contract[:1], contract[1:]), ((), ())), pr...  98.7 us
    unnamed x428, local copies, waits for them, and re-layouts  53.2 us
    ppermute x112, starting transfers between devices, across(): lax.ppermute(value, 'tp', [(place, place ^ bits) for place in range(count)])  46.1 us
    dynamic_update_slice x40, local copies, waits for them, and re-layouts, spread_weight(): whole = lax.dynamic_update_slice(whole, block, (row, column))  41.6 us
  transfers between devices with their start and end apart: 246, of which 95 were waited for; matrix products, arithmetic and copies ran while one was open for 18% of the time, Pallas kernels for 1%

profile of v1, /device:TPU:0, one launch (start us, length us, event | category | flops | bytes accessed | tf_op | source)
XLA Modules:
  0.0 1492.9 jit_solution(3222689162356908402)
XLA Ops:
  100.4 20.5 %collective-permute-done.35 = bf16[256,512]{0,1:T(8,128)(2,1)S(1)} collective-permute-done((bf16[256,512]{0,1:T(8,128)(2,1)}, bf16[256,512]{0,1:T(8,128)(2,1)S(1)}, u32[]{:S(2)}, u32[]{:S(2)}) %collective-permute-start.35) | collective-permute-done | bytes 262176 | tf_op jit(solution)/shard_map/ppermute | solution.py:512
  298.4 14.0 collective-permute-start.71
  315.7 13.4 collective-permute-done.242
  374.2 25.7 %collective-permute-done.86 = bf16[256,1408]{0,1:T(8,128)(2,1)S(1)} collective-permute-done((bf16[256,1408]{0,1:T(8,128)(2,1)S(1)}, bf16[256,1408]{0,1:T(8,128)(2,1)S(1)}, u32[]{:S(2)}, u32[]{:S(2)}) %collective-permute-start.86) | collective-permute-done | bytes 720928 | tf_op jit(solution)/shard_map/ppermute | solution.py:512
  405.4 13.2 collective-permute-done.87
  462.3 19.2 %collective-permute-done.46 = bf16[80,2048]{1,0:T(8,128)(2,1)S(1)} collective-permute-done((bf16[80,2048]{1,0:T(8,128)(2,1)S(1)}, bf16[80,2048]{1,0:T(8,128)(2,1)S(1)}, u32[]{:S(2)}, u32[]{:S(2)}) %collective-permute-start.46) | collective-permute-done | bytes 327712 | tf_op jit(solution)/shard_map/ppermute | solution.py:512
  484.7 35.3 %collective-permute-done.76 = bf16[256,1408]{1,0:T(8,128)(2,1)S(1)} collective-permute-done((bf16[256,1408]{1,0:T(8,128)(2,1)S(1)}, bf16[256,1408]{1,0:T(8,128)(2,1)S(1)}, u32[]{:S(2)}, u32[]{:S(2)}) %collective-permute-start.76) | collective-permute-done | bytes 720928 | tf_op jit(solution)/shard_map/ppermute | solution.py:512
  579.7 13.1 multiply_reduce_fusion
  599.4 12.6 convolution_convert_fusion.9
  758.4 12.9 collective-permute-done.236
  771.2 15.4 %collective-permute-done.235 = bf16[256,1408]{1,0:T(8,128)(2,1)S(1)} collective-permute-done((bf16[256,1408]{1,0:T(8,128)(2,1)S(1)}, bf16[256,1408]{1,0:T(8,128)(2,1)S(1)}, u32[]{:S(2)}, u32[]{:S(2)}) %collective-permute-start.235) | collective-permute-done | bytes 720928 | tf_op jit(solution)/shard_map/ppermute | solution.py:512
  803.8 13.7 collective-permute-done.224
  819.3 13.7 collective-permute-done.222
  864.3 15.2 %collective-permute-done.231 = bf16[256,1408]{1,0:T(8,128)(2,1)} collective-permute-done((bf16[256,1408]{1,0:T(8,128)(2,1)}, bf16[256,1408]{1,0:T(8,128)(2,1)}, u32[]{:S(2)}, u32[]{:S(2)}) %collective-permute-start.231) | collective-permute-done | bytes 720928 | tf_op jit(solution)/shard_map/ppermute | solution.py:512
  938.5 20.2 %collective-permute-done.97 = bf16[80,2048]{1,0:T(8,128)(2,1)} collective-permute-done((bf16[80,2048]{1,0:T(8,128)(2,1)}, bf16[80,2048]{1,0:T(8,128)(2,1)}, u32[]{:S(2)}, u32[]{:S(2)}) %collective-permute-start.97) | collective-permute-done | bytes 327712 | tf_op jit(solution)/shard_map/ppermute | solution.py:512
  996.6 26.9 %collective-permute-done.237 = bf16[256,1408]{1,0:T(8,128)(2,1)S(1)} collective-permute-done((bf16[256,1408]{1,0:T(8,128)(2,1)}, bf16[256,1408]{1,0:T(8,128)(2,1)S(1)}, u32[]{:S(2)}, u32[]{:S(2)}) %collective-permute-start.237) | collective-permute-done | bytes 720928 | tf_op jit(solution)/shard_map/ppermute | solution.py:512
  1024.6 57.8 %collective-permute-done.239 = bf16[256,1408]{1,0:T(8,128)(2,1)S(1)} collective-permute-done((bf16[256,1408]{1,0:T(8,128)(2,1)S(1)}, bf16[256,1408]{1,0:T(8,128)(2,1)S(1)}, u32[]{:S(2)}, u32[]{:S(2)}) %collective-permute-start.239) | collective-permute-done | bytes 720928 | tf_op jit(solution)/shard_map/ppermute | solution.py:512
  1082.4 14.4 collective-permute-start.230
  1098.0 12.9 collective-permute-done.241
  1133.4 19.7 %collective-permute-done.232 = bf16[256,1408]{1,0:T(8,128)(2,1)S(1)} collective-permute-done((bf16[256,1408]{1,0:T(8,128)(2,1)S(1)}, bf16[256,1408]{1,0:T(8,128)(2,1)S(1)}, u32[]{:S(2)}, u32[]{:S(2)}) %collective-permute-start.232) | collective-permute-done | bytes 720928 | tf_op jit(solution)/shard_map/ppermute | solution.py:512
  1222.5 14.7 shard_map.272
  1313.4 15.7 %collective-permute-done.199 = bf16[256,768]{0,1:T(8,128)(2,1)S(1)} collective-permute-done((bf16[256,768]{0,1:T(8,128)(2,1)S(1)}, bf16[256,768]{0,1:T(8,128)(2,1)S(1)}, u32[]{:S(2)}, u32[]{:S(2)}) %collective-permute-start.199) | collective-permute-done | bytes 393248 | tf_op jit(solution)/shard_map/ppermute | solution.py:512
  1419.5 13.1 collective-permute-start.165
  1444.3 12.6 collective-permute-done.161
  (1265 shorter events, 1042.4 us)
Async XLA Ops:
  2.2 59.4 %collective-permute-start = (s32[4,4,80]{2,0,1:T(4,128)S(1)}, s32[4,4,80]{2,0,1:T(4,128)S(1)}, u32[]{:S(2)}, u32[]{:S(2)}) collective-permute-start(s32[4,4,80]{2,0,1:T(4,128)S(1)} %bitcast.927), channel_id=1, source_target_pairs={{0,4},{4,8},{8,12},{12,0},{1,5},{5,9},{9,13},{13,1},{2,6},{6,10},{... | collective-permute-start | bytes 15368 | tf_op jit(solution)/shard_map/ppermute | solution.py:512
  121.0 86.7 %collective-permute-start.17 = (bf16[80,2048]{1,0:T(8,128)(2,1)S(1)}, bf16[80,2048]{1,0:T(8,128)(2,1)S(1)}, u32[]{:S(2)}, u32[]{:S(2)}) collective-permute-start(bf16[80,2048]{1,0:T(8,128)(2,1)S(1)} %get-tuple-element.274), channel_id=1, source_target_pairs={{0,8},{4,12},{8,0},{12,4},{1,9},{5,13},{9,1},{13,5},{2,10},{6,14},... | collective-permute-start | bytes 983048 | tf_op jit(solution)/shard_map/ppermute | solution.py:512
  207.7 72.2 %collective-permute-start.119 = (bf16[80,2048]{1,0:T(8,128)(2,1)S(1)}, bf16[80,2048]{1,0:T(8,128)(2,1)}, u32[]{:S(2)}, u32[]{:S(2)}) collective-permute-start(bf16[80,2048]{1,0:T(8,128)(2,1)S(1)} %get-tuple-element.292), channel_id=1, source_target_pairs={{0,12},{4,0},{8,4},{12,8},{1,13},{5,1},{9,5},{13,9},{2,14},{6,2},{... | collective-permute-start | bytes 983048 | tf_op jit(solution)/shard_map/ppermute | solution.py:512
  217.2 131.9 %collective-permute-start.72 = (bf16[256,1408]{1,0:T(8,128)(2,1)}, bf16[256,1408]{1,0:T(8,128)(2,1)}, u32[]{:S(2)}, u32[]{:S(2)}) collective-permute-start(bf16[256,1408]{1,0:T(8,128)(2,1)} %get-tuple-element.387), channel_id=1, source_target_pairs={{0,8},{4,12},{8,0},{12,4},{1,9},{5,13},{9,1},{13,5},{2,10},{6,14},... | collective-permute-start | bytes 2162696 | tf_op jit(solution)/shard_map/ppermute | solution.py:512
  228.9 127.6 %collective-permute-start.74 = (bf16[256,1408]{1,0:T(8,128)(2,1)}, bf16[256,1408]{1,0:T(8,128)(2,1)}, u32[]{:S(2)}, u32[]{:S(2)}) collective-permute-start(bf16[256,1408]{1,0:T(8,128)(2,1)} %get-tuple-element.385), channel_id=1, source_target_pairs={{0,12},{4,0},{8,4},{12,8},{1,13},{5,1},{9,5},{13,9},{2,14},{6,2},{... | collective-permute-start | bytes 2162696 | tf_op jit(solution)/shard_map/ppermute | solution.py:512
  279.9 170.2 %collective-permute-start.77 = (bf16[256,1408]{1,0:T(8,128)(2,1)}, bf16[256,1408]{1,0:T(8,128)(2,1)}, u32[]{:S(2)}, u32[]{:S(2)}) collective-permute-start(bf16[256,1408]{1,0:T(8,128)(2,1)} %get-tuple-element.383), channel_id=1, source_target_pairs={{0,4},{4,8},{8,12},{12,0},{1,5},{5,9},{9,13},{13,1},{2,6},{6,10},{... | collective-permute-start | bytes 2162696 | tf_op jit(solution)/shard_map/ppermute | solution.py:512
  356.5 93.9 %collective-permute-start.79 = (bf16[256,1408]{1,0:T(8,128)(2,1)S(1)}, bf16[256,1408]{1,0:T(8,128)(2,1)S(1)}, u32[]{:S(2)}, u32[]{:S(2)}) collective-permute-start(bf16[256,1408]{1,0:T(8,128)(2,1)S(1)} %copy-done.69), channel_id=1, source_target_pairs={{0,8},{4,12},{8,0},{12,4},{1,9},{5,13},{9,1},{13,5},{2,10},{6,14},... | collective-permute-start | bytes 2162696 | tf_op jit(solution)/shard_map/ppermute | solution.py:512
  455.6 69.0 %collective-permute-start.78 = (bf16[256,1408]{1,0:T(8,128)(2,1)}, bf16[256,1408]{1,0:T(8,128)(2,1)S(1)}, u32[]{:S(2)}, u32[]{:S(2)}) collective-permute-start(bf16[256,1408]{1,0:T(8,128)(2,1)} %collective-permute-done.77), channel_id=1, source_target_pairs={{0,16},{16,0},{1,17},{17,1},{2,18},{18,2},{3,19},{19,3},{4,20},{20... | collective-permute-start | bytes 2162696 | tf_op jit(solution)/shard_map/ppermute | solution.py:512
  460.3 67.8 %collective-permute-start.80 = (bf16[256,1408]{1,0:T(8,128)(2,1)S(1)}, bf16[256,1408]{1,0:T(8,128)(2,1)S(1)}, u32[]{:S(2)}, u32[]{:S(2)}) collective-permute-start(bf16[256,1408]{1,0:T(8,128)(2,1)S(1)} %collective-permute-done.79), channel_id=1, source_target_pairs={{0,16},{16,0},{1,17},{17,1},{2,18},{18,2},{3,19},{19,3},{4,20},{20... | collective-permute-start | bytes 2162696 | tf_op jit(solution)/shard_map/ppermute | solution.py:512
  462.0 70.6 %collective-permute-start.82 = (bf16[256,1408]{1,0:T(8,128)(2,1)S(1)}, bf16[256,1408]{1,0:T(8,128)(2,1)S(1)}, u32[]{:S(2)}, u32[]{:S(2)}) collective-permute-start(bf16[256,1408]{1,0:T(8,128)(2,1)S(1)} %collective-permute-done.81), channel_id=1, source_target_pairs={{0,16},{16,0},{1,17},{17,1},{2,18},{18,2},{3,19},{19,3},{4,20},{20... | collective-permute-start | bytes 2162696 | tf_op jit(solution)/shard_map/ppermute | solution.py:512
  751.9 65.6 %collective-permute-start.224 = (bf16[256,1408]{1,0:T(8,128)(2,1)S(1)}, bf16[256,1408]{1,0:T(8,128)(2,1)S(1)}, u32[]{:S(2)}, u32[]{:S(2)}) collective-permute-start(bf16[256,1408]{1,0:T(8,128)(2,1)S(1)} %copy-done.83), channel_id=1, source_target_pairs={{0,16},{16,0},{1,17},{17,1},{2,18},{18,2},{3,19},{19,3},{4,20},{20... | collective-permute-start | bytes 2162696 | tf_op jit(solution)/shard_map/ppermute | solution.py:512
  755.8 77.2 %collective-permute-start.222 = (bf16[256,1408]{1,0:T(8,128)(2,1)S(1)}, bf16[256,1408]{1,0:T(8,128)(2,1)S(1)}, u32[]{:S(2)}, u32[]{:S(2)}) collective-permute-start(bf16[256,1408]{1,0:T(8,128)(2,1)S(1)} %copy-done.82), channel_id=1, source_target_pairs={{0,16},{16,0},{1,17},{17,1},{2,18},{18,2},{3,19},{19,3},{4,20},{20... | collective-permute-start | bytes 2162696 | tf_op jit(solution)/shard_map/ppermute | solution.py:512
  771.2 141.8 %collective-permute-start.135 = (bf16[80,2048]{1,0:T(8,128)(2,1)}, bf16[80,2048]{1,0:T(8,128)(2,1)}, u32[]{:S(2)}, u32[]{:S(2)}) collective-permute-start(bf16[80,2048]{1,0:T(8,128)(2,1)} %get-tuple-element.419), channel_id=1, source_target_pairs={{0,1},{1,0},{2,3},{3,2},{4,5},{5,4},{6,7},{7,6},{8,9},{9,8},{10,11... | collective-permute-start | bytes 983048 | tf_op jit(solution)/shard_map/ppermute | solution.py:517
  786.7 61.8 %collective-permute-start.221 = (bf16[256,1408]{1,0:T(8,128)(2,1)S(1)}, bf16[256,1408]{1,0:T(8,128)(2,1)S(1)}, u32[]{:S(2)}, u32[]{:S(2)}) collective-permute-start(bf16[256,1408]{1,0:T(8,128)(2,1)S(1)} %copy-done.80), channel_id=1, source_target_pairs={{0,16},{16,0},{1,17},{17,1},{2,18},{18,2},{3,19},{19,3},{4,20},{20... | collective-permute-start | bytes 2162696 | tf_op jit(solution)/shard_map/ppermute | solution.py:512
  802.1 61.8 %collective-permute-start.233 = (bf16[256,1408]{1,0:T(8,128)(2,1)}, bf16[256,1408]{1,0:T(8,128)(2,1)S(1)}, u32[]{:S(2)}, u32[]{:S(2)}) collective-permute-start(bf16[256,1408]{1,0:T(8,128)(2,1)} %get-tuple-element.343), channel_id=1, source_target_pairs={{0,16},{16,0},{1,17},{17,1},{2,18},{18,2},{3,19},{19,3},{4,20},{20... | collective-permute-start | bytes 2162696 | tf_op jit(solution)/shard_map/ppermute | solution.py:512
  817.6 61.9 %collective-permute-start.231 = (bf16[256,1408]{1,0:T(8,128)(2,1)}, bf16[256,1408]{1,0:T(8,128)(2,1)}, u32[]{:S(2)}, u32[]{:S(2)}) collective-permute-start(bf16[256,1408]{1,0:T(8,128)(2,1)} %get-tuple-element.344), channel_id=1, source_target_pairs={{0,16},{16,0},{1,17},{17,1},{2,18},{18,2},{3,19},{19,3},{4,20},{20... | collective-permute-start | bytes 2162696 | tf_op jit(solution)/shard_map/ppermute | solution.py:512
  833.0 61.9 %collective-permute-start.229 = (bf16[256,1408]{1,0:T(8,128)(2,1)}, bf16[256,1408]{1,0:T(8,128)(2,1)}, u32[]{:S(2)}, u32[]{:S(2)}) collective-permute-start(bf16[256,1408]{1,0:T(8,128)(2,1)} %get-tuple-element.345), channel_id=1, source_target_pairs={{0,16},{16,0},{1,17},{17,1},{2,18},{18,2},{3,19},{19,3},{4,20},{20... | collective-permute-start | bytes 2162696 | tf_op jit(solution)/shard_map/ppermute | solution.py:512
  970.9 150.4 %collective-permute-start.223 = (bf16[256,1408]{1,0:T(8,128)(2,1)}, bf16[256,1408]{1,0:T(8,128)(2,1)S(1)}, u32[]{:S(2)}, u32[]{:S(2)}) collective-permute-start(bf16[256,1408]{1,0:T(8,128)(2,1)} %get-tuple-element.349), channel_id=1, source_target_pairs={{0,4},{4,8},{8,12},{12,0},{1,5},{5,9},{9,13},{13,1},{2,6},{6,10},{... | collective-permute-start | bytes 2162696 | tf_op jit(solution)/shard_map/ppermute | solution.py:512
  972.3 153.7 %collective-permute-start.225 = (bf16[256,1408]{1,0:T(8,128)(2,1)}, bf16[256,1408]{1,0:T(8,128)(2,1)S(1)}, u32[]{:S(2)}, u32[]{:S(2)}) collective-permute-start(bf16[256,1408]{1,0:T(8,128)(2,1)} %get-tuple-element.348), channel_id=1, source_target_pairs={{0,8},{4,12},{8,0},{12,4},{1,9},{5,13},{9,1},{13,5},{2,10},{6,14},... | collective-permute-start | bytes 2162696 | tf_op jit(solution)/shard_map/ppermute | solution.py:512
  987.3 139.9 %collective-permute-start.227 = (bf16[256,1408]{1,0:T(8,128)(2,1)S(1)}, bf16[256,1408]{1,0:T(8,128)(2,1)S(1)}, u32[]{:S(2)}, u32[]{:S(2)}) collective-permute-start(bf16[256,1408]{1,0:T(8,128)(2,1)S(1)} %copy-done.77), channel_id=1, source_target_pairs={{0,12},{4,0},{8,4},{12,8},{1,13},{5,1},{9,5},{13,9},{2,14},{6,2},{... | collective-permute-start | bytes 2162696 | tf_op jit(solution)/shard_map/ppermute | solution.py:512
  995.5 87.0 %collective-permute-start.239 = (bf16[256,1408]{1,0:T(8,128)(2,1)S(1)}, bf16[256,1408]{1,0:T(8,128)(2,1)S(1)}, u32[]{:S(2)}, u32[]{:S(2)}) collective-permute-start(bf16[256,1408]{1,0:T(8,128)(2,1)S(1)} %copy-done.78), channel_id=1, source_target_pairs={{0,8},{4,12},{8,0},{12,4},{1,9},{5,13},{9,1},{13,5},{2,10},{6,14},... | collective-permute-start | bytes 2162696 | tf_op jit(solution)/shard_map/ppermute | solution.py:512
  1023.4 87.5 %collective-permute-start.241 = (bf16[256,1408]{1,0:T(8,128)(2,1)S(1)}, bf16[256,1408]{1,0:T(8,128)(2,1)S(1)}, u32[]{:S(2)}, u32[]{:S(2)}) collective-permute-start(bf16[256,1408]{1,0:T(8,128)(2,1)S(1)} %copy-done.76), channel_id=1, source_target_pairs={{0,12},{4,0},{8,4},{12,8},{1,13},{5,1},{9,5},{13,9},{2,14},{6,2},{... | collective-permute-start | bytes 2162696 | tf_op jit(solution)/shard_map/ppermute | solution.py:512
  1293.8 150.5 %collective-permute-start.170 = (bf16[80,2048]{1,0:T(8,128)(2,1)S(1)}, bf16[80,2048]{1,0:T(8,128)(2,1)S(1)}, u32[]{:S(2)}, u32[]{:S(2)}) collective-permute-start(bf16[80,2048]{1,0:T(8,128)(2,1)S(1)} %get-tuple-element.407), channel_id=1, source_target_pairs={{0,1},{1,0},{2,3},{3,2},{4,5},{5,4},{6,7},{7,6},{8,9},{9,8},{10,11... | collective-permute-start | bytes 983048 | tf_op jit(solution)/shard_map/ppermute | solution.py:517
  1369.9 74.4 %collective-permute-start.172 = (bf16[80,2048]{1,0:T(8,128)(2,1)S(1)}, bf16[80,2048]{1,0:T(8,128)(2,1)S(1)}, u32[]{:S(2)}, u32[]{:S(2)}) collective-permute-start(bf16[80,2048]{1,0:T(8,128)(2,1)S(1)} %fusion.49), channel_id=1, source_target_pairs={{0,2},{1,3},{2,0},{3,1},{4,6},{5,7},{6,4},{7,5},{8,10},{9,11},{10,... | collective-permute-start | bytes 983048 | tf_op jit(solution)/shard_map/ppermute | solution.py:517
  (395 other events, 11097.8 us)

commit v2 on v1

--- a/solution.py
+++ b/solution.py
@@ -5,6 +5,8 @@
 from jax.experimental.pallas import tpu as pltpu
 from jax.sharding import PartitionSpec as P
 
+SHARD, CTX, TP = "shard", "ctx", "tp"
+BOTH = (SHARD, CTX)
 HEAD_DIM = 128
 TOP = 2
 SEG = 64
@@ -145,22 +147,22 @@
     choose = attention_routes.shape[1]
     segment = SEG
     units_here = count // segment
-    group_units = lax.axis_size("ctx") * units_here
+    group_units = lax.axis_size(CTX) * units_here
     scale = head_dim ** (-0.5)
     gain_one, router_one, query_full, key_full, value_full, output_full, gain_two, router_two = (
-        lax.all_gather(attention_gain, ("shard", "ctx"), axis=0, tiled=True),
-        lax.all_gather(attention_router, ("shard", "ctx"), axis=0, tiled=True),
-        lax.all_gather(query_weight, ("shard", "ctx"), axis=1, tiled=True),
-        lax.all_gather(key_weight, ("shard", "ctx"), axis=0, tiled=True),
-        lax.all_gather(value_weight, ("shard", "ctx"), axis=0, tiled=True),
-        lax.all_gather(output_weight, ("shard", "ctx"), axis=2, tiled=True),
-        lax.all_gather(expert_gain, ("shard", "ctx"), axis=0, tiled=True),
-        lax.all_gather(expert_router, ("shard", "ctx"), axis=0, tiled=True),
+        lax.all_gather(attention_gain, BOTH, axis=0, tiled=True),
+        lax.all_gather(attention_router, BOTH, axis=0, tiled=True),
+        lax.all_gather(query_weight, BOTH, axis=1, tiled=True),
+        lax.all_gather(key_weight, BOTH, axis=0, tiled=True),
+        lax.all_gather(value_weight, BOTH, axis=0, tiled=True),
+        lax.all_gather(output_weight, BOTH, axis=2, tiled=True),
+        lax.all_gather(expert_gain, BOTH, axis=0, tiled=True),
+        lax.all_gather(expert_router, BOTH, axis=0, tiled=True),
     )
     first_unit = (
-        lax.axis_index("shard") * lax.axis_size("ctx") + lax.axis_index("ctx")
+        lax.axis_index(SHARD) * lax.axis_size(CTX) + lax.axis_index(CTX)
     ) * units_here
-    group_first = lax.axis_index("shard") * group_units
+    group_first = lax.axis_index(SHARD) * group_units
     own_units = first_unit + jnp.arange(units_here, dtype=jnp.int32)
     chain = ancestors(parents, own_units)
     valid = chain >= 0
@@ -196,8 +198,8 @@
     )
     values = jnp.dot(normed, value_full, preferred_element_type=jnp.float32).astype(jnp.bfloat16)
     all_keys, all_values = (
-        lax.all_gather(keys, "ctx", axis=0, tiled=True),
-        lax.all_gather(values, "ctx", axis=0, tiled=True),
+        lax.all_gather(keys, CTX, axis=0, tiled=True),
+        lax.all_gather(values, CTX, axis=0, tiled=True),
     )
     path_keys = all_keys.reshape(group_units, segment, local_width)[local_chain].reshape(
         units_here, PATH * segment, local_heads, head_dim
@@ -229,18 +231,18 @@
     out_pairs = out_slots.reshape(experts * capacity, width)[head_slot].reshape(
         count, choose, width
     )
-    attention = lax.psum(jnp.sum(head_gates[:, :, None] * out_pairs, axis=1), "tp")
+    attention = lax.psum(jnp.sum(head_gates[:, :, None] * out_pairs, axis=1), TP)
     hidden_state = residual + attention
-    peak_all = lax.pmax(head_peak, ("shard", "ctx"))
+    peak_all = lax.pmax(head_peak, BOTH)
     gain_second = gain_two.astype(jnp.float32)
     normed_two = normalize(hidden_state, gain_second).astype(jnp.bfloat16)
     expert_gates = gating(normed_two, router_two, expert_routes)
     expert_slot, expert_pair, expert_filled = slot_tables(expert_routes, experts, capacity)
     expert_rows = dispatch(normed_two, expert_pair, expert_filled, choose, experts, capacity)
     gate_full, up_full, down_full = (
-        lax.all_gather(gate_weight, ("shard", "ctx"), axis=1, tiled=True),
-        lax.all_gather(up_weight, ("shard", "ctx"), axis=1, tiled=True),
-        lax.all_gather(down_weight, ("shard", "ctx"), axis=2, tiled=True),
+        lax.all_gather(gate_weight, BOTH, axis=1, tiled=True),
+        lax.all_gather(up_weight, BOTH, axis=1, tiled=True),
+        lax.all_gather(down_weight, BOTH, axis=2, tiled=True),
     )
     gate_pre = jnp.einsum(
         "ecd,edf->ecf", expert_rows, gate_full, preferred_element_type=jnp.float32
@@ -254,7 +256,7 @@
         count, choose, width
     )
     feed = lax.psum(
-        jnp.sum(expert_gates[:, :, None] * down_pairs, axis=1).astype(jnp.bfloat16), "tp"
+        jnp.sum(expert_gates[:, :, None] * down_pairs, axis=1).astype(jnp.bfloat16), TP
     ).astype(jnp.float32)
     output = (hidden_state + feed).astype(jnp.bfloat16)
     upstream = cotangent.astype(jnp.float32)
@@ -298,16 +300,16 @@
             (
                 lax.psum_scatter(
                     gate_term.astype(jnp.bfloat16),
-                    ("shard", "ctx"),
+                    BOTH,
                     scatter_dimension=0,
                     tiled=True,
                 ).astype(jnp.float32),
                 lax.psum_scatter(
-                    up_term.astype(jnp.bfloat16), ("shard", "ctx"), scatter_dimension=0, tiled=True
+                    up_term.astype(jnp.bfloat16), BOTH, scatter_dimension=0, tiled=True
                 ).astype(jnp.float32),
                 lax.psum_scatter(
                     down_term.astype(jnp.bfloat16),
-                    ("shard", "ctx"),
+                    BOTH,
                     scatter_dimension=1,
                     tiled=True,
                 ).astype(jnp.float32),
@@ -316,7 +318,7 @@
     gate_gradient = jnp.stack([item[0] for item in collected])
     up_gradient = jnp.stack([item[1] for item in collected])
     down_gradient = jnp.stack([item[2] for item in collected])
-    normed_two_back, expert_gate_back = lax.psum((normed_two_part, expert_gate_part), "tp")
+    normed_two_back, expert_gate_back = lax.psum((normed_two_part, expert_gate_part), TP)
     expert_logit_back = gating_back(expert_gate_back, expert_gates, expert_routes, experts)
     router_two_term = jnp.einsum(
         "td,te->de", normed_two.astype(jnp.float32), expert_logit_back, precision=HIGH
@@ -388,13 +390,13 @@
     key_mine, value_mine = (
         lax.psum_scatter(
             key_group.reshape(group_units * segment, local_width).astype(jnp.bfloat16),
-            "ctx",
+            CTX,
             scatter_dimension=0,
             tiled=True,
         ).astype(jnp.float32),
         lax.psum_scatter(
             value_group.reshape(group_units * segment, local_width).astype(jnp.bfloat16),
-            "ctx",
+            CTX,
             scatter_dimension=0,
             tiled=True,
         ).astype(jnp.float32),
@@ -435,8 +437,8 @@
         + jnp.einsum("tf,df->td", value_back, value_full, preferred_element_type=jnp.float32)
     )
     normed_back, head_gate_back = (
-        lax.psum(normed_part.astype(jnp.bfloat16), "tp").astype(jnp.float32),
-        lax.psum(head_gate_part.astype(jnp.bfloat16), "tp").astype(jnp.float32),
+        lax.psum(normed_part.astype(jnp.bfloat16), TP).astype(jnp.float32),
+        lax.psum(head_gate_part.astype(jnp.bfloat16), TP).astype(jnp.float32),
     )
     head_logit_back = gating_back(head_gate_back, head_gates, attention_routes, experts)
     router_one_term = jnp.einsum(
@@ -458,28 +460,28 @@
         router_two_gradient,
     ) = (
         lax.psum_scatter(
-            gain_one_term.astype(jnp.bfloat16), ("shard", "ctx"), scatter_dimension=0, tiled=True
+            gain_one_term.astype(jnp.bfloat16), BOTH, scatter_dimension=0, tiled=True
         ).astype(jnp.float32),
         lax.psum_scatter(
-            router_one_term.astype(jnp.bfloat16), ("shard", "ctx"), scatter_dimension=0, tiled=True
+            router_one_term.astype(jnp.bfloat16), BOTH, scatter_dimension=0, tiled=True
         ).astype(jnp.float32),
         lax.psum_scatter(
-            query_term.astype(jnp.bfloat16), ("shard", "ctx"), scatter_dimension=1, tiled=True
+            query_term.astype(jnp.bfloat16), BOTH, scatter_dimension=1, tiled=True
         ).astype(jnp.float32),
         lax.psum_scatter(
-            key_term.astype(jnp.bfloat16), ("shard", "ctx"), scatter_dimension=0, tiled=True
+            key_term.astype(jnp.bfloat16), BOTH, scatter_dimension=0, tiled=True
         ).astype(jnp.float32),
         lax.psum_scatter(
-            value_term.astype(jnp.bfloat16), ("shard", "ctx"), scatter_dimension=0, tiled=True
+            value_term.astype(jnp.bfloat16), BOTH, scatter_dimension=0, tiled=True
         ).astype(jnp.float32),
         lax.psum_scatter(
-            output_term.astype(jnp.bfloat16), ("shard", "ctx"), scatter_dimension=2, tiled=True
+            output_term.astype(jnp.bfloat16), BOTH, scatter_dimension=2, tiled=True
         ).astype(jnp.float32),
         lax.psum_scatter(
-            gain_two_term.astype(jnp.bfloat16), ("shard", "ctx"), scatter_dimension=0, tiled=True
+            gain_two_term.astype(jnp.bfloat16), BOTH, scatter_dimension=0, tiled=True
         ).astype(jnp.float32),
         lax.psum_scatter(
-            router_two_term.astype(jnp.bfloat16), ("shard", "ctx"), scatter_dimension=0, tiled=True
+            router_two_term.astype(jnp.bfloat16), BOTH, scatter_dimension=0, tiled=True
         ).astype(jnp.float32),
     )
     factor = jnp.sqrt(jnp.minimum(1.0, CLIP / peak_all))
@@ -513,8 +515,8 @@
 
 
 def across(value, bits):
-    count = lax.axis_size("tp")
-    return lax.ppermute(value, "tp", [(place, place ^ bits) for place in range(count)])
+    count = lax.axis_size(TP)
+    return lax.ppermute(value, TP, [(place, place ^ bits) for place in range(count)])
 
 
 def f32(value):
@@ -531,91 +533,166 @@
     )
 
 
-def gather_tokens(own):
-    blocks = []
-    for step in range(lax.axis_size("ctx")):
-        first = along(own, "ctx", step)
-        second = across(first, 2)
-        blocks += [first, across(first, 1), second, across(second, 1)]
-    return jnp.concatenate(blocks, axis=0)
-
-
-def scatter_tokens(part):
-    steps = lax.axis_size("ctx")
-    pieces = part.reshape((steps, 2, 2, part.shape[0] // (4 * steps)) + part.shape[1:])
-    total = None
-    for step in range(steps - 1, -1, -1):
-        piece = pieces[step]
-        upper = across(bf16(piece[1, 1]), 1)
-        lower = across(bf16(piece[0, 1]), 1)
-        high = f32(piece[1, 0]) + f32(upper)
-        low = f32(piece[0, 0]) + f32(lower)
-        done = low + f32(across(bf16(high), 2))
-        if step:
-            done = f32(along(bf16(done), "ctx", -step))
-        total = done if total is None else total + done
-    return total
-
-
-def scatter_small(part):
-    steps = lax.axis_size("ctx")
-    half = part[:, :, 0::2] + across(part[:, :, 1::2], 1)
-    done = half[:, :, 0] + across(half[:, :, 1], 2)
-    return [along(done[:, step], "ctx", -step) for step in range(steps)]
+def either(bit, zero, one):
+    return jnp.where(bit == 0, zero, one)
+
+
+def tp_bits():
+    place = lax.axis_index(TP)
+    return place % 2, place // 2
+
+
+def in_columns(own, other, far, both):
+    low, high = tp_bits()
+    first, second = either(low, own, other), either(low, other, own)
+    third, fourth = either(low, far, both), either(low, both, far)
+    return jnp.concatenate(
+        [
+            either(high, first, third),
+            either(high, second, fourth),
+            either(high, third, first),
+            either(high, fourth, second),
+        ],
+        axis=1,
+    )
+
+
+def from_ctx(blocks):
+    return [along(block, CTX, step) for step, block in enumerate(blocks)]
+
+
+def gather_pairs(near):
+    far = [across(block, 2) for block in near]
+
+    def stacked(items):
+        steps, rows = len(items), items[0].shape[0]
+        whole = jnp.zeros((steps * rows, items[0].shape[1]), items[0].dtype)
+        for step, item in enumerate(items):
+            row = ((lax.axis_index(CTX) - step) % steps) * rows
+            whole = lax.dynamic_update_slice(whole, item, (row, 0))
+        return whole
+
+    return stacked(near), stacked(far)
+
+
+def gather_columns(near):
+    own, far = gather_pairs(near)
+    return in_columns(own, across(own, 1), far, across(far, 1))
+
+
+def gather_dense(own):
+    whole = lax.all_gather(own, (TP, CTX), axis=0, tiled=True)
+    tps = lax.axis_size(TP)
+    whole = whole.reshape(tps, whole.shape[0] // tps, own.shape[1])
+    return jnp.concatenate([whole[index] for index in range(tps)], axis=1)
+
+
+def outward_kernel(left_ref, right_ref, out_ref):
+    out_ref[0] = bf16(dot(left_ref[...], right_ref[...], (1, 1)))
+
+
+def by_quarter(left, right):
+    tps = lax.axis_size(TP)
+    count, depth = left.shape
+    size = right.shape[0] // tps
+    return pl.pallas_call(
+        outward_kernel,
+        grid=(tps, count // ROWS),
+        in_specs=[
+            pl.BlockSpec((ROWS, depth), lambda q, i: (i, 0)),
+            pl.BlockSpec((size, depth), lambda q, i: (q, 0)),
+        ],
+        out_specs=pl.BlockSpec((1, ROWS, size), lambda q, i: (q, i, 0)),
+        out_shape=jax.ShapeDtypeStruct((tps, count, size), jnp.bfloat16),
+        compiler_params=pltpu.CompilerParams(vmem_limit_bytes=32 * 1024 * 1024),
+        cost_estimate=pl.CostEstimate(
+            flops=2 * count * depth * right.shape[0],
+            bytes_accessed=2 * (tps * count * depth + right.size + count * right.shape[0]),
+            transcendentals=0,
+        ),
+    )(left, right)
+
+
+def scatter_dense(left, right):
+    part = by_quarter(left, right)
+    part = part.reshape(-1, part.shape[2])
+    return f32(lax.psum_scatter(part, (TP, CTX), scatter_dimension=0, tiled=True))
+
+
+def scatter_columns(part):
+    steps = lax.axis_size(CTX)
+    low, high = tp_bits()
+    size = part.shape[1] // 4
+    quarter = [part[:, index * size : (index + 1) * size] for index in range(4)]
+    sent = jnp.concatenate(
+        [either(low, quarter[1], quarter[0]), either(low, quarter[3], quarter[2])], axis=1
+    )
+    came = across(sent, 1)
+    first = f32(either(low, quarter[0], quarter[1])) + f32(came[:, :size])
+    second = f32(either(low, quarter[2], quarter[3])) + f32(came[:, size:])
+    kept = bf16(either(high, first, second))
+    sent = bf16(either(high, second, first))
+    rows = part.shape[0] // steps
+    result = [None] * steps
+    for step in list(range(1, steps)) + [0]:
+        row = ((lax.axis_index(CTX) - step) % steps) * rows
+        own, other = [lax.dynamic_slice_in_dim(item, row, rows, axis=0) for item in (kept, sent)]
+        done = bf16(f32(own) + f32(across(other, 2)))
+        result[step] = along(done, CTX, -step)
+    return result
+
+
+def tp_sum(part):
+    return part + across(part, 1) + across(part, 2) + across(part, 3)
 
 
 def share_out(own):
-    rows = own.shape[0]
-    second = across(own, 2)
-    blocks = [own, across(own, 1), second, across(second, 1)]
-    place = lax.axis_index("tp")
-    whole = jnp.zeros((rows * 4, own.shape[1]), own.dtype)
-    for bits in range(4):
-        whole = lax.dynamic_update_slice(whole, blocks[bits], ((place ^ bits) * rows, 0))
-    return whole
-
-
-def spread_weight(parts, whole, column):
-    steps, rows = parts.shape[0], parts.shape[1]
-    shards = lax.axis_size("shard")
-    here, side = lax.axis_index("ctx"), lax.axis_index("shard")
-    for step in range(steps):
-        mine = lax.dynamic_index_in_dim(parts, (here + step) % steps, 0, keepdims=False)
-        mine = along(mine, "ctx", step)
-        source = (here - step) % steps
-        for turn in range(shards):
-            block = along(mine, "shard", turn)
-            row = (((side - turn) % shards) * steps + source) * rows
-            whole = lax.dynamic_update_slice(whole, block, (row, column))
-    return whole
-
-
-def return_gradient(term):
-    steps, shards = lax.axis_size("ctx"), lax.axis_size("shard")
-    rows = term.shape[0] // (steps * shards)
-    here, side = lax.axis_index("ctx"), lax.axis_index("shard")
-    result = []
-    for step in range(steps):
-        target = (here + step) % steps
-        total = None
-        for turn in range(shards):
-            row = (((side + turn) % shards) * steps + target) * rows
-            piece = lax.dynamic_slice(term, (row, 0), (rows, term.shape[1]))
-            piece = f32(along(piece, "shard", turn))
-            total = piece if total is None else total + piece
-        result.append(along(bf16(total), "ctx", step))
-    return result
-
-
-def in_order(blocks):
-    steps = len(blocks)
-    here = lax.axis_index("ctx")
-    whole = jnp.zeros((steps,) + blocks[0].shape, jnp.float32)
-    for step in range(steps):
-        whole = lax.dynamic_update_slice(
-            whole, f32(blocks[step])[None], ((here - step) % steps,) + (0,) * blocks[0].ndim
-        )
-    return whole
+    return in_columns(own, across(own, 1), across(own, 2), across(own, 3))
+
+
+def tie(*values):
+    return lax.optimization_barrier(values)
+
+
+def after(value, *others):
+    return lax.optimization_barrier((value, *others))[0]
+
+
+def by_place(blocks):
+    order = (lax.axis_index(CTX) - jnp.arange(len(blocks))) % len(blocks)
+    return jnp.stack(blocks)[order]
+
+
+def exchange(parts):
+    return lax.all_to_all(parts, CTX, 0, 0)
+
+
+def swap(value):
+    return lax.ppermute(value, SHARD, [(0, 1), (1, 0)])
+
+
+def joined(near, far):
+    first = lax.axis_index(SHARD) == 0
+    return jnp.concatenate([jnp.where(first, near, far), jnp.where(first, far, near)], axis=0)
+
+
+def halves(value):
+    half = value.shape[1] // 2
+    side = lax.axis_index(SHARD)
+    return (
+        lax.dynamic_slice_in_dim(value, side * half, half, axis=1),
+        lax.dynamic_slice_in_dim(value, (1 - side) * half, half, axis=1),
+    )
+
+
+def far_gradient(rows, change):
+    return bf16(dot(halves(rows)[1], change, (0, 0)))
+
+
+def near_gradient(rows, change, arrived):
+    total = bf16(dot(halves(rows)[0], change, (0, 0)) + f32(arrived))
+    steps = lax.axis_size(CTX)
+    return total.reshape(steps, total.shape[0] // steps, total.shape[1])
 
 
 def attend_kernel(q_ref, k_ref, v_ref, bias_ref, mixed_ref, norm_ref, peak_ref):
@@ -735,22 +812,21 @@
     return jnp.concatenate([value[..., half:], value[..., :half]], axis=-1)
 
 
-def small_gradient(part):
-    steps, shards = lax.axis_size("ctx"), lax.axis_size("shard")
-    here, side = lax.axis_index("ctx"), lax.axis_index("shard")
-    part = part + across(part, 1) + across(part, 2) + across(part, 3)
-    pieces = part.reshape(part.shape[0], shards, steps, part.shape[1] // (shards * steps))
-    total = None
-    for turn in range(shards):
-        for step in range(steps):
-            piece = lax.dynamic_slice(
-                pieces,
-                (0, (side + turn) % shards, (here + step) % steps, 0),
-                (pieces.shape[0], 1, 1, pieces.shape[3]),
-            )[:, 0, 0]
-            piece = along(along(piece, "shard", turn), "ctx", step)
-            total = piece if total is None else total + piece
-    return total
+def small_gradient(part, extra):
+    steps = lax.axis_size(CTX)
+    here, side = lax.axis_index(CTX), lax.axis_index(SHARD)
+    whole = jnp.concatenate([share_out(part), extra], axis=0)
+    half = whole.shape[1] // 2
+    whole = either(side, whole[:, :half], whole[:, half:]) + swap(
+        either(side, whole[:, half:], whole[:, :half])
+    )
+    pieces = whole.reshape(whole.shape[0], steps, half // steps).transpose(1, 0, 2)
+    return sum(
+        along(
+            lax.dynamic_index_in_dim(pieces, (here + step) % steps, 0, keepdims=False), CTX, step
+        )
+        for step in range(steps)
+    )
 
 
 def on_device_fast(
@@ -774,68 +850,94 @@
     count, width = inputs.shape
     experts, depth_here, local_width = query_weight.shape
     hidden = gate_weight.shape[2]
-    steps, shards, tps = lax.axis_size("ctx"), lax.axis_size("shard"), lax.axis_size("tp")
-    here, side, place = lax.axis_index("ctx"), lax.axis_index("shard"), lax.axis_index("tp")
+    steps, shards, tps = lax.axis_size(CTX), lax.axis_size(SHARD), lax.axis_size(TP)
+    here, side, place = lax.axis_index(CTX), lax.axis_index(SHARD), lax.axis_index(TP)
     heads = local_width // HEAD_DIM
-    rows = count // tps
+    rows, quarter = count // tps, width // tps
     tokens = count * steps
-    capacity = CAP
-
-    own_inputs = lax.dynamic_slice(inputs, (place * rows, 0), (rows, width))
-    all_inputs = gather_tokens(own_inputs)
+    slots = -(-CAP // 64) * 64
+
+    def own_columns(value):
+        return lax.dynamic_slice_in_dim(value, place * quarter, quarter, axis=value.ndim - 1)
+
+    own_inputs = own_columns(inputs)
+    def gather_rows(value):
+        value = lax.dynamic_slice_in_dim(value, place * rows, rows, axis=0)
+        return lax.all_gather(value, (CTX, TP), axis=0, tiled=True)
+
+    all_inputs = gather_rows(inputs)
     small = jnp.concatenate(
         [attention_gain[None], expert_gain[None], attention_router.T, expert_router.T], axis=0
     )
-    relative = [along(small, "ctx", step) for step in range(steps)]
-    relative = jnp.stack(
-        [jnp.stack([along(item, "shard", turn) for item in relative]) for turn in range(shards)]
-    )
-    side_order = (side - jnp.arange(shards)) % shards
-    here_order = (here - jnp.arange(steps)) % steps
-    small_all = relative[side_order][:, here_order]
-    small_all = small_all.transpose(2, 0, 1, 3).reshape(small.shape[0], width)
+    routes = jnp.concatenate([attention_routes.T, expert_routes.T], axis=0)
+    packed = jnp.zeros((small.shape[0] + 2 * TOP, max(count, depth_here)), jnp.bfloat16)
+    packed = lax.dynamic_update_slice(packed, small, (0, 0))
+    packed = lax.dynamic_update_slice(packed, bf16(routes), (small.shape[0], 0))
+    packed_near = [along(packed, CTX, step) for step in range(steps)]
+    packed_all = by_place(packed_near)
+    routes_all = packed_all[:, small.shape[0] :, :count].transpose(1, 0, 2).astype(jnp.int32)
+    head_routes = routes_all[:TOP].reshape(TOP, tokens)
+    own_head_routes, own_expert_routes = routes[:TOP], routes[TOP:]
+    small_near = packed_all[:, : small.shape[0], :depth_here].transpose(1, 0, 2)
+    small_near = small_near.reshape(small.shape[0], steps * depth_here).T
+    small_all = joined(small_near, swap(small_near)).T
     gain_first, gain_second = f32(small_all[0]), f32(small_all[1])
     router_first, router_second = small_all[2 : 2 + experts], small_all[2 + experts :]
-
-    routes = jnp.concatenate([attention_routes.T, expert_routes.T], axis=0)
-    bits_order = place ^ jnp.arange(tps)
-    routes_here = routes.reshape(2 * TOP, tps, rows)[:, bits_order]
-    routes_all = jnp.concatenate(
-        [along(routes_here, "ctx", step).reshape(2 * TOP, count) for step in range(steps)], axis=1
-    )
-    head_routes, expert_routes_all = routes_all[:TOP], routes_all[TOP:]
-    own_head_routes = routes_here[:TOP, 0]
-    own_expert_routes = routes_here[TOP:, 0]
-
-    query_parts = query_weight.reshape(experts, depth_here, heads, HEAD_DIM)
-    query_parts = query_parts.transpose(2, 1, 0, 3).reshape(heads, depth_here, experts * HEAD_DIM)
-    key_parts = key_weight.reshape(depth_here, heads, HEAD_DIM).transpose(1, 0, 2)
-    value_parts = value_weight.reshape(depth_here, heads, HEAD_DIM).transpose(1, 0, 2)
-    project_parts = jnp.concatenate([query_parts, key_parts, value_parts], axis=2)
-    output_parts = output_weight.reshape(experts, heads, HEAD_DIM, depth_here)
-    output_parts = output_parts.transpose(1, 3, 0, 2).reshape(
-        heads, depth_here, experts * HEAD_DIM
-    )
-    down_parts = down_weight.transpose(0, 2, 1)
-    project = spread_weight(
-        project_parts, jnp.zeros((width, project_parts.shape[2]), jnp.bfloat16), 0
-    )
-    outward = spread_weight(
-        output_parts, jnp.zeros((width, output_parts.shape[2]), jnp.bfloat16), 0
-    )
-    gate_up = spread_weight(gate_weight, jnp.zeros((width, 2 * hidden), jnp.bfloat16), 0)
-    gate_up = spread_weight(up_weight, gate_up, hidden)
-    down = spread_weight(down_parts, jnp.zeros((width, hidden), jnp.bfloat16), 0)
-    own_cotangent = lax.dynamic_slice(cotangent, (place * rows, 0), (rows, width))
-    all_cotangent = gather_tokens(own_cotangent)
-
-    number = jnp.arange(tokens, dtype=jnp.int32)
-    block = number // count
-    bits = (number % count) // rows
-    token = ((here - block) % steps) * count + (place ^ bits) * rows + number % rows
+    own_small = f32(own_columns(small_all))
+    own_gain_first, own_gain_second = own_small[0], own_small[1]
+    own_router_first, own_router_second = own_small[2 : 2 + experts], own_small[2 + experts :]
+
+    def rows_of(value):
+        return value.reshape(-1, value.shape[2])
+
+    def project_parts(query, key, value):
+        query = query.reshape(experts, depth_here, heads, HEAD_DIM).transpose(2, 1, 0, 3)
+        key, value = [
+            item.reshape(depth_here, heads, HEAD_DIM).transpose(1, 0, 2) for item in (key, value)
+        ]
+        query = query.reshape(heads, depth_here, experts * HEAD_DIM)
+        return jnp.concatenate([query, key, value], axis=2)
+
+    def output_parts(weight):
+        weight = weight.reshape(experts, heads, HEAD_DIM, depth_here).transpose(1, 3, 0, 2)
+        return weight.reshape(heads, depth_here, experts * HEAD_DIM)
+
+    nears = [exchange(project_parts(query_weight, key_weight, value_weight))]
+    weight, nears[0] = tie(output_weight, nears[0])
+    fars = [swap(nears[0])]
+    nears.append(exchange(output_parts(weight)))
+    weight, nears[1] = tie(gate_weight, nears[1])
+    nears.append(exchange(weight))
+    project = joined(rows_of(nears[0]), rows_of(fars[0]))
+    own_upstream = own_columns(cotangent)
+
+    target = (here + jnp.arange(steps, dtype=jnp.int32)) % steps
+    named = own_expert_routes[None] == target[:, None, None]
+    member = named[:, 0] | named[:, 1]
+    slot = jnp.cumsum(member.astype(jnp.int32), axis=1) - 1
+    onehot = (slot[:, None, :] == jnp.arange(slots, dtype=jnp.int32)[None, :, None]) & member[
+        :, None, :
+    ]
+    onehot_all = onehot.astype(jnp.bfloat16).reshape(steps * slots, count)
+
+    def picked_slots(value):
+        picked = bf16(dot(onehot_all, value, (1, 0)))
+        return from_ctx([picked[step * slots : (step + 1) * slots] for step in range(steps)])
+
+    def from_slots(value):
+        return dot(onehot_all, jnp.concatenate(scatter_columns(value), axis=0), (0, 0))
+
+    chosen = (routes_all[TOP] == here) | (routes_all[TOP + 1] == here)
+    chosen_slot = jnp.cumsum(chosen.astype(jnp.int32), axis=1) - 1
+    chosen_onehot = (
+        chosen_slot[:, None, :] == jnp.arange(slots, dtype=jnp.int32)[None, :, None]
+    ) & chosen[:, None, :]
+
+    token = jnp.arange(tokens, dtype=jnp.int32)
     unit = token // SEG
     group_units = tokens // SEG
     group_first = side * group_units
+    parents, all_inputs = tie(parents, all_inputs)
     chain = ancestors(parents, group_first + jnp.arange(group_units, dtype=jnp.int32))
     valid = chain >= 0
     depth = jnp.sum(valid[:, 1:].astype(jnp.int32), axis=1, dtype=jnp.int32)
@@ -863,6 +965,9 @@
     normed = bf16(normalize(f32(all_inputs), gain_first))
     head_gates = pair_gates(dot(router_first, normed, (1, 1)), head_routes)
     raw = dot(normed, project, (1, 0))
+    nears[1], raw = tie(nears[1], raw)
+    fars.append(swap(nears[1]))
+    outward = joined(rows_of(nears[1]), rows_of(fars[1]))
     chosen_heads = [
         [head_routes[choice][:, None] == expert for expert in range(experts)]
         for choice in range(TOP)
@@ -902,111 +1007,137 @@
     gated_mixed = bf16(
         place_pair([head_gates[choice][:, None] * mixed_pair[choice] for choice in range(TOP)])
     )
-    attention = scatter_tokens(bf16(dot(gated_mixed, outward, (1, 1))))
+    weight, nears[2] = tie(up_weight, nears[2])
+    fars.append(swap(nears[2]))
+    nears.append(exchange(weight))
+    attention, nears[3], fars[2] = tie(scatter_dense(gated_mixed, outward), nears[3], fars[2])
+    fars.append(swap(nears[3]))
+    down_parts = after(down_weight, nears[3]).transpose(0, 2, 1)
+    half = depth_here // 2
+    down_near = [exchange(down_parts[:, :half])]
+    down_far = [swap(down_near[0])]
     hidden_state = f32(own_inputs) + attention
-    own_normed_two = bf16(normalize(hidden_state, gain_second))
-    normed_two = gather_tokens(own_normed_two)
-
-    expert_gates = pair_gates(dot(router_second, normed_two, (1, 1)), expert_routes_all)
-    named = [expert_routes_all[choice] == here for choice in range(TOP)]
-    gate_of = sum(jnp.where(named[choice], expert_gates[choice], 0.0) for choice in range(TOP))
-    member = (named[0] | named[1]).reshape(steps, count)
-    slot = jnp.cumsum(member.astype(jnp.int32), axis=1) - 1
-    onehot = (
-        (slot[:, None, :] == jnp.arange(capacity, dtype=jnp.int32)[None, :, None])
-        & member[:, None, :]
-    )
-    gate_slot = jnp.sum(
-        jnp.where(onehot, gate_of.reshape(steps, 1, count), 0.0), axis=2
-    ).reshape(steps * capacity, 1)
-    onehot = onehot.astype(jnp.bfloat16)
-
-    def to_slots(value):
-        return bf16(
-            jnp.einsum(
-                "bst,btd->bsd",
-                onehot,
-                value.reshape(steps, count, width),
-                preferred_element_type=jnp.float32,
-            )
-        ).reshape(steps * capacity, width)
-
-    def from_slots(value):
-        return bf16(
-            jnp.einsum(
-                "bst,bsd->btd",
-                onehot,
-                value.reshape(steps, capacity, width),
-                preferred_element_type=jnp.float32,
-            )
-        ).reshape(tokens, width)
-
-    slot_rows = to_slots(normed_two)
-    slot_upstream = to_slots(all_cotangent)
-    both = dot(slot_rows, gate_up, (1, 0))
-    gate_pre, up_pre = both[:, :hidden], both[:, hidden:]
+    statistics = tp_sum(
+        jnp.concatenate(
+            [
+                jnp.sum(hidden_state * hidden_state, axis=1)[None],
+                jnp.einsum(
+                    "td,ed->et", hidden_state * own_gain_second, own_router_second, precision=HIGH
+                ),
+            ],
+            axis=0,
+        )
+    )
+    norm_two = lax.rsqrt(statistics[0] / width + EPS)
+    expert_gates = pair_gates(statistics[1:] * norm_two, own_expert_routes)
+    own_normed_two = bf16(hidden_state * norm_two[:, None] * own_gain_second)
+    gate_of = jnp.where(named[:, 0], expert_gates[0], 0.0) + jnp.where(
+        named[:, 1], expert_gates[1], 0.0
+    )
+    gate_sent = jnp.sum(jnp.where(onehot, gate_of[:, None, :], 0.0), axis=2)
+    gate_slot = by_place(from_ctx([gate_sent[step : step + 1] for step in range(steps)]))
+    gate_slot = gate_slot.reshape(steps * slots, 1)
+    row_blocks = picked_slots(own_normed_two)
+    down_near.append(exchange(after(down_parts, *row_blocks)[:, half:]))
+    down_far.append(swap(down_near[1]))
+    slot_rows, down_near[0] = tie(gather_columns(row_blocks), down_near[0])
+    down_near[1], gate_slot = tie(down_near[1], gate_slot)
+    all_cotangent = gather_rows(after(cotangent, *row_blocks))
+    slot_upstream = bf16(
+        jnp.einsum(
+            "bst,btd->bsd",
+            chosen_onehot.astype(jnp.bfloat16),
+            all_cotangent.reshape(steps, count, width),
+            preferred_element_type=jnp.float32,
+        )
+    ).reshape(steps * slots, width)
+
+    def whole(index):
+        return joined(rows_of(nears[index]), rows_of(fars[index]))
+
+    gate, up = whole(2), whole(3)
+    down = joined(
+        rows_of(jnp.concatenate(down_near, axis=1)), rows_of(jnp.concatenate(down_far, axis=1))
+    )
+    gate_pre = dot(slot_rows, gate, (1, 0))
+    up_pre = dot(slot_rows, up, (1, 0))
     act_raw = dot(slot_upstream, down, (1, 0))
     sigmoid = jax.nn.sigmoid(gate_pre)
     activated = gate_pre * sigmoid * up_pre
     gated_act = bf16(activated * gate_slot)
-    gate_back_slot = jnp.sum(activated * act_raw, axis=1)
+    gate_back_slot = jnp.sum(activated * act_raw, axis=1, keepdims=True)
     act_back = act_raw * gate_slot
-    both_back = bf16(
-        jnp.concatenate(
-            [
-                act_back * up_pre * sigmoid * (1.0 + gate_pre * (1.0 - sigmoid)),
-                act_back * gate_pre * sigmoid,
-            ],
-            axis=1,
-        )
-    )
-    rows_back = from_slots(bf16(dot(both_back, gate_up, (1, 1))))
-    gate_change = jnp.sum(
-        jnp.where(onehot > 0, gate_back_slot.reshape(steps, capacity, 1), 0.0), axis=1
-    ).reshape(1, steps, tps, rows)
-    normed_two_back = scatter_tokens(rows_back)
-    gate_changes = scatter_small(gate_change)
-    down_blocks = return_gradient(bf16(dot(slot_upstream, gated_act, (0, 0))))
-    gate_up_term = bf16(dot(slot_rows, both_back, (0, 0)))
-    gate_blocks = return_gradient(gate_up_term[:, :hidden])
-    up_blocks = return_gradient(gate_up_term[:, hidden:])
-    feed = scatter_tokens(from_slots(bf16(dot(gated_act, down, (1, 1)))))
-    output = share_out(bf16(hidden_state + feed))
-
-    own_expert_gates = pair_gates(dot(router_second, own_normed_two, (1, 1)), own_expert_routes)
+    gate_back = bf16(act_back * up_pre * sigmoid * (1.0 + gate_pre * (1.0 - sigmoid)))
+    up_back = bf16(act_back * gate_pre * sigmoid)
+    pairs = [(slot_upstream, gated_act), (slot_rows, gate_back), (slot_rows, up_back)]
+    far_terms = [far_gradient(*pair) for pair in pairs]
+    arrived = [swap(term) for term in far_terms]
+    rows_back = bf16(
+        dot(after(gate_back, *far_terms), gate, (1, 1)) + dot(up_back, up, (1, 1))
+    )
+    fed = bf16(dot(gated_act, down, (1, 1)))
+    gate_sums = tp_sum(after(gate_back_slot, rows_back).reshape(steps, slots))
+    gate_sums = jnp.concatenate(
+        [
+            along(lax.dynamic_slice_in_dim(gate_sums, (here - step) % steps, 1), CTX, -step)
+            for step in range(steps)
+        ]
+    )
+    gate_changes = jnp.sum(jnp.where(onehot, gate_sums[:, :, None], 0.0), axis=1)
+    normed_two_back, ready = tie(
+        from_slots(rows_back), near_gradient(*pairs[0], arrived[0])
+    )
+
     expert_gate_back = [
         sum(
-            jnp.where(own_expert_routes[choice] == (here + step) % steps, gate_changes[step][0], 0.0)
-            for step in range(steps)
+            jnp.where(named[step, choice], gate_changes[step], 0.0) for step in range(steps)
         )
         for choice in range(TOP)
     ]
     expert_logit_back = pair_gates_back(
-        expert_gate_back, own_expert_gates, own_expert_routes, experts
+        expert_gate_back, expert_gates, own_expert_routes, experts
     )
     router_second_term = jnp.einsum(
         "et,td->ed", expert_logit_back, f32(own_normed_two), precision=HIGH
     )
     normed_two_back = normed_two_back + jnp.einsum(
-        "et,ed->td", expert_logit_back, f32(router_second), precision=HIGH
-    )
-    hidden_back, gain_second_term = normalize_back(normed_two_back, hidden_state, gain_second)
-    hidden_back = hidden_back + f32(own_cotangent)
-    second_small = small_gradient(
-        jnp.concatenate([gain_second_term[None], router_second_term], axis=0)
-    )
-
-    all_back = gather_tokens(bf16(hidden_back))
+        "et,ed->td", expert_logit_back, own_router_second, precision=HIGH
+    )
+    scaled = normed_two_back * own_gain_second
+    mean = tp_sum(jnp.sum(scaled * hidden_state, axis=1)[None])[0] / width
+    gain_second_term = jnp.sum(normed_two_back * hidden_state * norm_two[:, None], axis=0)
+    hidden_back = (
+        f32(own_upstream)
+        + norm_two[:, None] * scaled
+        - hidden_state * (norm_two**3 * mean)[:, None]
+    )
+
+    down_back = exchange(ready)
+    all_back, gate_ready = tie(
+        gather_dense(bf16(hidden_back)),
+        near_gradient(slot_rows, after(gate_back, hidden_back), arrived[1]),
+    )
     raw_back = dot(all_back, outward, (1, 0))
     pair_back = [pick(raw_back, choice) for choice in range(TOP)]
     head_change = jnp.stack(
         [jnp.sum(mixed_pair[choice] * pair_back[choice], axis=1) for choice in range(TOP)]
     )
+    head_sums = tp_sum(head_change).reshape(TOP, steps, count).transpose(1, 0, 2)
+    head_gate_back = sum(
+        along(
+            lax.dynamic_index_in_dim(head_sums, (here - step) % steps, 0, keepdims=False),
+            CTX,
+            -step,
+        )
+        for step in range(steps)
+    )
     mixed_back = bf16(
         jnp.concatenate(
             [head_gates[choice][:, None] * pair_back[choice] for choice in range(TOP)], axis=0
         )
     )
+    mixed_back, down_back = tie(mixed_back, down_back)
+    gate_returned = [exchange(after(gate_ready, down_back)[:, :half])]
     query_change, key_change, value_change = attend_back(
         queries, keys, values, bias, norm, mixed_back
     )
@@ -1022,13 +1153,38 @@
             axis=1,
         )
     )
-    normed_back = scatter_tokens(bf16(dot(change, project, (1, 1))))
-    head_changes = scatter_small(head_change.reshape(TOP, steps, tps, rows))
-    output_blocks = return_gradient(bf16(dot(all_back, gated_mixed, (0, 0))))
-    project_blocks = return_gradient(bf16(dot(normed, change, (0, 0))))
-    own_normed = bf16(normalize(f32(own_inputs), gain_first))
-    own_head_gates = pair_gates(dot(router_first, own_normed, (1, 1)), own_head_routes)
-    head_gate_back = sum(head_changes)
+    change, head_gate_back, arrived[2], gate_returned[0] = tie(
+        change, head_gate_back, arrived[2], gate_returned[0]
+    )
+    feed = from_slots(after(fed, change))
+    gate_returned.append(exchange(after(gate_ready, gate_returned[0])[:, half:]))
+    up_ready = near_gradient(slot_rows, after(up_back, change), arrived[2])
+    pairs += [(all_back, gated_mixed), (normed, change)]
+    arrived += [swap(far_gradient(*pair)) for pair in pairs[3:]]
+    up_returned = exchange(after(up_ready, gate_returned[1]))
+    normed_back, feed, output_ready, project_ready, gate_returned[1], up_returned = tie(
+        scatter_dense(change, project),
+        feed,
+        near_gradient(*pairs[3], arrived[3]),
+        near_gradient(*pairs[4], arrived[4]),
+        gate_returned[1],
+        up_returned,
+    )
+    output = share_out(bf16(hidden_state + feed))
+    output_all = exchange(output_ready)
+    project_all = exchange(after(project_ready, output_all))
+    output_all, project_all = f32(output_all), f32(project_all)
+    down_gradient = f32(down_back.transpose(0, 2, 1))
+    gate_gradient = f32(jnp.concatenate(gate_returned, axis=1))
+    up_gradient = f32(up_returned)
+    own_rows = f32(inputs)
+    norm_one = lax.rsqrt(jnp.mean(own_rows * own_rows, axis=1) + EPS)
+    own_values = f32(own_inputs)
+    own_normed = bf16(own_values * norm_one[:, None] * own_gain_first)
+    own_head_gates = [
+        lax.dynamic_slice_in_dim(gate_item, here * count, count, axis=0)
+        for gate_item in head_gates
+    ]
     head_logit_back = pair_gates_back(
         [head_gate_back[choice] for choice in range(TOP)],
         own_head_gates,
@@ -1039,18 +1195,33 @@
         "et,td->ed", head_logit_back, f32(own_normed), precision=HIGH
     )
     normed_back = normed_back + jnp.einsum(
-        "et,ed->td", head_logit_back, f32(router_first), precision=HIGH
-    )
-    input_back, gain_first_term = normalize_back(normed_back, f32(own_inputs), gain_first)
-    input_gradient = share_out(bf16(input_back + hidden_back))
-    first_small = small_gradient(
-        jnp.concatenate([gain_first_term[None], router_first_term], axis=0)
-    )
-
-    gate_gradient = in_order(gate_blocks)
-    up_gradient = in_order(up_blocks)
-    down_gradient = in_order([item.T for item in down_blocks])
-    project_all = in_order(project_blocks)
+        "et,ed->td", head_logit_back, own_router_first, precision=HIGH
+    )
+    scaled = normed_back * own_gain_first
+    mean = tp_sum(jnp.sum(scaled * own_values, axis=1)[None])[0] / width
+    gain_first_term = jnp.sum(normed_back * own_values * norm_one[:, None], axis=0)
+    input_gradient = share_out(
+        bf16(
+            hidden_back
+            + norm_one[:, None] * scaled
+            - own_values * (norm_one**3 * mean)[:, None]
+        )
+    )
+    small_sums = small_gradient(
+        jnp.concatenate(
+            [
+                gain_first_term[None],
+                gain_second_term[None],
+                router_first_term,
+                router_second_term,
+            ],
+            axis=0,
+        ),
+        jnp.where(
+            jnp.arange(width)[None] % depth_here == side * steps + here, jnp.max(peaks), 0.0
+        ),
+    )
+
     query_gradient = (
         project_all[:, :, :inner]
         .reshape(heads, depth_here, experts, HEAD_DIM)
@@ -1064,30 +1235,29 @@
         project_all[:, :, inner + HEAD_DIM :].transpose(1, 0, 2).reshape(depth_here, local_width)
     )
     output_gradient = (
-        in_order(output_blocks)
+        f32(output_all)
         .reshape(heads, depth_here, experts, HEAD_DIM)
         .transpose(2, 0, 3, 1)
         .reshape(experts, local_width, depth_here)
     )
 
-    peak = jnp.max(peaks, axis=0, keepdims=True)
-    for turn_by in range(1, shards):
-        peak = jnp.maximum(peak, along(peak, "shard", turn_by))
-    head_peaks = in_order([along(peak, "ctx", step) for step in range(steps)])
-    factor = jnp.sqrt(jnp.minimum(1.0, CLIP / head_peaks)).reshape(local_width)
+    head_peaks = jnp.max(
+        small_sums[-1, : shards * steps].reshape(shards, steps), axis=0
+    )
+    factor = jnp.repeat(jnp.sqrt(jnp.minimum(1.0, CLIP / head_peaks)), HEAD_DIM)
     clipped_query = bf16(f32(query_weight) * factor)
     clipped_key = bf16(f32(key_weight) * factor)
     return (
         output,
         input_gradient,
-        first_small[0],
-        first_small[1:].T,
+        small_sums[0],
+        small_sums[2 : 2 + experts].T,
         query_gradient,
         key_gradient,
         value_gradient,
         output_gradient,
-        second_small[0],
-        second_small[1:].T,
+        small_sums[1],
+        small_sums[2 + experts : 2 + 2 * experts].T,
         gate_gradient,
         up_gradient,
         down_gradient,
@@ -1098,12 +1268,13 @@
 
 def on_device(*arrays):
     experts, _, local_width = arrays[6].shape
-    steps = lax.axis_size("ctx")
+    steps = lax.axis_size(CTX)
     tokens = arrays[0].shape[0] * steps
     fits = (
         experts == steps
         and local_width == steps * HEAD_DIM
-        and lax.axis_size("tp") == 4
+        and lax.axis_size(TP) == 4
+        and lax.axis_size(SHARD) == 2
         and tokens % ROWS == 0
     )
     return on_device_fast(*arrays) if fits else on_device_general(*arrays)
@@ -1111,43 +1282,43 @@
 
 def solution(mesh):
     placed = (
-        P(("shard", "ctx"), None),
+        P(BOTH, None),
         P(),
-        P(("shard", "ctx"), None),
-        P(("shard", "ctx"), None),
-        P(("shard", "ctx")),
-        P(("shard", "ctx"), None),
-        P(None, ("shard", "ctx"), "tp"),
-        P(("shard", "ctx"), "tp"),
-        P(("shard", "ctx"), "tp"),
-        P(None, "tp", ("shard", "ctx")),
-        P(("shard", "ctx")),
-        P(("shard", "ctx"), None),
-        P(None, ("shard", "ctx"), "tp"),
-        P(None, ("shard", "ctx"), "tp"),
-        P(None, "tp", ("shard", "ctx")),
-        P(("shard", "ctx"), None),
+        P(BOTH, None),
+        P(BOTH, None),
+        P(BOTH),
+        P(BOTH, None),
+        P(None, BOTH, TP),
+        P(BOTH, TP),
+        P(BOTH, TP),
+        P(None, TP, BOTH),
+        P(BOTH),
+        P(BOTH, None),
+        P(None, BOTH, TP),
+        P(None, BOTH, TP),
+        P(None, TP, BOTH),
+        P(BOTH, None),
     )
     return jax.shard_map(
         on_device,
         mesh=mesh,
         in_specs=placed,
         out_specs=(
-            P(("shard", "ctx"), None),
-            P(("shard", "ctx"), None),
-            P(("shard", "ctx")),
-            P(("shard", "ctx"), None),
-            P(None, ("shard", "ctx"), "tp"),
-            P(("shard", "ctx"), "tp"),
-            P(("shard", "ctx"), "tp"),
-            P(None, "tp", ("shard", "ctx")),
-            P(("shard", "ctx")),
-            P(("shard", "ctx"), None),
-            P(None, ("shard", "ctx"), "tp"),
-            P(None, ("shard", "ctx"), "tp"),
-            P(None, "tp", ("shard", "ctx")),
-            P(None, ("shard", "ctx"), "tp"),
-            P(("shard", "ctx"), "tp"),
+            P(BOTH, None),
+            P(BOTH, None),
+            P(BOTH),
+            P(BOTH, None),
+            P(None, BOTH, TP),
+            P(BOTH, TP),
+            P(BOTH, TP),
+            P(None, TP, BOTH),
+            P(BOTH),
+            P(BOTH, None),
+            P(None, BOTH, TP),
+            P(None, BOTH, TP),
+            P(None, TP, BOTH),
+            P(None, BOTH, TP),
+            P(BOTH, TP),
         ),
         check_vma=False,
     )

time: 1510 us -> 1020 us (0.68)
  waiting for transfers between devices: 743 us -> 483 us
  starting transfers between devices: 332 us -> 149 us
  local copies, waits for them, and re-layouts: 199 us -> 99.4 us
  other arithmetic: 73.2 us -> 101 us
    ppermute x134 -> x24, waiting for transfers between devices: 589 us -> 139 us  [along(): lax.ppermute(value, axis, [(place, (place + step) % count) for place in r...]
    ppermute x134 -> x24, starting transfers between devices: 286 us -> 39.8 us  [along(): lax.ppermute(value, axis, [(place, (place + step) % count) for place in r...]
    reduce_scatter x0 -> x2, waiting for transfers between devices: none -> 97.2 us  [scatter_dense(): lax.psum_scatter(part, (TP, CTX), scatter_dimension=0, tiled=True)]
    all_to_all x0 -> x12, waiting for transfers between devices: none -> 67.2 us  [exchange(): return lax.all_to_all(parts, CTX, 0, 0)]
    all_to_all x0 -> x12, starting transfers between devices: none -> 64.5 us  [exchange(): return lax.all_to_all(parts, CTX, 0, 0)]
    dynamic_update_slice x53 -> x8, local copies, waits for them, and re-layouts: 52.1 us -> 4.85 us  [the longest x7 4.72 us: stacked(): whole = lax.dynamic_update_slice(whole, item, (row, 0))]
    unnamed x428 -> x220, local copies, waits for them, and re-layouts: 53.2 us -> 25.8 us
    all_gather x0 -> x3, waiting for transfers between devices: none -> 24.4 us  [the longest x1 24.4 us: gather_dense(): whole = lax.all_gather(own, (TP, CTX), axis=0, tiled=True)]
  transfers between devices with their start and end apart: 246 -> 94, of which waited for: 95 -> 46; matrix products, arithmetic and copies ran while one was open for 18% -> 24% of each run, Pallas kernels for 1% -> 3%
where the time goes in v2:
time: 1020 us; the launch traced here: 1010 us
  waiting for transfers between devices  483 us (47%)
  starting transfers between devices  149 us (15%)
  matrix products  120 us (12%)
  other arithmetic  101 us (10%)
  local copies, waits for them, and re-layouts  99.4 us (10%)
  Pallas kernels  41.5 us (4%)
  between operations  16.2 us (2%)
    ppermute x24, waiting for transfers between devices, along(): lax.ppermute(value, axis, [(place, (place + step) % count) for place in r...  139 us
    dot_general x23, matrix products, dot(): lax.dot_general(left, right, ((contract[:1], contract[1:]), ((), ())), pr...  111 us
    ppermute x13, waiting for transfers between devices, swap(): return lax.ppermute(value, SHARD, [(0, 1), (1, 0)])  107 us
    reduce_scatter x2, waiting for transfers between devices, scatter_dense(): lax.psum_scatter(part, (TP, CTX), scatter_dimension=0, tiled=True)  97.2 us
    all_to_all x12, waiting for transfers between devices, exchange(): return lax.all_to_all(parts, CTX, 0, 0)  67.2 us
    all_to_all x12, starting transfers between devices, exchange(): return lax.all_to_all(parts, CTX, 0, 0)  64.5 us
    ppermute x40, waiting for transfers between devices, across(): lax.ppermute(value, TP, [(place, place ^ bits) for place in range(count)])  47.6 us
    ppermute x24, starting transfers between devices, along(): lax.ppermute(value, axis, [(place, (place + step) % count) for place in r...  39.8 us
  transfers between devices with their start and end apart: 94, of which 46 were waited for; matrix products, arithmetic and copies ran while one was open for 24% of the time, Pallas kernels for 3%

profile of v2, /device:TPU:0, one launch (start us, length us, event | category | flops | bytes accessed | tf_op | source)
XLA Modules:
  0.0 1010.1 jit_solution(8107174432550740359)
XLA Ops:
  25.3 30.6 %collective-permute-done.2 = bf16[14,320]{1,0:T(8,128)(2,1)S(1)} collective-permute-done((bf16[14,320]{1,0:T(8,128)(2,1)S(1)}, bf16[14,320]{1,0:T(8,128)(2,1)S(1)}, u32[]{:S(2)}, u32[]{:S(2)}) %collective-permute-start.2) | collective-permute-done | bytes 8992 | tf_op jit(solution)/shard_map/ppermute | solution.py:514
  56.0 14.1 %collective-permute-done.1 = bf16[14,320]{1,0:T(8,128)(2,1)S(1)} collective-permute-done((bf16[14,320]{1,0:T(8,128)(2,1)S(1)}, bf16[14,320]{1,0:T(8,128)(2,1)S(1)}, u32[]{:S(2)}, u32[]{:S(2)}) %collective-permute-start.1) | collective-permute-done | bytes 8992 | tf_op jit(solution)/shard_map/ppermute | solution.py:514
  81.0 30.9 %collective-permute-done.3 = bf16[1024,10]{0,1:T(8,128)(2,1)S(1)} collective-permute-done((bf16[1024,10]{0,1:T(8,128)(2,1)S(1)}, bf16[1024,10]{0,1:T(8,128)(2,1)S(1)}, u32[]{:S(2)}, u32[]{:S(2)}) %collective-permute-start.3) | collective-permute-done | bytes 20512 | tf_op jit(solution)/shard_map/ppermute | solution.py:671
  156.4 11.7 %shard_map.271 = (bf16[2560,128]{1,0:T(8,128)(2,1)S(1)}, f32[2560,128]{1,0:T(8,128)S(1)}, f32[80,128]{1,0:T(8,128)S(1)}) custom-call(bf16[2560,128]{1,0:T(8,128)(2,1)S(1)} %pad_maximum_fusion.25.q_ref, bf16[1280,128]{1,0:T(8,128)(2,1)S(1)} %get-tuple-element.163.k_ref, bf16[1280,128]{1,0:T(8,128)(2,1)S(1)} %slice.866.v_ref, ...), custom_call_target="tpu_custom_call" | custom-call | flops 1677721600 | bytes 9175040 | tf_op jit(solution)/shard_map/pallas_call | solution.py:739
  191.5 97.2 %reduce-scatter.3.cloned.1.call-done = bf16[320,512]{1,0:T(8,128)(2,1)} async-done(((bf16[5120,512]{1,0:T(8,128)(2,1)}), bf16[320,512]{1,0:T(8,128)(2,1)}) %reduce-scatter.3.cloned.1.call-update) | async-done | bytes 327696 | tf_op jit(solution)/shard_map/reduce_scatter | solution.py:619
  306.9 12.3 %collective-permute-done.11 = bf16[192,512]{1,0:T(8,128)(2,1)S(1)} collective-permute-done((bf16[192,512]{1,0:T(8,128)(2,1)S(1)}, bf16[192,512]{1,0:T(8,128)(2,1)S(1)}, u32[]{:S(2)}, u32[]{:S(2)}) %collective-permute-start.11) | collective-permute-done | bytes 196640 | tf_op jit(solution)/shard_map/ppermute | solution.py:514
  355.5 14.4 %collective-permute-done.21 = f32[1,192]{1,0:T(1,128)S(1)} collective-permute-done((f32[1,192]{1,0:T(1,128)S(1)}, f32[1,192]{1,0:T(1,128)S(1)}, u32[]{:S(2)}, u32[]{:S(2)}) %collective-permute-start.21) | collective-permute-done | bytes 800 | tf_op jit(solution)/shard_map/ppermute | solution.py:514
  374.7 18.0 %collective-permute-done.20 = f32[1,192]{1,0:T(1,128)S(1)} collective-permute-done((f32[1,192]{1,0:T(1,128)S(1)}, f32[1,192]{1,0:T(1,128)S(1)}, u32[]{:S(2)}, u32[]{:S(2)}) %collective-permute-start.20) | collective-permute-done | bytes 800 | tf_op jit(solution)/shard_map/ppermute | solution.py:514
  415.7 21.9 %all-to-all-done.5 = bf16[4,128,1408]{2,1,0:T(8,128)(2,1)} async-done(((bf16[4,128,1408]{2,1,0:T(8,128)(2,1)}), bf16[4,128,1408]{2,1,0:T(8,128)(2,1)}, u32[]{:S(2)}, u32[]{:S(2)}) %all-to-all-start.5) | async-done | bytes 1441824 | tf_op jit(solution)/shard_map/all_to_all | solution.py:667
  453.2 17.6 %collective-permute-done.23 = bf16[4,128,1408]{2,1,0:T(8,128)(2,1)S(1)} collective-permute-done((bf16[4,128,1408]{2,1,0:T(8,128)(2,1)}, bf16[4,128,1408]{2,1,0:T(8,128)(2,1)S(1)}, u32[]{:S(2)}, u32[]{:S(2)}) %collective-permute-start.23) | collective-permute-done | bytes 1441824 | tf_op jit(solution)/shard_map/ppermute | solution.py:671
  478.5 11.9 %multiply_reduce_fusion = (f32[768]{0:T(1024)S(1)}, bf16[768,1408]{1,0:T(8,128)(2,1)S(1)}, bf16[768,1408]{1,0:T(8,128)(2,1)S(1)}, bf16[768,1408]{1,0:T(8,128)(2,1)S(1)}) fusion(f32[768,1408]{1,0:T(8,128)} %fusion.8, f32[768,1408]{1,0:T(8,128)} %fusion.6, f32[768]{0:T(1024)S(1)} %reduce.17, bf16[768,2048]{1,0:T(8,128)(2,1)S(1)} %bitcast.314, ...), kind=kOutput, calls=%fused_computation.30 | convolution fusion | flops 4462345216 | bytes 24057856 | tf_op jit(solution)/shard_map/dot_general | solution.py:531
  503.8 8.4 fusion.5
  512.3 8.8 add_convert_fusion
  600.2 50.6 %collective-permute-done.43 = bf16[1024,1408]{1,0:T(8,128)(2,1)} collective-permute-done((bf16[1024,1408]{1,0:T(8,128)(2,1)}, bf16[1024,1408]{1,0:T(8,128)(2,1)}, u32[]{:S(2)}, u32[]{:S(2)}) %collective-permute-start.43) | collective-permute-done | bytes 2883616 | tf_op jit(solution)/shard_map/ppermute | solution.py:671
  650.8 7.2 add_convert_fusion.2
  658.0 24.4 %all-gather.8.cloned.1.call-done = bf16[5120,512]{1,0:T(8,128)(2,1)} async-done(((bf16[320,512]{1,0:T(8,128)(2,1)}), bf16[5120,512]{1,0:T(8,128)(2,1)}) %all-gather.8.cloned.1.call-update) | async-done | bytes 5242896 | tf_op jit(solution)/shard_map/all_gather | solution.py:584
  698.2 8.5 all-to-all-start.7
  712.1 14.6 %shard_map.273 = (f32[2560,128]{1,0:T(8,128)S(1)}, f32[1280,128]{1,0:T(8,128)S(1)}, f32[1280,128]{1,0:T(8,128)S(1)}) custom-call(bf16[2560,128]{1,0:T(8,128)(2,1)S(1)} %copy-done.7, bf16[1280,128]{1,0:T(8,128)(2,1)S(1)} %copy-done.11, bf16[1280,128]{1,0:T(8,128)(2,1)S(1)} %copy-done.13, bf16[1280,1280]{1,0:T(8,128)(2,1)} %select_convert_fusion.bias_ref, ...), custom_call_target="tpu_custom_call" | custom-call | flops 4194304000 | bytes 10485760 | tf_op jit(solution)/shard_map/pallas_call | solution.py:764
  745.6 8.3 shard_map.274
  763.1 10.7 %fusion.11 = bf16[768,2048]{1,0:T(8,128)(2,1)} fusion(bf16[768,1408]{1,0:T(8,128)(2,1)} %copy-done.96, bf16[1024,1408]{1,0:T(8,128)(2,1)} %bitcast.322, bf16[1024,1408]{1,0:T(8,128)(2,1)} %bitcast.320), kind=kOutput, calls=%fused_computation.45 | convolution fusion | flops 4442292224 | bytes 11075584 | tf_op jit(solution)/shard_map/dot_general | solution.py:531
  786.5 26.9 %all-to-all-done.8 = bf16[4,128,1408]{2,1,0:T(8,128)(2,1)S(1)} async-done(((bf16[4,128,1408]{2,1,0:T(8,128)(2,1)}), bf16[4,128,1408]{2,1,0:T(8,128)(2,1)S(1)}, u32[]{:S(2)}, u32[]{:S(2)}) %all-to-all-start.8) | async-done | bytes 1441824 | tf_op jit(solution)/shard_map/all_to_all | solution.py:667
  871.3 11.0 %collective-permute-done.58 = bf16[192,512]{1,0:T(8,128)(2,1)S(1)} collective-permute-done((bf16[192,512]{1,0:T(8,128)(2,1)S(1)}, bf16[192,512]{1,0:T(8,128)(2,1)S(1)}, u32[]{:S(2)}, u32[]{:S(2)}) %collective-permute-start.58) | collective-permute-done | bytes 196640 | tf_op jit(solution)/shard_map/ppermute | solution.py:514
  882.4 19.8 %collective-permute-done.56 = bf16[192,512]{1,0:T(8,128)(2,1)S(1)} collective-permute-done((bf16[192,512]{1,0:T(8,128)(2,1)S(1)}, bf16[192,512]{1,0:T(8,128)(2,1)S(1)}, u32[]{:S(2)}, u32[]{:S(2)}) %collective-permute-start.56) | collective-permute-done | bytes 196640 | tf_op jit(solution)/shard_map/ppermute | solution.py:514
  971.2 18.3 %all-to-all-done.11 = bf16[4,256,768]{2,1,0:T(8,128)(2,1)S(1)} async-done(((bf16[4,256,768]{2,1,0:T(8,128)(2,1)}), bf16[4,256,768]{2,1,0:T(8,128)(2,1)S(1)}, u32[]{:S(2)}, u32[]{:S(2)}) %all-to-all-start.11) | async-done | bytes 1572896 | tf_op jit(solution)/shard_map/all_to_all | solution.py:667
  (677 shorter events, 495.9 us)
Async XLA Ops:
  7.2 112.8 %all-gather.4.cloned.1.call-start = ((), (), s32[]{:S(2)}) async-start(), calls=%async_computation.14 | async-start | bytes 5570560 | tf_op jit(solution)/shard_map/all_gather | solution.py:866
  13.2 57.5 %all-to-all-start = ((bf16[4,256,768]{2,1,0:T(8,128)(2,1)}), bf16[4,256,768]{2,1,0:T(8,128)(2,1)S(1)}, u32[]{:S(2)}, u32[]{:S(2)}) async-start(bf16[4,256,768]{2,1,0:T(8,128)(2,1)} %pad_maximum_fusion.17), calls=%async_computation | async-start | bytes 3145728 | tf_op jit(solution)/shard_map/all_to_all | solution.py:667
  23.6 46.4 %collective-permute-start.1 = (bf16[14,320]{1,0:T(8,128)(2,1)S(1)}, bf16[14,320]{1,0:T(8,128)(2,1)S(1)}, u32[]{:S(2)}, u32[]{:S(2)}) collective-permute-start(bf16[14,320]{1,0:T(8,128)(2,1)S(1)} %dynamic_update_slice.31), channel_id=1, source_target_pairs={{0,8},{4,12},{8,0},{12,4},{1,9},{5,13},{9,1},{13,5},{2,10},{6,14},... | collective-permute-start | bytes 26888 | tf_op jit(solution)/shard_map/ppermute | solution.py:514
  23.6 46.4 %collective-permute-start = (bf16[14,320]{1,0:T(8,128)(2,1)S(1)}, bf16[14,320]{1,0:T(8,128)(2,1)S(1)}, u32[]{:S(2)}, u32[]{:S(2)}) collective-permute-start(bf16[14,320]{1,0:T(8,128)(2,1)S(1)} %dynamic_update_slice.31), channel_id=1, source_target_pairs={{0,4},{4,8},{8,12},{12,0},{1,5},{5,9},{9,13},{13,1},{2,6},{6,10},{... | collective-permute-start | bytes 26888 | tf_op jit(solution)/shard_map/ppermute | solution.py:514
  112.0 71.4 %all-to-all-start.2 = ((bf16[4,256,1408]{2,1,0:T(8,128)(2,1)}), bf16[4,256,1408]{2,1,0:T(8,128)(2,1)}, u32[]{:S(2)}, u32[]{:S(2)}) async-start(bf16[4,256,1408]{2,1,0:T(8,128)(2,1)} %param.28), calls=%async_computation.3 | async-start | bytes 5767168 | tf_op jit(solution)/shard_map/all_to_all | solution.py:667
  116.7 172.1 %reduce-scatter.3.cloned.1.call-start = ((), (), s32[]{:S(2)}) async-start(), calls=%async_computation.15 | async-start | bytes 5570560 | tf_op jit(solution)/shard_map/reduce_scatter | solution.py:619
  183.4 108.8 %all-to-all-start.3 = ((bf16[4,256,1408]{2,1,0:T(8,128)(2,1)}), bf16[4,256,1408]{2,1,0:T(8,128)(2,1)}, u32[]{:S(2)}, u32[]{:S(2)}) async-start(bf16[4,256,1408]{2,1,0:T(8,128)(2,1)} %param.29), calls=%async_computation.4 | async-start | bytes 5767168 | tf_op jit(solution)/shard_map/all_to_all | solution.py:667
  188.5 285.5 %all-gather.6.cloned.1.call-start = ((), (), s32[]{:S(2)}) async-start(), calls=%async_computation.16 | async-start | bytes 5570560 | tf_op jit(solution)/shard_map/all_gather | solution.py:866
  188.5 102.1 %collective-permute-start.6 = (bf16[4,256,1408]{2,1,0:T(8,128)(2,1)}, bf16[4,256,1408]{2,1,0:T(8,128)(2,1)S(1)}, u32[]{:S(2)}, u32[]{:S(2)}) collective-permute-start(bf16[4,256,1408]{2,1,0:T(8,128)(2,1)} %all-to-all-done.2), channel_id=1, source_target_pairs={{0,16},{16,0},{1,17},{17,1},{2,18},{18,2},{3,19},{19,3},{4,20},{20... | collective-permute-start | bytes 8650760 | tf_op jit(solution)/shard_map/ppermute | solution.py:671
  322.8 118.6 %collective-permute-start.24 = (bf16[4,256,1408]{2,1,0:T(8,128)(2,1)}, bf16[4,256,1408]{2,1,0:T(8,128)(2,1)}, u32[]{:S(2)}, u32[]{:S(2)}) collective-permute-start(bf16[4,256,1408]{2,1,0:T(8,128)(2,1)} %all-to-all-done.3), channel_id=1, source_target_pairs={{0,16},{16,0},{1,17},{17,1},{2,18},{18,2},{3,19},{19,3},{4,20},{20... | collective-permute-start | bytes 8650760 | tf_op jit(solution)/shard_map/ppermute | solution.py:671
  331.6 64.6 %all-to-all-start.4 = ((bf16[4,128,1408]{2,1,0:T(8,128)(2,1)}), bf16[4,128,1408]{2,1,0:T(8,128)(2,1)S(1)}, u32[]{:S(2)}, u32[]{:S(2)}) async-start(bf16[4,128,1408]{2,1,0:T(8,128)(2,1)} %slice.579), calls=%async_computation.5 | async-start | bytes 2883584 | tf_op jit(solution)/shard_map/all_to_all | solution.py:667
  341.0 51.7 %collective-permute-start.20 = (f32[1,192]{1,0:T(1,128)S(1)}, f32[1,192]{1,0:T(1,128)S(1)}, u32[]{:S(2)}, u32[]{:S(2)}) collective-permute-start(f32[1,192]{1,0:T(1,128)S(1)} %get-tuple-element.301), channel_id=1, source_target_pairs={{0,8},{4,12},{8,0},{12,4},{1,9},{5,13},{9,1},{13,5},{2,10},{6,14},... | collective-permute-start | bytes 2312 | tf_op jit(solution)/shard_map/ppermute | solution.py:514
  354.8 47.8 %collective-permute-start.13 = (bf16[768,512]{1,0:T(8,128)(2,1)S(1)}, bf16[768,512]{1,0:T(8,128)(2,1)}, u32[]{:S(2)}, u32[]{:S(2)}) collective-permute-start(bf16[768,512]{1,0:T(8,128)(2,1)S(1)} %constant_dynamic-update-slice_fusion.8), channel_id=1, source_target_pairs={{0,1},{1,0},{2,3},{3,2},{4,5},{5,4},{6,7},{7,6},{8,9},{9,8},{10,11... | collective-permute-start | bytes 2359304 | tf_op jit(solution)/shard_map/ppermute | solution.py:519
  402.7 279.7 %all-gather.8.cloned.1.call-start = ((), (), s32[]{:S(2)}) async-start(), calls=%async_computation.17 | async-start | bytes 5570560 | tf_op jit(solution)/shard_map/all_gather | solution.py:584
  502.6 69.4 %collective-permute-start.33 = (bf16[1024,1408]{1,0:T(8,128)(2,1)}, bf16[1024,1408]{1,0:T(8,128)(2,1)}, u32[]{:S(2)}, u32[]{:S(2)}) collective-permute-start(bf16[1024,1408]{1,0:T(8,128)(2,1)} %convolution_convert_fusion.2), channel_id=1, source_target_pairs={{0,16},{16,0},{1,17},{17,1},{2,18},{18,2},{3,19},{19,3},{4,20},{20... | collective-permute-start | bytes 8650760 | tf_op jit(solution)/shard_map/ppermute | solution.py:671
  585.0 65.8 %collective-permute-start.43 = (bf16[1024,1408]{1,0:T(8,128)(2,1)}, bf16[1024,1408]{1,0:T(8,128)(2,1)}, u32[]{:S(2)}, u32[]{:S(2)}) collective-permute-start(bf16[1024,1408]{1,0:T(8,128)(2,1)} %convolution_convert_fusion.1), channel_id=1, source_target_pairs={{0,16},{16,0},{1,17},{17,1},{2,18},{18,2},{3,19},{19,3},{4,20},{20... | collective-permute-start | bytes 8650760 | tf_op jit(solution)/shard_map/ppermute | solution.py:671
  587.9 156.1 %collective-permute-start.50 = (bf16[1024,1408]{1,0:T(8,128)(2,1)}, bf16[1024,1408]{1,0:T(8,128)(2,1)}, u32[]{:S(2)}, u32[]{:S(2)}) collective-permute-start(bf16[1024,1408]{1,0:T(8,128)(2,1)} %convolution_convert_fusion), channel_id=1, source_target_pairs={{0,16},{16,0},{1,17},{17,1},{2,18},{18,2},{3,19},{19,3},{4,20},{20... | collective-permute-start | bytes 8650760 | tf_op jit(solution)/shard_map/ppermute | solution.py:671
  594.2 101.4 %all-to-all-start.6 = ((bf16[4,256,1408]{1,2,0:T(8,128)(2,1)}), bf16[4,256,1408]{1,2,0:T(8,128)(2,1)}, u32[]{:S(2)}, u32[]{:S(2)}) async-start(bf16[4,256,1408]{1,2,0:T(8,128)(2,1)} %copy.79), calls=%async_computation.7 | async-start | bytes 5767168 | tf_op jit(solution)/shard_map/all_to_all | solution.py:667
  706.7 196.9 %reduce-scatter.5.cloned.1.call-start = ((), (), s32[]{:S(2)}) async-start(), calls=%async_computation.18 | async-start | bytes 5570560 | tf_op jit(solution)/shard_map/reduce_scatter | solution.py:619
  759.5 54.0 %all-to-all-start.8 = ((bf16[4,128,1408]{2,1,0:T(8,128)(2,1)}), bf16[4,128,1408]{2,1,0:T(8,128)(2,1)S(1)}, u32[]{:S(2)}, u32[]{:S(2)}) async-start(bf16[4,128,1408]{2,1,0:T(8,128)(2,1)} %slice.509), calls=%async_computation.10 | async-start | bytes 2883584 | tf_op jit(solution)/shard_map/all_to_all | solution.py:667
  778.7 53.8 %collective-permute-start.59 = (bf16[1024,512]{1,0:T(8,128)(2,1)}, bf16[1024,512]{1,0:T(8,128)(2,1)}, u32[]{:S(2)}, u32[]{:S(2)}) collective-permute-start(bf16[1024,512]{1,0:T(8,128)(2,1)} %fusion.30), channel_id=1, source_target_pairs={{0,16},{16,0},{1,17},{17,1},{2,18},{18,2},{3,19},{19,3},{4,20},{20... | collective-permute-start | bytes 3145736 | tf_op jit(solution)/shard_map/ppermute | solution.py:671
  813.4 91.2 %all-to-all-start.9 = ((bf16[4,256,1408]{2,1,0:T(8,128)(2,1)}), bf16[4,256,1408]{2,1,0:T(8,128)(2,1)}, u32[]{:S(2)}, u32[]{:S(2)}) async-start(bf16[4,256,1408]{2,1,0:T(8,128)(2,1)} %bitcast.300), calls=%async_computation.11 | async-start | bytes 5767168 | tf_op jit(solution)/shard_map/all_to_all | solution.py:667
  906.5 49.1 %collective-permute-start.63 = (bf16[320,512]{1,0:T(8,128)(2,1)}, bf16[320,512]{1,0:T(8,128)(2,1)}, u32[]{:S(2)}, u32[]{:S(2)}) collective-permute-start(bf16[320,512]{1,0:T(8,128)(2,1)} %add_convert_fusion.6), channel_id=1, source_target_pairs={{0,3},{1,2},{2,1},{3,0},{4,7},{5,6},{6,5},{7,4},{8,11},{9,10},{10,... | collective-permute-start | bytes 983048 | tf_op jit(solution)/shard_map/ppermute | solution.py:519
  906.5 49.5 %collective-permute-start.62 = (bf16[320,512]{1,0:T(8,128)(2,1)}, bf16[320,512]{1,0:T(8,128)(2,1)}, u32[]{:S(2)}, u32[]{:S(2)}) collective-permute-start(bf16[320,512]{1,0:T(8,128)(2,1)} %add_convert_fusion.6), channel_id=1, source_target_pairs={{0,2},{1,3},{2,0},{3,1},{4,6},{5,7},{6,4},{7,5},{8,10},{9,11},{10,... | collective-permute-start | bytes 983048 | tf_op jit(solution)/shard_map/ppermute | solution.py:519
  (173 other events, 2982.4 us)
Sparse Core Ops, SparseCore 0:
  10.9 91.2 all-gather.3
  183.5 105.1 reduce-scatter.2
  321.2 76.3 all-gather.5
  585.1 97.1 all-gather.7
  756.4 91.3 reduce-scatter.4

commit v3 on v2

--- a/solution.py
+++ b/solution.py
@@ -597,12 +597,12 @@
     size = right.shape[0] // tps
     return pl.pallas_call(
         outward_kernel,
-        grid=(tps, count // ROWS),
+        grid=(tps,),
         in_specs=[
-            pl.BlockSpec((ROWS, depth), lambda q, i: (i, 0)),
-            pl.BlockSpec((size, depth), lambda q, i: (q, 0)),
+            pl.BlockSpec((count, depth), lambda q: (0, 0)),
+            pl.BlockSpec((size, depth), lambda q: (q, 0)),
         ],
-        out_specs=pl.BlockSpec((1, ROWS, size), lambda q, i: (q, i, 0)),
+        out_specs=pl.BlockSpec((1, count, size), lambda q: (q, 0, 0)),
         out_shape=jax.ShapeDtypeStruct((tps, count, size), jnp.bfloat16),
         compiler_params=pltpu.CompilerParams(vmem_limit_bytes=32 * 1024 * 1024),
         cost_estimate=pl.CostEstimate(
@@ -727,7 +727,7 @@
     dk_ref[...] += dot(score_back, q_ref[...], (0, 0)) * scale
 
 
-ROWS = 256
+ROWS = 640
 
 
 def attend(queries, keys, values, bias):
@@ -1136,7 +1136,7 @@
             [head_gates[choice][:, None] * pair_back[choice] for choice in range(TOP)], axis=0
         )
     )
-    mixed_back, down_back = tie(mixed_back, down_back)
+    mixed_back, down_back, head_gate_back = tie(mixed_back, down_back, head_gate_back)
     gate_returned = [exchange(after(gate_ready, down_back)[:, :half])]
     query_change, key_change, value_change = attend_back(
         queries, keys, values, bias, norm, mixed_back
@@ -1153,9 +1153,7 @@
             axis=1,
         )
     )
-    change, head_gate_back, arrived[2], gate_returned[0] = tie(
-        change, head_gate_back, arrived[2], gate_returned[0]
-    )
+    change, arrived[2], gate_returned[0] = tie(change, arrived[2], gate_returned[0])
     feed = from_slots(after(fed, change))
     gate_returned.append(exchange(after(gate_ready, gate_returned[0])[:, half:]))
     up_ready = near_gradient(slot_rows, after(up_back, change), arrived[2])
@@ -1173,7 +1171,6 @@
     output = share_out(bf16(hidden_state + feed))
     output_all = exchange(output_ready)
     project_all = exchange(after(project_ready, output_all))
-    output_all, project_all = f32(output_all), f32(project_all)
     down_gradient = f32(down_back.transpose(0, 2, 1))
     gate_gradient = f32(jnp.concatenate(gate_returned, axis=1))
     up_gradient = f32(up_returned)
@@ -1234,12 +1231,16 @@
     value_gradient = (
         project_all[:, :, inner + HEAD_DIM :].transpose(1, 0, 2).reshape(depth_here, local_width)
     )
+    query_gradient, key_gradient, value_gradient = [
+        f32(after(item)) for item in (query_gradient, key_gradient, value_gradient)
+    ]
     output_gradient = (
-        f32(output_all)
+        output_all
         .reshape(heads, depth_here, experts, HEAD_DIM)
         .transpose(2, 0, 3, 1)
         .reshape(experts, local_width, depth_here)
     )
+    output_gradient = f32(after(output_gradient))
 
     head_peaks = jnp.max(
         small_sums[-1, : shards * steps].reshape(shards, steps), axis=0

time: 1020 us -> 1010 us (level)
  waiting for transfers between devices: 483 us -> 498 us
    all_to_all x12, waiting for transfers between devices: 67.2 us -> 78.5 us  [exchange(): return lax.all_to_all(parts, CTX, 0, 0)]
    convert_element_type x7 -> x10, other arithmetic: 17.3 us -> 21.9 us  [f32(): return value.astype(jnp.float32)]
    unnamed x220 -> x208, local copies, waits for them, and re-layouts: 25.8 us -> 25.6 us
  transfers between devices with their start and end apart: 94 -> 94, of which waited for: 46 -> 48; matrix products, arithmetic and copies ran while one was open for 24% -> 24% of each run, Pallas kernels for 3% -> 3%
where the time goes in v3:
time: 1010 us
  waiting for transfers between devices  498 us (49%)
  starting transfers between devices  146 us (14%)
  matrix products  120 us (12%)
  other arithmetic  106 us (10%)
  local copies, waits for them, and re-layouts  89.6 us (9%)
  Pallas kernels  33.3 us (3%)
  between operations  16.1 us (2%)
    ppermute x24, waiting for transfers between devices, along(): lax.ppermute(value, axis, [(place, (place + step) % count) for place in r...  143 us
    dot_general x23, matrix products, dot(): lax.dot_general(left, right, ((contract[:1], contract[1:]), ((), ())), pr...  112 us
    ppermute x13, waiting for transfers between devices, swap(): return lax.ppermute(value, SHARD, [(0, 1), (1, 0)])  110 us
    reduce_scatter x2, waiting for transfers between devices, scatter_dense(): lax.psum_scatter(part, (TP, CTX), scatter_dimension=0, tiled=True)  97.5 us
    all_to_all x12, waiting for transfers between devices, exchange(): return lax.all_to_all(parts, CTX, 0, 0)  78.5 us
    all_to_all x12, starting transfers between devices, exchange(): return lax.all_to_all(parts, CTX, 0, 0)  58.4 us
    ppermute x40, waiting for transfers between devices, across(): lax.ppermute(value, TP, [(place, place ^ bits) for place in range(count)])  44.1 us
    ppermute x24, starting transfers between devices, along(): lax.ppermute(value, axis, [(place, (place + step) % count) for place in r...  42 us
  transfers between devices with their start and end apart: 94, of which 48 were waited for; matrix products, arithmetic and copies ran while one was open for 24% of the time, Pallas kernels for 3%

profile of v3, /device:TPU:0, one launch (start us, length us, event | category | flops | bytes accessed | tf_op | source)
XLA Modules:
  0.0 1008.9 jit_solution(13820362005653692495)
XLA Ops:
  24.8 31.1 %collective-permute-done.2 = bf16[14,320]{1,0:T(8,128)(2,1)S(1)} collective-permute-done((bf16[14,320]{1,0:T(8,128)(2,1)S(1)}, bf16[14,320]{1,0:T(8,128)(2,1)S(1)}, u32[]{:S(2)}, u32[]{:S(2)}) %collective-permute-start.2) | collective-permute-done | bytes 8992 | tf_op jit(solution)/shard_map/ppermute | solution.py:514
  56.0 14.1 %collective-permute-done.1 = bf16[14,320]{1,0:T(8,128)(2,1)S(1)} collective-permute-done((bf16[14,320]{1,0:T(8,128)(2,1)S(1)}, bf16[14,320]{1,0:T(8,128)(2,1)S(1)}, u32[]{:S(2)}, u32[]{:S(2)}) %collective-permute-start.1) | collective-permute-done | bytes 8992 | tf_op jit(solution)/shard_map/ppermute | solution.py:514
  81.0 30.9 %collective-permute-done.3 = bf16[1024,10]{0,1:T(8,128)(2,1)S(1)} collective-permute-done((bf16[1024,10]{0,1:T(8,128)(2,1)S(1)}, bf16[1024,10]{0,1:T(8,128)(2,1)S(1)}, u32[]{:S(2)}, u32[]{:S(2)}) %collective-permute-start.3) | collective-permute-done | bytes 20512 | tf_op jit(solution)/shard_map/ppermute | solution.py:671
  156.2 11.4 %shard_map.271 = (bf16[2560,128]{1,0:T(8,128)(2,1)S(1)}, f32[2560,128]{1,0:T(8,128)S(1)}, f32[32,128]{1,0:T(8,128)S(1)}) custom-call(bf16[2560,128]{1,0:T(8,128)(2,1)S(1)} %pad_maximum_fusion.25.q_ref, bf16[1280,128]{1,0:T(8,128)(2,1)S(1)} %get-tuple-element.163.k_ref, bf16[1280,128]{1,0:T(8,128)(2,1)S(1)} %slice.866.v_ref, ...), custom_call_target="tpu_custom_call" | custom-call | flops 1677721600 | bytes 9175040 | tf_op jit(solution)/shard_map/pallas_call | solution.py:739
  190.2 97.5 %reduce-scatter.3.cloned.1.call-done = bf16[320,512]{1,0:T(8,128)(2,1)} async-done(((bf16[5120,512]{1,0:T(8,128)(2,1)}), bf16[320,512]{1,0:T(8,128)(2,1)}) %reduce-scatter.3.cloned.1.call-update) | async-done | bytes 327696 | tf_op jit(solution)/shard_map/reduce_scatter | solution.py:619
  306.0 12.3 %collective-permute-done.11 = bf16[192,512]{1,0:T(8,128)(2,1)S(1)} collective-permute-done((bf16[192,512]{1,0:T(8,128)(2,1)S(1)}, bf16[192,512]{1,0:T(8,128)(2,1)S(1)}, u32[]{:S(2)}, u32[]{:S(2)}) %collective-permute-start.11) | collective-permute-done | bytes 196640 | tf_op jit(solution)/shard_map/ppermute | solution.py:514
  354.7 14.3 %collective-permute-done.21 = f32[1,192]{1,0:T(1,128)S(1)} collective-permute-done((f32[1,192]{1,0:T(1,128)S(1)}, f32[1,192]{1,0:T(1,128)S(1)}, u32[]{:S(2)}, u32[]{:S(2)}) %collective-permute-start.21) | collective-permute-done | bytes 800 | tf_op jit(solution)/shard_map/ppermute | solution.py:514
  373.8 17.8 %collective-permute-done.20 = f32[1,192]{1,0:T(1,128)S(1)} collective-permute-done((f32[1,192]{1,0:T(1,128)S(1)}, f32[1,192]{1,0:T(1,128)S(1)}, u32[]{:S(2)}, u32[]{:S(2)}) %collective-permute-start.20) | collective-permute-done | bytes 800 | tf_op jit(solution)/shard_map/ppermute | solution.py:514
  414.5 22.1 %all-to-all-done.5 = bf16[4,128,1408]{2,1,0:T(8,128)(2,1)} async-done(((bf16[4,128,1408]{2,1,0:T(8,128)(2,1)}), bf16[4,128,1408]{2,1,0:T(8,128)(2,1)}, u32[]{:S(2)}, u32[]{:S(2)}) %all-to-all-start.5) | async-done | bytes 1441824 | tf_op jit(solution)/shard_map/all_to_all | solution.py:667
  452.5 17.3 %collective-permute-done.23 = bf16[4,128,1408]{2,1,0:T(8,128)(2,1)S(1)} collective-permute-done((bf16[4,128,1408]{2,1,0:T(8,128)(2,1)}, bf16[4,128,1408]{2,1,0:T(8,128)(2,1)S(1)}, u32[]{:S(2)}, u32[]{:S(2)}) %collective-permute-start.23) | collective-permute-done | bytes 1441824 | tf_op jit(solution)/shard_map/ppermute | solution.py:671
  477.5 11.9 %multiply_reduce_fusion = (f32[768]{0:T(1024)S(1)}, bf16[768,1408]{1,0:T(8,128)(2,1)S(1)}, bf16[768,1408]{1,0:T(8,128)(2,1)S(1)}, bf16[768,1408]{1,0:T(8,128)(2,1)S(1)}) fusion(f32[768,1408]{1,0:T(8,128)} %fusion.8, f32[768,1408]{1,0:T(8,128)} %fusion.6, f32[768]{0:T(1024)S(1)} %reduce.17, bf16[768,2048]{1,0:T(8,128)(2,1)S(1)} %bitcast.315, ...), kind=kOutput, calls=%fused_computation.30 | convolution fusion | flops 4462345216 | bytes 24057856 | tf_op jit(solution)/shard_map/dot_general | solution.py:531
  503.4 8.6 fusion.5
  512.0 8.8 add_convert_fusion
  599.3 50.9 %collective-permute-done.43 = bf16[1024,1408]{1,0:T(8,128)(2,1)} collective-permute-done((bf16[1024,1408]{1,0:T(8,128)(2,1)}, bf16[1024,1408]{1,0:T(8,128)(2,1)}, u32[]{:S(2)}, u32[]{:S(2)}) %collective-permute-start.43) | collective-permute-done | bytes 2883616 | tf_op jit(solution)/shard_map/ppermute | solution.py:671
  650.1 7.2 add_convert_fusion.2
  657.3 24.3 %all-gather.8.cloned.1.call-done = bf16[5120,512]{1,0:T(8,128)(2,1)} async-done(((bf16[320,512]{1,0:T(8,128)(2,1)}), bf16[5120,512]{1,0:T(8,128)(2,1)}) %all-gather.8.cloned.1.call-update) | async-done | bytes 5242896 | tf_op jit(solution)/shard_map/all_gather | solution.py:584
  696.1 7.2 collective-permute-start.47
  721.1 13.4 %shard_map.273 = (f32[2560,128]{1,0:T(8,128)S(1)}, f32[1280,128]{1,0:T(8,128)S(1)}, f32[1280,128]{1,0:T(8,128)S(1)}) custom-call(bf16[2560,128]{1,0:T(8,128)(2,1)S(1)} %copy-done.7, bf16[1280,128]{1,0:T(8,128)(2,1)S(1)} %copy-done.10, bf16[1280,128]{1,0:T(8,128)(2,1)S(1)} %copy-done.12, bf16[1280,1280]{1,0:T(8,128)(2,1)} %select_convert_fusion.bias_ref, ...), custom_call_target="tpu_custom_call" | custom-call | flops 4194304000 | bytes 10485760 | tf_op jit(solution)/shard_map/pallas_call | solution.py:764
  764.9 10.7 %fusion.11 = bf16[768,2048]{1,0:T(8,128)(2,1)} fusion(bf16[768,1408]{1,0:T(8,128)(2,1)} %copy-done.90, bf16[1024,1408]{1,0:T(8,128)(2,1)} %bitcast.323, bf16[1024,1408]{1,0:T(8,128)(2,1)} %bitcast.321), kind=kOutput, calls=%fused_computation.45 | convolution fusion | flops 4442292224 | bytes 11075584 | tf_op jit(solution)/shard_map/dot_general | solution.py:531
  788.7 27.9 %all-to-all-done.8 = bf16[4,128,1408]{2,1,0:T(8,128)(2,1)S(1)} async-done(((bf16[4,128,1408]{2,1,0:T(8,128)(2,1)}), bf16[4,128,1408]{2,1,0:T(8,128)(2,1)S(1)}, u32[]{:S(2)}, u32[]{:S(2)}) %all-to-all-start.8) | async-done | bytes 1441824 | tf_op jit(solution)/shard_map/all_to_all | solution.py:667
  862.5 7.4 collective-permute-done.60
  873.4 13.2 %collective-permute-done.58 = bf16[192,512]{1,0:T(8,128)(2,1)S(1)} collective-permute-done((bf16[192,512]{1,0:T(8,128)(2,1)S(1)}, bf16[192,512]{1,0:T(8,128)(2,1)S(1)}, u32[]{:S(2)}, u32[]{:S(2)}) %collective-permute-start.58) | collective-permute-done | bytes 196640 | tf_op jit(solution)/shard_map/ppermute | solution.py:514
  886.6 19.7 %collective-permute-done.56 = bf16[192,512]{1,0:T(8,128)(2,1)S(1)} collective-permute-done((bf16[192,512]{1,0:T(8,128)(2,1)S(1)}, bf16[192,512]{1,0:T(8,128)(2,1)S(1)}, u32[]{:S(2)}, u32[]{:S(2)}) %collective-permute-start.56) | collective-permute-done | bytes 196640 | tf_op jit(solution)/shard_map/ppermute | solution.py:514
  973.4 19.5 %all-to-all-done.11 = bf16[4,256,768]{2,1,0:T(8,128)(2,1)S(1)} async-done(((bf16[4,256,768]{2,1,0:T(8,128)(2,1)}), bf16[4,256,768]{2,1,0:T(8,128)(2,1)S(1)}, u32[]{:S(2)}, u32[]{:S(2)}) %all-to-all-start.11) | async-done | bytes 1572896 | tf_op jit(solution)/shard_map/all_to_all | solution.py:667
  (668 shorter events, 493.2 us)
Async XLA Ops:
  7.2 112.4 %all-gather.4.cloned.1.call-start = ((), (), s32[]{:S(2)}) async-start(), calls=%async_computation.14 | async-start | bytes 5570560 | tf_op jit(solution)/shard_map/all_gather | solution.py:866
  13.2 57.5 %all-to-all-start = ((bf16[4,256,768]{2,1,0:T(8,128)(2,1)}), bf16[4,256,768]{2,1,0:T(8,128)(2,1)S(1)}, u32[]{:S(2)}, u32[]{:S(2)}) async-start(bf16[4,256,768]{2,1,0:T(8,128)(2,1)} %pad_maximum_fusion.17), calls=%async_computation | async-start | bytes 3145728 | tf_op jit(solution)/shard_map/all_to_all | solution.py:667
  112.0 69.6 %all-to-all-start.2 = ((bf16[4,256,1408]{2,1,0:T(8,128)(2,1)}), bf16[4,256,1408]{2,1,0:T(8,128)(2,1)}, u32[]{:S(2)}, u32[]{:S(2)}) async-start(bf16[4,256,1408]{2,1,0:T(8,128)(2,1)} %param.28), calls=%async_computation.3 | async-start | bytes 5767168 | tf_op jit(solution)/shard_map/all_to_all | solution.py:667
  116.7 171.1 %reduce-scatter.3.cloned.1.call-start = ((), (), s32[]{:S(2)}) async-start(), calls=%async_computation.15 | async-start | bytes 5570560 | tf_op jit(solution)/shard_map/reduce_scatter | solution.py:619
  181.5 109.6 %all-to-all-start.3 = ((bf16[4,256,1408]{2,1,0:T(8,128)(2,1)}), bf16[4,256,1408]{2,1,0:T(8,128)(2,1)}, u32[]{:S(2)}, u32[]{:S(2)}) async-start(bf16[4,256,1408]{2,1,0:T(8,128)(2,1)} %param.29), calls=%async_computation.4 | async-start | bytes 5767168 | tf_op jit(solution)/shard_map/all_to_all | solution.py:667
  186.1 286.9 %all-gather.6.cloned.1.call-start = ((), (), s32[]{:S(2)}) async-start(), calls=%async_computation.16 | async-start | bytes 5570560 | tf_op jit(solution)/shard_map/all_gather | solution.py:866
  186.2 103.4 %collective-permute-start.6 = (bf16[4,256,1408]{2,1,0:T(8,128)(2,1)}, bf16[4,256,1408]{2,1,0:T(8,128)(2,1)S(1)}, u32[]{:S(2)}, u32[]{:S(2)}) collective-permute-start(bf16[4,256,1408]{2,1,0:T(8,128)(2,1)} %all-to-all-done.2), channel_id=1, source_target_pairs={{0,16},{16,0},{1,17},{17,1},{2,18},{18,2},{3,19},{19,3},{4,20},{20... | collective-permute-start | bytes 8650760 | tf_op jit(solution)/shard_map/ppermute | solution.py:671
  322.1 118.6 %collective-permute-start.24 = (bf16[4,256,1408]{2,1,0:T(8,128)(2,1)}, bf16[4,256,1408]{2,1,0:T(8,128)(2,1)}, u32[]{:S(2)}, u32[]{:S(2)}) collective-permute-start(bf16[4,256,1408]{2,1,0:T(8,128)(2,1)} %all-to-all-done.3), channel_id=1, source_target_pairs={{0,16},{16,0},{1,17},{17,1},{2,18},{18,2},{3,19},{19,3},{4,20},{20... | collective-permute-start | bytes 8650760 | tf_op jit(solution)/shard_map/ppermute | solution.py:671
  330.7 64.4 %all-to-all-start.4 = ((bf16[4,128,1408]{2,1,0:T(8,128)(2,1)}), bf16[4,128,1408]{2,1,0:T(8,128)(2,1)S(1)}, u32[]{:S(2)}, u32[]{:S(2)}) async-start(bf16[4,128,1408]{2,1,0:T(8,128)(2,1)} %slice.579), calls=%async_computation.5 | async-start | bytes 2883584 | tf_op jit(solution)/shard_map/all_to_all | solution.py:667
  340.1 51.5 %collective-permute-start.20 = (f32[1,192]{1,0:T(1,128)S(1)}, f32[1,192]{1,0:T(1,128)S(1)}, u32[]{:S(2)}, u32[]{:S(2)}) collective-permute-start(f32[1,192]{1,0:T(1,128)S(1)} %get-tuple-element.301), channel_id=1, source_target_pairs={{0,8},{4,12},{8,0},{12,4},{1,9},{5,13},{9,1},{13,5},{2,10},{6,14},... | collective-permute-start | bytes 2312 | tf_op jit(solution)/shard_map/ppermute | solution.py:514
  353.9 47.7 %collective-permute-start.13 = (bf16[768,512]{1,0:T(8,128)(2,1)S(1)}, bf16[768,512]{1,0:T(8,128)(2,1)}, u32[]{:S(2)}, u32[]{:S(2)}) collective-permute-start(bf16[768,512]{1,0:T(8,128)(2,1)S(1)} %constant_dynamic-update-slice_fusion.8), channel_id=1, source_target_pairs={{0,1},{1,0},{2,3},{3,2},{4,5},{5,4},{6,7},{7,6},{8,9},{9,8},{10,11... | collective-permute-start | bytes 2359304 | tf_op jit(solution)/shard_map/ppermute | solution.py:519
  401.7 279.9 %all-gather.8.cloned.1.call-start = ((), (), s32[]{:S(2)}) async-start(), calls=%async_computation.17 | async-start | bytes 5570560 | tf_op jit(solution)/shard_map/all_gather | solution.py:584
  404.0 46.8 %collective-permute-start.22 = (bf16[4,128,1408]{2,1,0:T(8,128)(2,1)S(1)}, bf16[4,128,1408]{2,1,0:T(8,128)(2,1)}, u32[]{:S(2)}, u32[]{:S(2)}) collective-permute-start(bf16[4,128,1408]{2,1,0:T(8,128)(2,1)S(1)} %all-to-all-done.4), channel_id=1, source_target_pairs={{0,16},{16,0},{1,17},{17,1},{2,18},{18,2},{3,19},{19,3},{4,20},{20... | collective-permute-start | bytes 4325384 | tf_op jit(solution)/shard_map/ppermute | solution.py:671
  501.9 69.6 %collective-permute-start.33 = (bf16[1024,1408]{1,0:T(8,128)(2,1)}, bf16[1024,1408]{1,0:T(8,128)(2,1)}, u32[]{:S(2)}, u32[]{:S(2)}) collective-permute-start(bf16[1024,1408]{1,0:T(8,128)(2,1)} %convolution_convert_fusion.2), channel_id=1, source_target_pairs={{0,16},{16,0},{1,17},{17,1},{2,18},{18,2},{3,19},{19,3},{4,20},{20... | collective-permute-start | bytes 8650760 | tf_op jit(solution)/shard_map/ppermute | solution.py:671
  584.3 65.8 %collective-permute-start.43 = (bf16[1024,1408]{1,0:T(8,128)(2,1)}, bf16[1024,1408]{1,0:T(8,128)(2,1)}, u32[]{:S(2)}, u32[]{:S(2)}) collective-permute-start(bf16[1024,1408]{1,0:T(8,128)(2,1)} %convolution_convert_fusion.1), channel_id=1, source_target_pairs={{0,16},{16,0},{1,17},{17,1},{2,18},{18,2},{3,19},{19,3},{4,20},{20... | collective-permute-start | bytes 8650760 | tf_op jit(solution)/shard_map/ppermute | solution.py:671
  587.5 154.8 %collective-permute-start.50 = (bf16[1024,1408]{1,0:T(8,128)(2,1)}, bf16[1024,1408]{1,0:T(8,128)(2,1)}, u32[]{:S(2)}, u32[]{:S(2)}) collective-permute-start(bf16[1024,1408]{1,0:T(8,128)(2,1)} %convolution_convert_fusion), channel_id=1, source_target_pairs={{0,16},{16,0},{1,17},{17,1},{2,18},{18,2},{3,19},{19,3},{4,20},{20... | collective-permute-start | bytes 8650760 | tf_op jit(solution)/shard_map/ppermute | solution.py:671
  593.6 115.1 %all-to-all-start.6 = ((bf16[4,256,1408]{1,2,0:T(8,128)(2,1)}), bf16[4,256,1408]{1,2,0:T(8,128)(2,1)}, u32[]{:S(2)}, u32[]{:S(2)}) async-start(bf16[4,256,1408]{1,2,0:T(8,128)(2,1)} %copy.79), calls=%async_computation.7 | async-start | bytes 5767168 | tf_op jit(solution)/shard_map/all_to_all | solution.py:667
  715.6 192.1 %reduce-scatter.5.cloned.1.call-start = ((), (), s32[]{:S(2)}) async-start(), calls=%async_computation.18 | async-start | bytes 5570560 | tf_op jit(solution)/shard_map/reduce_scatter | solution.py:619
  761.3 55.3 %all-to-all-start.8 = ((bf16[4,128,1408]{2,1,0:T(8,128)(2,1)}), bf16[4,128,1408]{2,1,0:T(8,128)(2,1)S(1)}, u32[]{:S(2)}, u32[]{:S(2)}) async-start(bf16[4,128,1408]{2,1,0:T(8,128)(2,1)} %slice.509), calls=%async_computation.10 | async-start | bytes 2883584 | tf_op jit(solution)/shard_map/all_to_all | solution.py:667
  780.5 59.0 %collective-permute-start.59 = (bf16[1024,512]{1,0:T(8,128)(2,1)}, bf16[1024,512]{1,0:T(8,128)(2,1)}, u32[]{:S(2)}, u32[]{:S(2)}) collective-permute-start(bf16[1024,512]{1,0:T(8,128)(2,1)} %fusion.30), channel_id=1, source_target_pairs={{0,16},{16,0},{1,17},{17,1},{2,18},{18,2},{3,19},{19,3},{4,20},{20... | collective-permute-start | bytes 3145736 | tf_op jit(solution)/shard_map/ppermute | solution.py:671
  816.6 92.2 %all-to-all-start.9 = ((bf16[4,256,1408]{2,1,0:T(8,128)(2,1)}), bf16[4,256,1408]{2,1,0:T(8,128)(2,1)}, u32[]{:S(2)}, u32[]{:S(2)}) async-start(bf16[4,256,1408]{2,1,0:T(8,128)(2,1)} %bitcast.300), calls=%async_computation.11 | async-start | bytes 5767168 | tf_op jit(solution)/shard_map/all_to_all | solution.py:667
  858.7 47.7 %collective-permute-start.56 = (bf16[192,512]{1,0:T(8,128)(2,1)S(1)}, bf16[192,512]{1,0:T(8,128)(2,1)S(1)}, u32[]{:S(2)}, u32[]{:S(2)}) collective-permute-start(bf16[192,512]{1,0:T(8,128)(2,1)S(1)} %get-tuple-element.235), channel_id=1, source_target_pairs={{0,8},{4,12},{8,0},{12,4},{1,9},{5,13},{9,1},{13,5},{2,10},{6,14},... | collective-permute-start | bytes 589832 | tf_op jit(solution)/shard_map/ppermute | solution.py:514
  910.7 47.8 %collective-permute-start.63 = (bf16[320,512]{1,0:T(8,128)(2,1)}, bf16[320,512]{1,0:T(8,128)(2,1)}, u32[]{:S(2)}, u32[]{:S(2)}) collective-permute-start(bf16[320,512]{1,0:T(8,128)(2,1)} %add_convert_fusion.6), channel_id=1, source_target_pairs={{0,3},{1,2},{2,1},{3,0},{4,7},{5,6},{6,5},{7,4},{8,11},{9,10},{10,... | collective-permute-start | bytes 983048 | tf_op jit(solution)/shard_map/ppermute | solution.py:519
  910.7 48.7 %collective-permute-start.62 = (bf16[320,512]{1,0:T(8,128)(2,1)}, bf16[320,512]{1,0:T(8,128)(2,1)}, u32[]{:S(2)}, u32[]{:S(2)}) collective-permute-start(bf16[320,512]{1,0:T(8,128)(2,1)} %add_convert_fusion.6), channel_id=1, source_target_pairs={{0,2},{1,3},{2,0},{3,1},{4,6},{5,7},{6,4},{7,5},{8,10},{9,11},{10,... | collective-permute-start | bytes 983048 | tf_op jit(solution)/shard_map/ppermute | solution.py:519
  (167 other events, 2709.0 us)
Sparse Core Ops, SparseCore 0:
  10.9 91.2 all-gather.3
  179.7 108.0 reduce-scatter.2
  320.3 76.2 all-gather.5
  584.5 97.0 all-gather.7
  758.2 95.1 reduce-scatter.4

commit v4 on v3

--- a/solution.py
+++ b/solution.py
@@ -1042,7 +1042,7 @@
     down_far.append(swap(down_near[1]))
     slot_rows, down_near[0] = tie(gather_columns(row_blocks), down_near[0])
     down_near[1], gate_slot = tie(down_near[1], gate_slot)
-    all_cotangent = gather_rows(after(cotangent, *row_blocks))
+    all_cotangent = gather_rows(after(cotangent, down_near[0]))
     slot_upstream = bf16(
         jnp.einsum(
             "bst,btd->bsd",

time: 1010 us -> 1040 us (1.030)
  starting transfers between devices: 146 us -> 167 us
    ppermute x24, waiting for transfers between devices: 143 us -> 114 us  [along(): lax.ppermute(value, axis, [(place, (place + step) % count) for place in r...]
    ppermute x24, starting transfers between devices: 42 us -> 64 us  [along(): lax.ppermute(value, axis, [(place, (place + step) % count) for place in r...]
    all_to_all x12, waiting for transfers between devices: 78.5 us -> 95.6 us  [exchange(): return lax.all_to_all(parts, CTX, 0, 0)]
    ppermute x13, waiting for transfers between devices: 110 us -> 122 us  [swap(): return lax.ppermute(value, SHARD, [(0, 1), (1, 0)])]
    unnamed x208 -> x200, local copies, waits for them, and re-layouts: 25.6 us -> 24.1 us
  transfers between devices with their start and end apart: 94 -> 94, of which waited for: 48 -> 44; matrix products, arithmetic and copies ran while one was open for 24% -> 23% of each run, Pallas kernels for 3% -> 3%
where the time goes in v4:
time: 1040 us
  waiting for transfers between devices  502 us (48%)
  starting transfers between devices  167 us (16%)
  matrix products  123 us (12%)
  other arithmetic  109 us (10%)
  local copies, waits for them, and re-layouts  87.2 us (8%)
  Pallas kernels  33.3 us (3%)
  between operations  16.1 us (2%)
    ppermute x13, waiting for transfers between devices, swap(): return lax.ppermute(value, SHARD, [(0, 1), (1, 0)])  122 us
    dot_general x23, matrix products, dot(): lax.dot_general(left, right, ((contract[:1], contract[1:]), ((), ())), pr...  114 us
    ppermute x24, waiting for transfers between devices, along(): lax.ppermute(value, axis, [(place, (place + step) % count) for place in r...  114 us
    reduce_scatter x2, waiting for transfers between devices, scatter_dense(): lax.psum_scatter(part, (TP, CTX), scatter_dimension=0, tiled=True)  97.5 us
    all_to_all x12, waiting for transfers between devices, exchange(): return lax.all_to_all(parts, CTX, 0, 0)  95.6 us
    ppermute x24, starting transfers between devices, along(): lax.ppermute(value, axis, [(place, (place + step) % count) for place in r...  64 us
    all_to_all x12, starting transfers between devices, exchange(): return lax.all_to_all(parts, CTX, 0, 0)  57.9 us
    ppermute x40, waiting for transfers between devices, across(): lax.ppermute(value, TP, [(place, place ^ bits) for place in range(count)])  47.5 us
  transfers between devices with their start and end apart: 94, of which 44 were waited for; matrix products, arithmetic and copies ran while one was open for 23% of the time, Pallas kernels for 3%

profile of v4, /device:TPU:0, one launch (start us, length us, event | category | flops | bytes accessed | tf_op | source)
XLA Modules:
  0.0 1037.0 jit_solution(9794086314631548687)
XLA Ops:
  24.8 31.1 %collective-permute-done.2 = bf16[14,320]{1,0:T(8,128)(2,1)S(1)} collective-permute-done((bf16[14,320]{1,0:T(8,128)(2,1)S(1)}, bf16[14,320]{1,0:T(8,128)(2,1)S(1)}, u32[]{:S(2)}, u32[]{:S(2)}) %collective-permute-start.2) | collective-permute-done | bytes 8992 | tf_op jit(solution)/shard_map/ppermute | solution.py:514
  56.0 14.1 %collective-permute-done.1 = bf16[14,320]{1,0:T(8,128)(2,1)S(1)} collective-permute-done((bf16[14,320]{1,0:T(8,128)(2,1)S(1)}, bf16[14,320]{1,0:T(8,128)(2,1)S(1)}, u32[]{:S(2)}, u32[]{:S(2)}) %collective-permute-start.1) | collective-permute-done | bytes 8992 | tf_op jit(solution)/shard_map/ppermute | solution.py:514
  81.5 30.4 %collective-permute-done.3 = bf16[1024,10]{0,1:T(8,128)(2,1)S(1)} collective-permute-done((bf16[1024,10]{0,1:T(8,128)(2,1)S(1)}, bf16[1024,10]{0,1:T(8,128)(2,1)S(1)}, u32[]{:S(2)}, u32[]{:S(2)}) %collective-permute-start.3) | collective-permute-done | bytes 20512 | tf_op jit(solution)/shard_map/ppermute | solution.py:671
  156.3 11.4 %shard_map.271 = (bf16[2560,128]{1,0:T(8,128)(2,1)S(1)}, f32[2560,128]{1,0:T(8,128)S(1)}, f32[32,128]{1,0:T(8,128)S(1)}) custom-call(bf16[2560,128]{1,0:T(8,128)(2,1)S(1)} %pad_maximum_fusion.25.q_ref, bf16[1280,128]{1,0:T(8,128)(2,1)S(1)} %get-tuple-element.163.k_ref, bf16[1280,128]{1,0:T(8,128)(2,1)S(1)} %slice.866.v_ref, ...), custom_call_target="tpu_custom_call" | custom-call | flops 1677721600 | bytes 9175040 | tf_op jit(solution)/shard_map/pallas_call | solution.py:739
  190.2 97.5 %reduce-scatter.3.cloned.1.call-done = bf16[320,512]{1,0:T(8,128)(2,1)} async-done(((bf16[5120,512]{1,0:T(8,128)(2,1)}), bf16[320,512]{1,0:T(8,128)(2,1)}) %reduce-scatter.3.cloned.1.call-update) | async-done | bytes 327696 | tf_op jit(solution)/shard_map/reduce_scatter | solution.py:619
  322.0 17.3 %collective-permute-done.12 = bf16[192,512]{1,0:T(8,128)(2,1)S(1)} collective-permute-done((bf16[192,512]{1,0:T(8,128)(2,1)}, bf16[192,512]{1,0:T(8,128)(2,1)S(1)}, u32[]{:S(2)}, u32[]{:S(2)}) %collective-permute-start.12) | collective-permute-done | bytes 196640 | tf_op jit(solution)/shard_map/ppermute | solution.py:514
  368.6 9.0 collective-permute-start.20
  393.8 8.9 fusion.6
  402.7 39.2 %all-to-all-done.5 = bf16[4,128,1408]{2,1,0:T(8,128)(2,1)} async-done(((bf16[4,128,1408]{2,1,0:T(8,128)(2,1)}), bf16[4,128,1408]{2,1,0:T(8,128)(2,1)}, u32[]{:S(2)}, u32[]{:S(2)}) %all-to-all-start.5) | async-done | bytes 1441824 | tf_op jit(solution)/shard_map/all_to_all | solution.py:667
  460.4 28.5 %collective-permute-done.23 = bf16[4,128,1408]{2,1,0:T(8,128)(2,1)S(1)} collective-permute-done((bf16[4,128,1408]{2,1,0:T(8,128)(2,1)}, bf16[4,128,1408]{2,1,0:T(8,128)(2,1)S(1)}, u32[]{:S(2)}, u32[]{:S(2)}) %collective-permute-start.23) | collective-permute-done | bytes 1441824 | tf_op jit(solution)/shard_map/ppermute | solution.py:671
  496.6 11.9 %multiply_reduce_fusion = (f32[768]{0:T(1024)S(1)}, bf16[768,1408]{1,0:T(8,128)(2,1)S(1)}, bf16[768,1408]{1,0:T(8,128)(2,1)S(1)}, bf16[768,1408]{1,0:T(8,128)(2,1)S(1)}) fusion(f32[768,1408]{1,0:T(8,128)} %fusion.8, f32[768,1408]{1,0:T(8,128)} %fusion.6, f32[768]{0:T(1024)S(1)} %reduce.17, bf16[768,2048]{1,0:T(8,128)(2,1)S(1)} %bitcast.315, ...), kind=kOutput, calls=%fused_computation.30 | convolution fusion | flops 4462345216 | bytes 24057856 | tf_op jit(solution)/shard_map/dot_general | solution.py:531
  522.5 8.6 fusion.5
  531.1 8.8 add_convert_fusion
  546.3 12.2 %collective-permute-start.39 = (f32[1,192]{1,0:T(1,128)S(1)}, f32[1,192]{1,0:T(1,128)S(1)}, u32[]{:S(2)}, u32[]{:S(2)}) collective-permute-start(f32[1,192]{1,0:T(1,128)S(1)} %get-tuple-element.296), channel_id=1, source_target_pairs={{0,4},{4,8},{8,12},{12,0},{1,5},{5,9},{9,13},{13,1},{2,6},{6,10},{... | collective-permute-start | bytes 2312 | tf_op jit(solution)/shard_map/ppermute | solution.py:514
  627.5 49.9 %collective-permute-done.43 = bf16[1024,1408]{1,0:T(8,128)(2,1)} collective-permute-done((bf16[1024,1408]{1,0:T(8,128)(2,1)}, bf16[1024,1408]{1,0:T(8,128)(2,1)}, u32[]{:S(2)}, u32[]{:S(2)}) %collective-permute-start.43) | collective-permute-done | bytes 2883616 | tf_op jit(solution)/shard_map/ppermute | solution.py:671
  677.4 7.2 add_convert_fusion.2
  684.6 25.4 %all-gather.8.cloned.1.call-done = bf16[5120,512]{1,0:T(8,128)(2,1)} async-done(((bf16[320,512]{1,0:T(8,128)(2,1)}), bf16[5120,512]{1,0:T(8,128)(2,1)}) %all-gather.8.cloned.1.call-update) | async-done | bytes 5242896 | tf_op jit(solution)/shard_map/all_gather | solution.py:584
  749.4 13.4 %shard_map.273 = (f32[2560,128]{1,0:T(8,128)S(1)}, f32[1280,128]{1,0:T(8,128)S(1)}, f32[1280,128]{1,0:T(8,128)S(1)}) custom-call(bf16[2560,128]{1,0:T(8,128)(2,1)S(1)} %copy-done.7, bf16[1280,128]{1,0:T(8,128)(2,1)S(1)} %copy-done.10, bf16[1280,128]{1,0:T(8,128)(2,1)S(1)} %copy-done.12, bf16[1280,1280]{1,0:T(8,128)(2,1)} %select_convert_fusion.bias_ref, ...), custom_call_target="tpu_custom_call" | custom-call | flops 4194304000 | bytes 10485760 | tf_op jit(solution)/shard_map/pallas_call | solution.py:764
  793.2 10.7 %fusion.11 = bf16[768,2048]{1,0:T(8,128)(2,1)} fusion(bf16[768,1408]{1,0:T(8,128)(2,1)} %copy-done.86, bf16[1024,1408]{1,0:T(8,128)(2,1)} %bitcast.323, bf16[1024,1408]{1,0:T(8,128)(2,1)} %bitcast.321), kind=kOutput, calls=%fused_computation.45 | convolution fusion | flops 4442292224 | bytes 11075584 | tf_op jit(solution)/shard_map/dot_general | solution.py:531
  817.0 27.9 %all-to-all-done.8 = bf16[4,128,1408]{2,1,0:T(8,128)(2,1)S(1)} async-done(((bf16[4,128,1408]{2,1,0:T(8,128)(2,1)}), bf16[4,128,1408]{2,1,0:T(8,128)(2,1)S(1)}, u32[]{:S(2)}, u32[]{:S(2)}) %all-to-all-start.8) | async-done | bytes 1441824 | tf_op jit(solution)/shard_map/all_to_all | solution.py:667
  890.8 7.5 collective-permute-done.60
  901.7 13.2 %collective-permute-done.58 = bf16[192,512]{1,0:T(8,128)(2,1)S(1)} collective-permute-done((bf16[192,512]{1,0:T(8,128)(2,1)S(1)}, bf16[192,512]{1,0:T(8,128)(2,1)S(1)}, u32[]{:S(2)}, u32[]{:S(2)}) %collective-permute-start.58) | collective-permute-done | bytes 196640 | tf_op jit(solution)/shard_map/ppermute | solution.py:514
  914.9 19.7 %collective-permute-done.56 = bf16[192,512]{1,0:T(8,128)(2,1)S(1)} collective-permute-done((bf16[192,512]{1,0:T(8,128)(2,1)S(1)}, bf16[192,512]{1,0:T(8,128)(2,1)S(1)}, u32[]{:S(2)}, u32[]{:S(2)}) %collective-permute-start.56) | collective-permute-done | bytes 196640 | tf_op jit(solution)/shard_map/ppermute | solution.py:514
  1001.5 19.5 %all-to-all-done.11 = bf16[4,256,768]{2,1,0:T(8,128)(2,1)S(1)} async-done(((bf16[4,256,768]{2,1,0:T(8,128)(2,1)}), bf16[4,256,768]{2,1,0:T(8,128)(2,1)S(1)}, u32[]{:S(2)}, u32[]{:S(2)}) %all-to-all-start.11) | async-done | bytes 1572896 | tf_op jit(solution)/shard_map/all_to_all | solution.py:667
  (660 shorter events, 497.7 us)
Async XLA Ops:
  7.2 112.4 %all-gather.4.cloned.1.call-start = ((), (), s32[]{:S(2)}) async-start(), calls=%async_computation.14 | async-start | bytes 5570560 | tf_op jit(solution)/shard_map/all_gather | solution.py:866
  13.2 57.5 %all-to-all-start = ((bf16[4,256,768]{2,1,0:T(8,128)(2,1)}), bf16[4,256,768]{2,1,0:T(8,128)(2,1)S(1)}, u32[]{:S(2)}, u32[]{:S(2)}) async-start(bf16[4,256,768]{2,1,0:T(8,128)(2,1)} %pad_maximum_fusion.17), calls=%async_computation | async-start | bytes 3145728 | tf_op jit(solution)/shard_map/all_to_all | solution.py:667
  111.9 69.6 %all-to-all-start.2 = ((bf16[4,256,1408]{2,1,0:T(8,128)(2,1)}), bf16[4,256,1408]{2,1,0:T(8,128)(2,1)}, u32[]{:S(2)}, u32[]{:S(2)}) async-start(bf16[4,256,1408]{2,1,0:T(8,128)(2,1)} %param.28), calls=%async_computation.3 | async-start | bytes 5767168 | tf_op jit(solution)/shard_map/all_to_all | solution.py:667
  116.7 171.1 %reduce-scatter.3.cloned.1.call-start = ((), (), s32[]{:S(2)}) async-start(), calls=%async_computation.15 | async-start | bytes 5570560 | tf_op jit(solution)/shard_map/reduce_scatter | solution.py:619
  181.6 109.6 %all-to-all-start.3 = ((bf16[4,256,1408]{2,1,0:T(8,128)(2,1)}), bf16[4,256,1408]{2,1,0:T(8,128)(2,1)}, u32[]{:S(2)}, u32[]{:S(2)}) async-start(bf16[4,256,1408]{2,1,0:T(8,128)(2,1)} %param.29), calls=%async_computation.4 | async-start | bytes 5767168 | tf_op jit(solution)/shard_map/all_to_all | solution.py:667
  186.2 103.4 %collective-permute-start.6 = (bf16[4,256,1408]{2,1,0:T(8,128)(2,1)}, bf16[4,256,1408]{2,1,0:T(8,128)(2,1)S(1)}, u32[]{:S(2)}, u32[]{:S(2)}) collective-permute-start(bf16[4,256,1408]{2,1,0:T(8,128)(2,1)} %all-to-all-done.2), channel_id=1, source_target_pairs={{0,16},{16,0},{1,17},{17,1},{2,18},{18,2},{3,19},{19,3},{4,20},{20... | collective-permute-start | bytes 8650760 | tf_op jit(solution)/shard_map/ppermute | solution.py:671
  308.5 50.4 %all-to-all-start.4 = ((bf16[4,128,1408]{2,1,0:T(8,128)(2,1)}), bf16[4,128,1408]{2,1,0:T(8,128)(2,1)S(1)}, u32[]{:S(2)}, u32[]{:S(2)}) async-start(bf16[4,128,1408]{2,1,0:T(8,128)(2,1)} %slice.579), calls=%async_computation.5 | async-start | bytes 2883584 | tf_op jit(solution)/shard_map/all_to_all | solution.py:667
  312.1 180.1 %all-gather.6.cloned.1.call-start = ((), (), s32[]{:S(2)}) async-start(), calls=%async_computation.16 | async-start | bytes 5570560 | tf_op jit(solution)/shard_map/all_gather | solution.py:866
  362.3 83.8 %collective-permute-start.24 = (bf16[4,256,1408]{2,1,0:T(8,128)(2,1)}, bf16[4,256,1408]{2,1,0:T(8,128)(2,1)}, u32[]{:S(2)}, u32[]{:S(2)}) collective-permute-start(bf16[4,256,1408]{2,1,0:T(8,128)(2,1)} %all-to-all-done.3), channel_id=1, source_target_pairs={{0,16},{16,0},{1,17},{17,1},{2,18},{18,2},{3,19},{19,3},{4,20},{20... | collective-permute-start | bytes 8650760 | tf_op jit(solution)/shard_map/ppermute | solution.py:671
  380.2 61.7 %all-to-all-start.5 = ((bf16[4,128,1408]{2,1,0:T(8,128)(2,1)}), bf16[4,128,1408]{2,1,0:T(8,128)(2,1)}, u32[]{:S(2)}, u32[]{:S(2)}) async-start(bf16[4,128,1408]{2,1,0:T(8,128)(2,1)} %slice.456), calls=%async_computation.6 | async-start | bytes 2883584 | tf_op jit(solution)/shard_map/all_to_all | solution.py:667
  385.3 324.6 %all-gather.8.cloned.1.call-start = ((), (), s32[]{:S(2)}) async-start(), calls=%async_computation.17 | async-start | bytes 5570560 | tf_op jit(solution)/shard_map/all_gather | solution.py:584
  391.9 67.1 %collective-permute-start.22 = (bf16[4,128,1408]{2,1,0:T(8,128)(2,1)S(1)}, bf16[4,128,1408]{2,1,0:T(8,128)(2,1)}, u32[]{:S(2)}, u32[]{:S(2)}) collective-permute-start(bf16[4,128,1408]{2,1,0:T(8,128)(2,1)S(1)} %all-to-all-done.4), channel_id=1, source_target_pairs={{0,16},{16,0},{1,17},{17,1},{2,18},{18,2},{3,19},{19,3},{4,20},{20... | collective-permute-start | bytes 4325384 | tf_op jit(solution)/shard_map/ppermute | solution.py:671
  441.9 47.0 %collective-permute-start.23 = (bf16[4,128,1408]{2,1,0:T(8,128)(2,1)}, bf16[4,128,1408]{2,1,0:T(8,128)(2,1)S(1)}, u32[]{:S(2)}, u32[]{:S(2)}) collective-permute-start(bf16[4,128,1408]{2,1,0:T(8,128)(2,1)} %all-to-all-done.5), channel_id=1, source_target_pairs={{0,16},{16,0},{1,17},{17,1},{2,18},{18,2},{3,19},{19,3},{4,20},{20... | collective-permute-start | bytes 4325384 | tf_op jit(solution)/shard_map/ppermute | solution.py:671
  521.0 77.8 %collective-permute-start.33 = (bf16[1024,1408]{1,0:T(8,128)(2,1)}, bf16[1024,1408]{1,0:T(8,128)(2,1)}, u32[]{:S(2)}, u32[]{:S(2)}) collective-permute-start(bf16[1024,1408]{1,0:T(8,128)(2,1)} %convolution_convert_fusion.2), channel_id=1, source_target_pairs={{0,16},{16,0},{1,17},{17,1},{2,18},{18,2},{3,19},{19,3},{4,20},{20... | collective-permute-start | bytes 8650760 | tf_op jit(solution)/shard_map/ppermute | solution.py:671
  611.6 65.8 %collective-permute-start.43 = (bf16[1024,1408]{1,0:T(8,128)(2,1)}, bf16[1024,1408]{1,0:T(8,128)(2,1)}, u32[]{:S(2)}, u32[]{:S(2)}) collective-permute-start(bf16[1024,1408]{1,0:T(8,128)(2,1)} %convolution_convert_fusion.1), channel_id=1, source_target_pairs={{0,16},{16,0},{1,17},{17,1},{2,18},{18,2},{3,19},{19,3},{4,20},{20... | collective-permute-start | bytes 8650760 | tf_op jit(solution)/shard_map/ppermute | solution.py:671
  614.6 156.0 %collective-permute-start.50 = (bf16[1024,1408]{1,0:T(8,128)(2,1)}, bf16[1024,1408]{1,0:T(8,128)(2,1)}, u32[]{:S(2)}, u32[]{:S(2)}) collective-permute-start(bf16[1024,1408]{1,0:T(8,128)(2,1)} %convolution_convert_fusion), channel_id=1, source_target_pairs={{0,16},{16,0},{1,17},{17,1},{2,18},{18,2},{3,19},{19,3},{4,20},{20... | collective-permute-start | bytes 8650760 | tf_op jit(solution)/shard_map/ppermute | solution.py:671
  620.8 116.2 %all-to-all-start.6 = ((bf16[4,256,1408]{1,2,0:T(8,128)(2,1)}), bf16[4,256,1408]{1,2,0:T(8,128)(2,1)}, u32[]{:S(2)}, u32[]{:S(2)}) async-start(bf16[4,256,1408]{1,2,0:T(8,128)(2,1)} %copy.79), calls=%async_computation.7 | async-start | bytes 5767168 | tf_op jit(solution)/shard_map/all_to_all | solution.py:667
  743.9 192.1 %reduce-scatter.5.cloned.1.call-start = ((), (), s32[]{:S(2)}) async-start(), calls=%async_computation.18 | async-start | bytes 5570560 | tf_op jit(solution)/shard_map/reduce_scatter | solution.py:619
  789.6 55.3 %all-to-all-start.8 = ((bf16[4,128,1408]{2,1,0:T(8,128)(2,1)}), bf16[4,128,1408]{2,1,0:T(8,128)(2,1)S(1)}, u32[]{:S(2)}, u32[]{:S(2)}) async-start(bf16[4,128,1408]{2,1,0:T(8,128)(2,1)} %slice.509), calls=%async_computation.10 | async-start | bytes 2883584 | tf_op jit(solution)/shard_map/all_to_all | solution.py:667
  808.8 59.0 %collective-permute-start.59 = (bf16[1024,512]{1,0:T(8,128)(2,1)}, bf16[1024,512]{1,0:T(8,128)(2,1)}, u32[]{:S(2)}, u32[]{:S(2)}) collective-permute-start(bf16[1024,512]{1,0:T(8,128)(2,1)} %fusion.30), channel_id=1, source_target_pairs={{0,16},{16,0},{1,17},{17,1},{2,18},{18,2},{3,19},{19,3},{4,20},{20... | collective-permute-start | bytes 3145736 | tf_op jit(solution)/shard_map/ppermute | solution.py:671
  844.9 92.2 %all-to-all-start.9 = ((bf16[4,256,1408]{2,1,0:T(8,128)(2,1)}), bf16[4,256,1408]{2,1,0:T(8,128)(2,1)}, u32[]{:S(2)}, u32[]{:S(2)}) async-start(bf16[4,256,1408]{2,1,0:T(8,128)(2,1)} %bitcast.300), calls=%async_computation.11 | async-start | bytes 5767168 | tf_op jit(solution)/shard_map/all_to_all | solution.py:667
  887.0 47.7 %collective-permute-start.56 = (bf16[192,512]{1,0:T(8,128)(2,1)S(1)}, bf16[192,512]{1,0:T(8,128)(2,1)S(1)}, u32[]{:S(2)}, u32[]{:S(2)}) collective-permute-start(bf16[192,512]{1,0:T(8,128)(2,1)S(1)} %get-tuple-element.235), channel_id=1, source_target_pairs={{0,8},{4,12},{8,0},{12,4},{1,9},{5,13},{9,1},{13,5},{2,10},{6,14},... | collective-permute-start | bytes 589832 | tf_op jit(solution)/shard_map/ppermute | solution.py:514
  939.0 47.7 %collective-permute-start.63 = (bf16[320,512]{1,0:T(8,128)(2,1)}, bf16[320,512]{1,0:T(8,128)(2,1)}, u32[]{:S(2)}, u32[]{:S(2)}) collective-permute-start(bf16[320,512]{1,0:T(8,128)(2,1)} %add_convert_fusion.6), channel_id=1, source_target_pairs={{0,3},{1,2},{2,1},{3,0},{4,7},{5,6},{6,5},{7,4},{8,11},{9,10},{10,... | collective-permute-start | bytes 983048 | tf_op jit(solution)/shard_map/ppermute | solution.py:519
  939.0 48.5 %collective-permute-start.62 = (bf16[320,512]{1,0:T(8,128)(2,1)}, bf16[320,512]{1,0:T(8,128)(2,1)}, u32[]{:S(2)}, u32[]{:S(2)}) collective-permute-start(bf16[320,512]{1,0:T(8,128)(2,1)} %add_convert_fusion.6), channel_id=1, source_target_pairs={{0,2},{1,3},{2,0},{3,1},{4,6},{5,7},{6,4},{7,5},{8,10},{9,11},{10,... | collective-permute-start | bytes 983048 | tf_op jit(solution)/shard_map/ppermute | solution.py:519
  (163 other events, 2701.5 us)
Sparse Core Ops, SparseCore 0:
  10.9 91.2 all-gather.3
  179.7 108.0 reduce-scatter.2
  360.7 86.0 all-gather.5
  611.7 98.1 all-gather.7
  786.5 95.1 reduce-scatter.4
